TPU v7x, 32 devices: a whole 2x2x4 slice. The times are simulated.
32 devices in a mesh: dp: 16 (over z, y, x), mp: 2 (over core).
Axes of the slice: x: 2, y: 2, z: 4, core: 2. Of those that a mesh axis runs over, the one named last changes fastest.
Arguments:
- patches: bfloat16 [32, 784, 768], P('dp'), may hold values from -6 to 6
- ctx_index: int32 [32, 512], P('dp'), may hold values from 0 to 783, as said below
- tgt_index: int32 [32, 256], P('dp'), may hold values from 0 to 783, as said below
- group: int32 [32], P('dp'), may hold values from 0 to 1
- tgt_count: int32 [32], P('dp'), may hold values from 64 to 256
- embed: float32 [768, 768], P('dp'), may hold values from -0.21875 to 0.21875
- embed_m: float32 [768, 768], P('dp'), may hold values from -2.3841858e-07 to 2.3841858e-07
- embed_v: float32 [768, 768], P('dp'), may hold values from 2.4914533e-17 to 9.965813e-17
- bridge: float32 [768, 768], P('dp'), may hold values from -0.21875 to 0.21875
- bridge_m: float32 [768, 768], P('dp'), may hold values from -2.3841858e-07 to 2.3841858e-07
- bridge_v: float32 [768, 768], P('dp'), may hold values from 2.4914533e-17 to 9.965813e-17
- enc_in: float32 [768, 5376], P('dp', 'mp'), may hold values from -0.21875 to 0.21875
- enc_in_m: float32 [768, 5376], P('dp', 'mp'), may hold values from -2.3841858e-07 to 2.3841858e-07
- enc_in_v: float32 [768, 5376], P('dp', 'mp'), may hold values from 2.4914533e-17 to 9.965813e-17
- enc_out: float32 [3840, 768], P('mp', 'dp'), may hold values from -0.21875 to 0.21875
- enc_out_m: float32 [3840, 768], P('mp', 'dp'), may hold values from -2.3841858e-07 to 2.3841858e-07
- enc_out_v: float32 [3840, 768], P('mp', 'dp'), may hold values from 2.4914533e-17 to 9.965813e-17
- enc_gains: float32 [6, 768], P(None, 'dp')
- enc_gains_m: float32 [6, 768], P(None, 'dp'), may hold values from -2.3841858e-07 to 2.3841858e-07
- enc_gains_v: float32 [6, 768], P(None, 'dp'), may hold values from 2.4914533e-17 to 9.965813e-17
- pred_in: float32 [384, 2688], P('dp', 'mp'), may hold values from -0.3125 to 0.3125
- pred_in_m: float32 [384, 2688], P('dp', 'mp'), may hold values from -2.3841858e-07 to 2.3841858e-07
- pred_in_v: float32 [384, 2688], P('dp', 'mp'), may hold values from 2.4914533e-17 to 9.965813e-17
- pred_out: float32 [1920, 384], P('mp', 'dp'), may hold values from -0.3125 to 0.3125
- pred_out_m: float32 [1920, 384], P('mp', 'dp'), may hold values from -2.3841858e-07 to 2.3841858e-07
- pred_out_v: float32 [1920, 384], P('mp', 'dp'), may hold values from 2.4914533e-17 to 9.965813e-17
- pred_gains: float32 [7, 384], P(None, 'dp')
- pred_gains_m: float32 [7, 384], P(None, 'dp'), may hold values from -2.3841858e-07 to 2.3841858e-07
- pred_gains_v: float32 [7, 384], P(None, 'dp'), may hold values from 2.4914533e-17 to 9.965813e-17
- t_embed: float32 [768, 768], P('dp'), may hold values from -0.21875 to 0.21875
- t_in: float32 [768, 5376], P('dp', 'mp'), may hold values from -0.21875 to 0.21875
- t_out: float32 [3840, 768], P('mp', 'dp'), may hold values from -0.21875 to 0.21875
- t_gains: float32 [6, 768], P(None, 'dp')
Outputs:
- embed_new: float32 [768, 768], P('dp')
- embed_m_new: float32 [768, 768], P('dp')
- embed_v_new: float32 [768, 768], P('dp')
- bridge_new: float32 [768, 768], P('dp')
- bridge_m_new: float32 [768, 768], P('dp')
- bridge_v_new: float32 [768, 768], P('dp')
- enc_in_new: float32 [768, 5376], P('dp', 'mp')
- enc_in_m_new: float32 [768, 5376], P('dp', 'mp')
- enc_in_v_new: float32 [768, 5376], P('dp', 'mp')
- enc_out_new: float32 [3840, 768], P('mp', 'dp')
- enc_out_m_new: float32 [3840, 768], P('mp', 'dp')
- enc_out_v_new: float32 [3840, 768], P('mp', 'dp')
- enc_gains_new: float32 [6, 768], P(None, 'dp')
- enc_gains_m_new: float32 [6, 768], P(None, 'dp')
- enc_gains_v_new: float32 [6, 768], P(None, 'dp')
- pred_in_new: float32 [384, 2688], P('dp', 'mp')
- pred_in_m_new: float32 [384, 2688], P('dp', 'mp')
- pred_in_v_new: float32 [384, 2688], P('dp', 'mp')
- pred_out_new: float32 [1920, 384], P('mp', 'dp')
- pred_out_m_new: float32 [1920, 384], P('mp', 'dp')
- pred_out_v_new: float32 [1920, 384], P('mp', 'dp')
- pred_gains_new: float32 [7, 384], P(None, 'dp')
- pred_gains_m_new: float32 [7, 384], P(None, 'dp')
- pred_gains_v_new: float32 [7, 384], P(None, 'dp')
- loss_sum: float32 [], replicated
- grad_norm: float32 [], replicated
Inputs may be any that keep to these rules, and one draw needn't show every extreme that they name: `ctx_index`: each row holds 512 distinct positions in increasing order, none of them in the same row of tgt_index. `tgt_index`: each row holds 256 distinct positions in increasing order.
All inputs are finite; a program needn't handle non-finite values.
Results may differ from a plain program's by a relative error of at most 0.04.
Values may be sent and summed in bfloat16 or wider, within the bound.
No kernel may reach another device: no remote copies, remote signals or barrier semaphores. Data moves between devices by JAX's collectives and lax.ppermute only.
A program may use at most 320 MiB of HBM per device.

v0:
```python
import jax
import jax.numpy as jnp
from jax import lax
from jax.sharding import PartitionSpec as P

D = 768
HEADS = 12
PW = 384
PHEADS = 12
SIDE = 14
SMALLP = 196
CTX = 512
TGT = 256
STEP = 10


LOW = jnp.bfloat16
WIDE = jnp.float32
CLIP_NORM = 0.0005
LEARN_RATE = 0.05
GAIN_RATE = 1.0
BETA_ONE = 0.9
BETA_TWO = 0.999
EPSILON = 1e-08
WEIGHT_DECAY = 0.05


def norm_rows(values, gain_row, shift_row):
    centred = values - jnp.mean(values, -1, keepdims=True)
    spread = jnp.mean(centred * centred, -1, keepdims=True)
    return centred * lax.rsqrt(spread + 1e-06) * gain_row + shift_row


def gelu_exact(values):
    return jax.nn.gelu(values, approximate=False)


def place(group, positions):
    single = group[:, None] == 1
    image_id = jnp.where(single, 0, positions[None, :] // SMALLP)
    within = jnp.where(single, positions[None, :], positions[None, :] % SMALLP)
    side_len = jnp.where(single, 2 * SIDE, SIDE)
    return (image_id, within // side_len, within % side_len)


def sincos(row_pos, col_pos, width):
    quarter = width // 4
    omega = 10000.0 ** (-jnp.arange(quarter).astype(WIDE) / quarter)
    row_angle = row_pos.astype(WIDE)[..., None] * omega
    col_angle = col_pos.astype(WIDE)[..., None] * omega
    return jnp.concatenate(
        [jnp.sin(row_angle), jnp.cos(row_angle), jnp.sin(col_angle), jnp.cos(col_angle)], -1
    )


def pick_rows(values, index):
    return jnp.take_along_axis(values, index[:, :, None], 1)


def across(partial_sum):
    return lax.psum(partial_sum, "mp")


def split_heads(projected, heads):
    slot_count, row_count, columns = projected.shape
    local = columns // 3
    shaped = projected.reshape(slot_count, row_count, 3, heads, local // heads)
    return (shaped[:, :, 0], shaped[:, :, 1], shaped[:, :, 2])


def soft_weights(query, key_part, same_image):
    scale = query.shape[-1] ** (-0.5)
    scores = jnp.einsum("srha,stha->shrt", query, key_part, preferred_element_type=WIDE) * scale
    return jnp.where(same_image[:, None], scores, -1e30)


def attend_forward(projected, same_image, heads):
    query, key_part, value_part = split_heads(projected, heads)
    scores = soft_weights(query, key_part, same_image)
    log_total = jax.nn.logsumexp(scores, -1, keepdims=True)
    soft = jnp.exp(scores - log_total).astype(LOW)
    mixed = jnp.einsum("shrt,stha->srha", soft, value_part, preferred_element_type=WIDE)
    return (mixed.reshape(mixed.shape[0], mixed.shape[1], -1).astype(LOW), log_total)


def attend_backward(projected, same_image, log_total, d_mixed, heads):
    query, key_part, value_part = split_heads(projected, heads)
    scale = query.shape[-1] ** (-0.5)
    soft = jnp.exp(soft_weights(query, key_part, same_image) - log_total)
    d_mix = d_mixed.reshape(query.shape)
    d_soft = jnp.einsum("srha,stha->shrt", d_mix, value_part, preferred_element_type=WIDE)
    d_value = jnp.einsum("shrt,srha->stha", soft.astype(LOW), d_mix, preferred_element_type=WIDE)
    d_scores = (soft * (d_soft - jnp.sum(d_soft * soft, -1, keepdims=True))).astype(LOW)
    d_query = jnp.einsum("shrt,stha->srha", d_scores, key_part, preferred_element_type=WIDE) * scale
    d_key = jnp.einsum("shrt,srha->stha", d_scores, query, preferred_element_type=WIDE) * scale
    stacked = jnp.stack([d_query, d_key, d_value], 2)
    return stacked.reshape(projected.shape).astype(LOW)


def layer_forward(hidden, same_image, w_in, w_out, gains, heads):
    local = (w_in.shape[1] - w_out.shape[0]) // 2
    normed_one = norm_rows(hidden, gains[0], gains[1]).astype(LOW)
    projected = jnp.einsum(
        "srw,wc->src", normed_one, w_in[:, : 3 * local], preferred_element_type=WIDE
    ).astype(LOW)
    mixed, log_total = attend_forward(projected, same_image, heads)
    middle = hidden + across(
        jnp.einsum("src,cw->srw", mixed, w_out[:local], preferred_element_type=WIDE)
    )
    normed_two = norm_rows(middle, gains[2], gains[3]).astype(LOW)
    pre_act = jnp.einsum(
        "srw,wc->src", normed_two, w_in[:, 3 * local :], preferred_element_type=WIDE
    )
    activated = gelu_exact(pre_act).astype(LOW)
    output = middle + across(
        jnp.einsum("src,cw->srw", activated, w_out[local:], preferred_element_type=WIDE)
    )
    return (
        output,
        (hidden, middle, normed_one, projected, mixed, log_total, normed_two, pre_act, activated),
    )


def layer_backward(d_out, saved, same_image, w_in, w_out, gains, heads):
    stream, middle, normed_one, projected, mixed, log_total, normed_two, pre_act, activated = saved
    local = (w_in.shape[1] - w_out.shape[0]) // 2
    d_branch = d_out.astype(LOW)
    d_act = jnp.einsum("srw,cw->src", d_branch, w_out[local:], preferred_element_type=WIDE)
    unused, pullback = jax.vjp(gelu_exact, pre_act)
    d_pre = pullback(d_act)[0].astype(LOW)
    grad_down = jnp.einsum("src,srw->cw", activated, d_branch, preferred_element_type=WIDE)
    grad_up = jnp.einsum("srw,src->wc", normed_two, d_pre, preferred_element_type=WIDE)
    d_normed = across(
        jnp.einsum("src,wc->srw", d_pre, w_in[:, 3 * local :], preferred_element_type=WIDE)
    )
    unused, pullback = jax.vjp(norm_rows, middle, gains[2], gains[3])
    d_mid, grad_gain_two, grad_shift_two = pullback(d_normed)
    d_middle = d_out + d_mid
    d_branch = d_middle.astype(LOW)
    d_mixed = jnp.einsum(
        "srw,cw->src", d_branch, w_out[:local], preferred_element_type=WIDE
    ).astype(LOW)
    grad_attn = jnp.einsum("src,srw->cw", mixed, d_branch, preferred_element_type=WIDE)
    d_projected = attend_backward(projected, same_image, log_total, d_mixed, heads)
    grad_qkv = jnp.einsum("srw,src->wc", normed_one, d_projected, preferred_element_type=WIDE)
    d_normed = across(
        jnp.einsum("src,wc->srw", d_projected, w_in[:, : 3 * local], preferred_element_type=WIDE)
    )
    unused, pullback = jax.vjp(norm_rows, stream, gains[0], gains[1])
    d_hid, grad_gain_one, grad_shift_one = pullback(d_normed)
    grad_in = jnp.concatenate([grad_qkv, grad_up], 1)
    grad_out = jnp.concatenate([grad_attn, grad_down], 0)
    grad_gains = jnp.stack([grad_gain_one, grad_shift_one, grad_gain_two, grad_shift_two])
    return (d_middle + d_hid, grad_in, grad_out, grad_gains)


def adam(weight, moment_one, moment_two, gradient, decay, rate):
    moment_one = BETA_ONE * moment_one + (1.0 - BETA_ONE) * gradient
    moment_two = BETA_TWO * moment_two + (1.0 - BETA_TWO) * gradient * gradient
    fixed_one = moment_one / (1.0 - BETA_ONE**STEP)
    fixed_two = moment_two / (1.0 - BETA_TWO**STEP)
    weight = weight - rate * (fixed_one / (jnp.sqrt(fixed_two) + EPSILON) + decay * weight)
    return [weight, moment_one, moment_two]


def shards(
    patches,
    ctx_index,
    tgt_index,
    group,
    tgt_count,
    embed,
    embed_m,
    embed_v,
    bridge,
    bridge_m,
    bridge_v,
    enc_in,
    enc_in_m,
    enc_in_v,
    enc_out,
    enc_out_m,
    enc_out_v,
    enc_gains,
    enc_gains_m,
    enc_gains_v,
    pred_in,
    pred_in_m,
    pred_in_v,
    pred_out,
    pred_out_m,
    pred_out_v,
    pred_gains,
    pred_gains_m,
    pred_gains_v,
    t_embed,
    t_in,
    t_out,
    t_gains,
):
    (
        embed_w,
        bridge_w,
        enc_in_w,
        enc_out_w,
        pred_in_w,
        pred_out_w,
        target_embed,
        target_in,
        target_out,
    ) = (
        lax.all_gather(embed.astype(LOW), "dp", axis=0, tiled=True),
        lax.all_gather(bridge.astype(LOW), "dp", axis=0, tiled=True),
        lax.all_gather(enc_in.astype(LOW), "dp", axis=0, tiled=True),
        lax.all_gather(enc_out.astype(LOW), "dp", axis=1, tiled=True),
        lax.all_gather(pred_in.astype(LOW), "dp", axis=0, tiled=True),
        lax.all_gather(pred_out.astype(LOW), "dp", axis=1, tiled=True),
        lax.all_gather(t_embed.astype(LOW), "dp", axis=0, tiled=True),
        lax.all_gather(t_in.astype(LOW), "dp", axis=0, tiled=True),
        lax.all_gather(t_out.astype(LOW), "dp", axis=1, tiled=True),
    )
    enc_gain, pred_gain, target_gain = (
        lax.all_gather(enc_gains, "dp", axis=1, tiled=True),
        lax.all_gather(pred_gains, "dp", axis=1, tiled=True),
        lax.all_gather(t_gains, "dp", axis=1, tiled=True),
    )
    mp_count = lax.axis_size("mp")
    heads_enc = HEADS // mp_count
    heads_pred = PHEADS // mp_count
    slot_count = patches.shape[0]
    positions = jnp.arange(patches.shape[1])
    image_id, row_pos, col_pos = place(group, positions)
    table = sincos(row_pos, col_pos, D)
    small_table = sincos(row_pos, col_pos, PW)
    target_start = (
        jnp.einsum("srp,pw->srw", patches, target_embed, preferred_element_type=WIDE) + table
    )
    same_all = image_id[:, :, None] == image_id[:, None, :]
    target_hidden, unused = layer_forward(
        target_start, same_all, target_in, target_out, target_gain, heads_enc
    )
    chosen = norm_rows(pick_rows(target_hidden, tgt_index), target_gain[4], target_gain[5])
    target = norm_rows(chosen, 1.0, 0.0)
    seen = pick_rows(patches, ctx_index)
    ctx_id = jnp.take_along_axis(image_id, ctx_index, 1)
    tgt_id = jnp.take_along_axis(image_id, tgt_index, 1)
    same_ctx = ctx_id[:, :, None] == ctx_id[:, None, :]
    start = jnp.einsum("srp,pw->srw", seen, embed_w, preferred_element_type=WIDE) + pick_rows(
        table, ctx_index
    )
    hidden, enc_saved = layer_forward(start, same_ctx, enc_in_w, enc_out_w, enc_gain, heads_enc)
    context = norm_rows(hidden, enc_gain[4], enc_gain[5]).astype(LOW)
    inward = jnp.einsum("srw,wp->srp", context, bridge_w[:, :PW], preferred_element_type=WIDE)
    joined = jnp.concatenate(
        [
            inward + pick_rows(small_table, ctx_index),
            pred_gain[6] + pick_rows(small_table, tgt_index),
        ],
        1,
    )
    joined_id = jnp.concatenate([ctx_id, tgt_id], 1)
    same_pred = joined_id[:, :, None] == joined_id[:, None, :]
    predicted, pred_saved = layer_forward(
        joined, same_pred, pred_in_w, pred_out_w, pred_gain, heads_pred
    )
    tail_rows = predicted[:, CTX:]
    final = norm_rows(tail_rows, pred_gain[4], pred_gain[5]).astype(LOW)
    guess = jnp.einsum("srp,wp->srw", final, bridge_w[:, PW:], preferred_element_type=WIDE)
    diff = guess - target
    size_abs = jnp.abs(diff)
    keep = (jnp.arange(TGT)[None, :] < tgt_count[:, None])[:, :, None]
    loss_local = jnp.sum(
        jnp.where(keep, jnp.where(size_abs < 1.0, 0.5 * diff * diff, size_abs - 0.5), 0.0)
    )
    count = slot_count * lax.axis_size("dp") * TGT * D
    d_guess = jnp.where(keep, jnp.clip(diff, -1.0, 1.0) / count, 0.0).astype(LOW)
    grad_bridge_out = jnp.einsum("srw,srp->wp", d_guess, final, preferred_element_type=WIDE)
    d_final = jnp.einsum("srw,wp->srp", d_guess, bridge_w[:, PW:], preferred_element_type=WIDE)
    unused, pullback = jax.vjp(norm_rows, tail_rows, pred_gain[4], pred_gain[5])
    d_tail, grad_final_gain, grad_final_shift = pullback(d_final)
    d_predicted = jnp.concatenate([jnp.zeros((slot_count, CTX, PW), WIDE), d_tail], 1)
    d_joined, grad_pred_in, grad_pred_out, grad_pred_norms = layer_backward(
        d_predicted, pred_saved, same_pred, pred_in_w, pred_out_w, pred_gain, heads_pred
    )
    d_inward = d_joined[:, :CTX].astype(LOW)
    grad_token = jnp.sum(d_joined[:, CTX:], (0, 1))
    grad_bridge_in = jnp.einsum("srw,srp->wp", context, d_inward, preferred_element_type=WIDE)
    d_context = jnp.einsum("srp,wp->srw", d_inward, bridge_w[:, :PW], preferred_element_type=WIDE)
    unused, pullback = jax.vjp(norm_rows, hidden, enc_gain[4], enc_gain[5])
    d_hidden, grad_ctx_gain, grad_ctx_shift = pullback(d_context)
    d_start, grad_enc_in, grad_enc_out, grad_enc_norms = layer_backward(
        d_hidden, enc_saved, same_ctx, enc_in_w, enc_out_w, enc_gain, heads_enc
    )
    grad_embed = jnp.einsum("srp,srw->pw", seen, d_start.astype(LOW), preferred_element_type=WIDE)
    grad_bridge = jnp.concatenate([grad_bridge_in, grad_bridge_out], 1)
    grad_enc_gains = jnp.concatenate(
        [grad_enc_norms, jnp.stack([grad_ctx_gain, grad_ctx_shift])], 0
    )
    grad_pred_gains = jnp.concatenate(
        [grad_pred_norms, jnp.stack([grad_final_gain, grad_final_shift]), grad_token[None]], 0
    )
    reduced = (
        lax.psum_scatter(grad_embed, "dp", scatter_dimension=0, tiled=True),
        lax.psum_scatter(grad_bridge, "dp", scatter_dimension=0, tiled=True),
        lax.psum_scatter(grad_enc_in, "dp", scatter_dimension=0, tiled=True),
        lax.psum_scatter(grad_enc_out, "dp", scatter_dimension=1, tiled=True),
        lax.psum_scatter(grad_enc_gains, "dp", scatter_dimension=1, tiled=True),
        lax.psum_scatter(grad_pred_in, "dp", scatter_dimension=0, tiled=True),
        lax.psum_scatter(grad_pred_out, "dp", scatter_dimension=1, tiled=True),
        lax.psum_scatter(grad_pred_gains, "dp", scatter_dimension=1, tiled=True),
    )
    split_squares = sum(
        (jnp.sum(reduced[index_pos] * reduced[index_pos]) for index_pos in (2, 3, 5, 6))
    )
    shared_squares = sum(
        (jnp.sum(reduced[index_pos] * reduced[index_pos]) for index_pos in (0, 1, 4, 7))
    )
    partial_squares = split_squares + shared_squares / mp_count
    loss_sum = lax.psum(loss_local, "dp")
    square_sum = lax.psum(partial_squares, ("dp", "mp"))
    grad_norm = jnp.sqrt(square_sum)
    factor = jnp.minimum(1.0, CLIP_NORM / (grad_norm + 1e-06))
    masters = (embed, bridge, enc_in, enc_out, enc_gains, pred_in, pred_out, pred_gains)
    firsts = (
        embed_m,
        bridge_m,
        enc_in_m,
        enc_out_m,
        enc_gains_m,
        pred_in_m,
        pred_out_m,
        pred_gains_m,
    )
    seconds = (
        embed_v,
        bridge_v,
        enc_in_v,
        enc_out_v,
        enc_gains_v,
        pred_in_v,
        pred_out_v,
        pred_gains_v,
    )
    results = []
    for index_pos in range(8):
        is_gain = index_pos in (4, 7)
        decay = 0.0 if is_gain else WEIGHT_DECAY
        rate = GAIN_RATE if is_gain else LEARN_RATE
        results.extend(
            adam(
                masters[index_pos],
                firsts[index_pos],
                seconds[index_pos],
                reduced[index_pos] * factor,
                decay,
                rate,
            )
        )
    return (
        results[0],
        results[1],
        results[2],
        results[3],
        results[4],
        results[5],
        results[6],
        results[7],
        results[8],
        results[9],
        results[10],
        results[11],
        results[12],
        results[13],
        results[14],
        results[15],
        results[16],
        results[17],
        results[18],
        results[19],
        results[20],
        results[21],
        results[22],
        results[23],
        loss_sum,
        grad_norm,
    )


def solution(mesh):
    in_specs = (
        P("dp", None, None),
        P("dp", None),
        P("dp", None),
        P("dp"),
        P("dp"),
        P("dp", None),
        P("dp", None),
        P("dp", None),
        P("dp", None),
        P("dp", None),
        P("dp", None),
        P("dp", "mp"),
        P("dp", "mp"),
        P("dp", "mp"),
        P("mp", "dp"),
        P("mp", "dp"),
        P("mp", "dp"),
        P(None, "dp"),
        P(None, "dp"),
        P(None, "dp"),
        P("dp", "mp"),
        P("dp", "mp"),
        P("dp", "mp"),
        P("mp", "dp"),
        P("mp", "dp"),
        P("mp", "dp"),
        P(None, "dp"),
        P(None, "dp"),
        P(None, "dp"),
        P("dp", None),
        P("dp", "mp"),
        P("mp", "dp"),
        P(None, "dp"),
    )
    out_specs = (
        P("dp", None),
        P("dp", None),
        P("dp", None),
        P("dp", None),
        P("dp", None),
        P("dp", None),
        P("dp", "mp"),
        P("dp", "mp"),
        P("dp", "mp"),
        P("mp", "dp"),
        P("mp", "dp"),
        P("mp", "dp"),
        P(None, "dp"),
        P(None, "dp"),
        P(None, "dp"),
        P("dp", "mp"),
        P("dp", "mp"),
        P("dp", "mp"),
        P("mp", "dp"),
        P("mp", "dp"),
        P("mp", "dp"),
        P(None, "dp"),
        P(None, "dp"),
        P(None, "dp"),
        P(),
        P(),
    )
    return jax.shard_map(shards, mesh=mesh, in_specs=in_specs, out_specs=out_specs, check_vma=False)
```

profile of v0, /device:TPU:0, one launch (start us, length us, event | category | flops | bytes accessed | tf_op | source)
XLA Modules:
  0.0 2082.7 jit_solution(4891913884345033787)
XLA Ops:
  30.0 19.1 gather_fusion.1
  58.3 14.0 gather_fusion
  72.2 43.0 %all-gather = f32[16,48,6]{1,2,0:T(8,128)S(1)} all-gather(f32[1,48,6]{1,2,0:T(8,128)S(1)} %bitcast.360), channel_id=1, replica_groups=mesh['dp'=16,'mp'=2] {'dp'}, dimensions={0}, use_global_device_ids=true | all-gather | bytes 19584 | tf_op jit(solution)/shard_map/all_gather | solution.py:223
  122.5 25.8 %all-gather.13.cloned.1.call-done = bf16[768,2688]{1,0:T(8,128)(2,1)} async-done(((bf16[48,2688]{1,0:T(8,128)(2,1)}), bf16[768,2688]{1,0:T(8,128)(2,1)}) %all-gather.13.cloned.1.call-update) | async-done | bytes 4128784 | tf_op jit(solution)/shard_map/all_gather | solution.py:214
  184.2 32.5 %all-gather.15.cloned.1.call-done = bf16[1920,768]{0,1:T(8,128)(2,1)} async-done(((bf16[1920,48]{0,1:T(8,128)(2,1)}), bf16[1920,768]{0,1:T(8,128)(2,1)}) %all-gather.15.cloned.1.call-update) | async-done | bytes 2949136 | tf_op jit(solution)/shard_map/all_gather | solution.py:215
  223.4 19.9 all-reduce.15.cloned.1.call-done
  251.3 15.1 multiply_convert_fusion.2
  284.5 17.2 gather_fusion.3
  315.6 41.8 %all-gather.2 = f32[16,48,6]{1,2,0:T(8,128)S(1)} all-gather(f32[1,48,6]{1,2,0:T(8,128)S(1)} %bitcast.362), channel_id=1, replica_groups=mesh['dp'=16,'mp'=2] {'dp'}, dimensions={0}, use_global_device_ids=true | all-gather | bytes 19584 | tf_op jit(solution)/shard_map/all_gather | solution.py:225
  358.1 36.5 %all-gather.1 = f32[16,24,7]{1,2,0:T(8,128)S(1)} all-gather(f32[1,24,7]{1,2,0:T(8,128)S(1)} %bitcast.361), channel_id=1, replica_groups=mesh['dp'=16,'mp'=2] {'dp'}, dimensions={0}, use_global_device_ids=true | all-gather | bytes 11424 | tf_op jit(solution)/shard_map/all_gather | solution.py:224
  395.4 53.4 %all_gather.42 = bf16[384,1344]{1,0:T(8,128)(2,1)} all-gather(bf16[24,1344]{1,0:T(8,128)(2,1)S(1)} %convert_element_type.204), channel_id=1, replica_groups=mesh['dp'=16,'mp'=2] {'dp'}, dimensions={0}, use_global_device_ids=true | all-gather | bytes 1096704 | tf_op jit(solution)/shard_map/all_gather | solution.py:216
  450.5 43.0 %all_gather.43 = bf16[960,384]{0,1:T(8,128)(2,1)} all-gather(bf16[960,24]{0,1:T(8,128)(2,1)S(1)} %convert_element_type.210), channel_id=1, replica_groups=mesh['dp'=16,'mp'=2] {'dp'}, dimensions={1}, use_global_device_ids=true | all-gather | bytes 783360 | tf_op jit(solution)/shard_map/all_gather | solution.py:217
  516.8 15.0 fusion
  531.9 14.7 exponential_reduce_fusion
  546.6 16.5 fusion.44
  606.4 13.3 convolution_convert_fusion.8
  623.0 32.0 %all-reduce.29.cloned.1.call-done = (f32[2,768,384]{2,1,0:T(8,128)}, f32[2,784,768]{2,1,0:T(8,128)}) async-done(((f32[2,768,384]{2,1,0:T(8,128)}, f32[2,784,768]{2,1,0:T(8,128)}), (f32[2,768,384]{2,1,0:T(8,128)}, f32[2,784,768]{2,1,0:T(8,128)})) %all-reduce.29.cloned.1.call-update) | async-done | bytes 7176208 | tf_op jit(solution)/shard_map/psum | solution.py:61
  693.4 29.5 %fusion.22 = f32[2,784,768]{2,1,0:T(8,128)} fusion(f32[2,784,1536]{2,1,0:T(8,128)} %get-tuple-element.234, bf16[1920,768]{0,1:T(8,128)(2,1)S(1)} %copy-done.99, u8[784,1536]{1,0:T(8,128)(4,1)S(1)} %get-tuple-element.105, u8[784,1536]{1,0:T(8,128)(4,1)S(1)} %get-tuple-element.104), kind=kOutput, calls=%fused_computation.78 | convolution fusion | flops 3867967488 | bytes 19218432 | tf_op jit(solution)/shard_map/src,cw->srw/dot_general | solution.py:116
  723.6 34.4 %all-reduce.27.cloned.1.call-done = (f32[2,784,768]{2,1,0:T(8,128)}, f32[2,768,384]{2,1,0:T(8,128)}) async-done(((f32[2,784,768]{2,1,0:T(8,128)}, f32[2,768,384]{2,1,0:T(8,128)}), (f32[2,784,768]{2,1,0:T(8,128)}, f32[2,768,384]{2,1,0:T(8,128)})) %all-reduce.27.cloned.1.call-update) | async-done | bytes 7176208 | tf_op jit(solution)/shard_map/psum | solution.py:61
  793.1 22.9 %all-reduce.19.cloned.1.call-done = f32[2,768,384]{2,1,0:T(8,128)} async-done(((f32[2,768,384]{2,1,0:T(8,128)}), f32[2,768,384]{2,1,0:T(8,128)}) %all-reduce.19.cloned.1.call-update) | async-done | bytes 2359312 | tf_op jit(solution)/shard_map/psum | solution.py:61
  823.4 23.4 %multiply_reduce_fusion = (f32[2,6,768]{2,1,0:T(8,128)S(1)}, f32[2,6,768,768]{2,3,1,0:T(8,128)}) fusion(f32[2,6,768,768]{2,3,1,0:T(8,128)} %get-tuple-element.228, f32[2,6,768]{2,1,0:T(8,128)S(1)} %log_add_fusion.1, pred[2,768,768]{1,2,0:T(8,128)(4,1)S(1)} %copy-done.20, bf16[2,768,6,32]{1,3,2,0:T(8,128)(2,1)S(1)} %bitcast.343, ...), kind=kOutput, calls=%fused_computation.11 | convolution fusion | flops 488365056 | bytes 59056128 | tf_op jit(solution)/shard_map/srha,stha->shrt/dot_general | solution.py:91
  846.8 23.8 %multiply_convert_fusion = bf16[2,6,768,768]{2,3,1,0:T(8,128)(2,1)} fusion(f32[2,6,768,768]{2,3,1,0:T(8,128)} %get-tuple-element.237, f32[2,6,768,768]{2,3,1,0:T(8,128)} %get-tuple-element.228, f32[2,6,768]{2,1,0:T(8,128)S(1)} %get-tuple-element.236, f32[2,6,768]{2,1,0:T(8,128)S(1)} %log_add_fusion.1, pred[2,768,768]{1,2,0:T(8,128)(4,1)} %broadcast_compare_fusion.1), kind=kLoop, calls=%fused_computation.10 | loop fusion | flops 42467328 | bytes 72032256 | tf_op jit(solution)/shard_map/convert_element_type | solution.py:93
  906.6 22.9 %all-reduce.21.cloned.1.call-done = f32[2,768,384]{2,1,0:T(8,128)} async-done(((f32[2,768,384]{2,1,0:T(8,128)}), f32[2,768,384]{2,1,0:T(8,128)}) %all-reduce.21.cloned.1.call-update) | async-done | bytes 2359312 | tf_op jit(solution)/shard_map/psum | solution.py:61
  955.9 24.5 %all-reduce.23.cloned.1.call-done = f32[2,512,768]{2,1,0:T(8,128)} async-done(((f32[2,512,768]{2,1,0:T(8,128)}), f32[2,512,768]{2,1,0:T(8,128)}) %all-reduce.23.cloned.1.call-update) | async-done | bytes 3145744 | tf_op jit(solution)/shard_map/psum | solution.py:61
  1098.5 77.6 %all-reduce.3 = (f32[7,384]{1,0:T(8,128)S(1)}, f32[]{:T(128)}) all-reduce(f32[7,384]{1,0:T(8,128)S(1)} %concatenate.47, f32[]{:T(128)} %fusion.47), channel_id=9, replica_groups=mesh['dp'=16,'mp'=2] {'dp'}, use_global_device_ids=true, to_apply=%region_77.78.clone | all-reduce | flops 2689 | bytes 21512
  1181.5 129.9 %reduce-scatter.29.cloned.1.call-done = f32[24,1344]{1,0:T(8,128)} async-done(((f32[384,1344]{1,0:T(8,128)}), f32[24,1344]{1,0:T(8,128)}) %reduce-scatter.29.cloned.1.call-update) | async-done | bytes 129040
  1313.0 130.8 %reduce-scatter.21.cloned.1.call-done = f32[48,768]{1,0:T(8,128)} async-done(((f32[768,768]{1,0:T(8,128)}), f32[48,768]{1,0:T(8,128)}) %reduce-scatter.21.cloned.1.call-update) | async-done | bytes 147472 | tf_op jit(solution)/shard_map/reduce_scatter | solution.py:304
  1445.4 124.9 %reduce-scatter.27.cloned.1.call-done = f32[48,6]{1,0:T(8,128)} async-done(((f32[768,6]{1,0:T(8,128)}), f32[48,6]{1,0:T(8,128)}) %reduce-scatter.27.cloned.1.call-update) | async-done | bytes 1168
  1571.7 131.0 %reduce-scatter.17.cloned.1.call-done = f32[48,768]{1,0:T(8,128)} async-done(((f32[768,768]{1,0:T(8,128)}), f32[48,768]{1,0:T(8,128)}) %reduce-scatter.17.cloned.1.call-update) | async-done | bytes 147472 | tf_op jit(solution)/shard_map/reduce_scatter | solution.py:303
  1706.9 144.4 %reduce-scatter.23.cloned.1.call-done = f32[48,1920]{1,0:T(8,128)} async-done(((f32[768,1920]{1,0:T(8,128)}), f32[48,1920]{1,0:T(8,128)}) %reduce-scatter.23.cloned.1.call-update) | async-done | bytes 368656
  1853.5 166.2 %reduce-scatter.19.cloned.1.call-done = f32[48,2688]{1,0:T(8,128)} async-done(((f32[768,2688]{1,0:T(8,128)}), f32[48,2688]{1,0:T(8,128)}) %reduce-scatter.19.cloned.1.call-update) | async-done | bytes 516112 | tf_op jit(solution)/shard_map/reduce_scatter | solution.py:305
  2024.1 39.4 %psum.94 = f32[]{:T(128)} all-reduce(f32[]{:T(128)S(6)} %add.584), channel_id=1, replica_groups=mesh['dp'=16,'mp'=2] {'dp','mp'}, use_global_device_ids=true, to_apply=%region_79.80 | all-reduce | flops 1 | bytes 8 | tf_op jit(solution)/shard_map/psum | solution.py:320
  (654 shorter events, 479.1 us)
Async XLA Ops:
  7.2 108.7 %all-gather.11.cloned.1.call-start = ((), (), s32[]{:S(2)}) async-start(), calls=%async_computation.7 | async-start | bytes 1253376 | tf_op jit(solution)/shard_map/all_gather | solution.py:212
  9.0 139.4 %all-gather.13.cloned.1.call-start = ((), (), s32[]{:S(2)}) async-start(), calls=%async_computation.8 | async-start | bytes 4386816 | tf_op jit(solution)/shard_map/all_gather | solution.py:214
  10.8 205.8 %all-gather.15.cloned.1.call-start = ((), (), s32[]{:S(2)}) async-start(), calls=%async_computation.9 | async-start | bytes 3133440 | tf_op jit(solution)/shard_map/all_gather | solution.py:215
  12.6 230.7 %all-reduce.15.cloned.1.call-start = ((), (), s32[]{:S(2)}) async-start(), calls=%async_computation.10 | async-start | bytes 6291456 | tf_op jit(solution)/shard_map/psum | solution.py:61
  220.8 272.9 %all-gather.19.cloned.1.call-start = ((), (), s32[]{:S(2)}) async-start(), calls=%async_computation.13 | async-start | bytes 1253376 | tf_op jit(solution)/shard_map/all_gather | solution.py:218
  221.5 280.4 %all-gather.21.cloned.1.call-start = ((), (), s32[]{:S(2)}) async-start(), calls=%async_computation.14 | async-start | bytes 4386816 | tf_op jit(solution)/shard_map/all_gather | solution.py:219
  222.3 340.8 %all-gather.23.cloned.1.call-start = ((), (), s32[]{:S(2)}) async-start(), calls=%async_computation.15 | async-start | bytes 3133440 | tf_op jit(solution)/shard_map/all_gather | solution.py:220
  223.1 345.1 %all-reduce.17.cloned.1.call-start = ((), (), s32[]{:S(2)}) async-start(), calls=%async_computation.11 | async-start | bytes 6291456 | tf_op jit(solution)/shard_map/psum | solution.py:61
  272.5 301.2 %all-gather.17.cloned.1.call-start = ((), (), s32[]{:S(2)}) async-start(), calls=%async_computation.12 | async-start | bytes 1253376 | tf_op jit(solution)/shard_map/all_gather | solution.py:213
  274.0 380.9 %all-reduce.29.cloned.1.call-start = ((), (), s32[]{:S(2)}) async-start(), calls=%async_computation.28 | async-start | bytes 14352384 | tf_op jit(solution)/shard_map/psum | solution.py:61
  622.9 135.1 %all-reduce.27.cloned.1.call-start = ((), (), s32[]{:S(2)}) async-start(), calls=%async_computation.27 | async-start | bytes 14352384 | tf_op jit(solution)/shard_map/psum | solution.py:61
  722.9 93.1 %all-reduce.19.cloned.1.call-start = ((), (), s32[]{:S(2)}) async-start(), calls=%async_computation.16 | async-start | bytes 4718592 | tf_op jit(solution)/shard_map/psum | solution.py:61
  793.0 136.4 %all-reduce.21.cloned.1.call-start = ((), (), s32[]{:S(2)}) async-start(), calls=%async_computation.17 | async-start | bytes 4718592 | tf_op jit(solution)/shard_map/psum | solution.py:61
  906.5 73.8 %all-reduce.23.cloned.1.call-start = ((), (), s32[]{:S(2)}) async-start(), calls=%async_computation.18 | async-start | bytes 6291456 | tf_op jit(solution)/shard_map/psum | solution.py:61
  955.8 93.4 %all-reduce.25.cloned.1.call-start = ((), (), s32[]{:S(2)}) async-start(), calls=%async_computation.19 | async-start | bytes 6291456 | tf_op jit(solution)/shard_map/psum | solution.py:61
  1024.7 154.9 %reduce-scatter.25.cloned.1.call-start = ((), (), s32[]{:S(2)}) async-start(), calls=%async_computation.24 | async-start | bytes 1671168
  1033.3 278.1 %reduce-scatter.29.cloned.1.call-start = ((), (), s32[]{:S(2)}) async-start(), calls=%async_computation.26 | async-start | bytes 2297856
  1040.4 403.5 %reduce-scatter.21.cloned.1.call-start = ((), (), s32[]{:S(2)}) async-start(), calls=%async_computation.22 | async-start | bytes 2506752 | tf_op jit(solution)/shard_map/reduce_scatter | solution.py:304
  1047.0 523.3 %reduce-scatter.27.cloned.1.call-start = ((), (), s32[]{:S(2)}) async-start(), calls=%async_computation.25 | async-start | bytes 417792
  1056.4 646.3 %reduce-scatter.17.cloned.1.call-start = ((), (), s32[]{:S(2)}) async-start(), calls=%async_computation.20 | async-start | bytes 2506752 | tf_op jit(solution)/shard_map/reduce_scatter | solution.py:303
  1064.1 787.2 %reduce-scatter.23.cloned.1.call-start = ((), (), s32[]{:S(2)}) async-start(), calls=%async_computation.23 | async-start | bytes 6266880
  1080.5 939.2 %reduce-scatter.19.cloned.1.call-start = ((), (), s32[]{:S(2)}) async-start(), calls=%async_computation.21 | async-start | bytes 8773632 | tf_op jit(solution)/shard_map/reduce_scatter | solution.py:305
  1095.6 968.7 %copy-start.148 = (f32[7,24]{1,0:T(8,128)S(1)}, f32[7,24]{1,0:T(8,128)}, u32[]{:S(2)}) copy-start(f32[7,24]{1,0:T(8,128)} %param.59) | copy-start | bytes 2020
  1095.6 969.4 %copy-start.145 = (f32[6,48]{1,0:T(8,128)S(1)}, f32[6,48]{1,0:T(8,128)}, u32[]{:S(2)}) copy-start(f32[6,48]{1,0:T(8,128)} %param.50) | copy-start | bytes 3460
  1095.6 969.4 %copy-start.154 = (f32[6,48]{1,0:T(8,128)S(1)}, f32[6,48]{1,0:T(8,128)}, u32[]{:S(2)}) copy-start(f32[6,48]{1,0:T(8,128)} %param.51) | copy-start | bytes 3460
  1095.6 969.4 %copy-start.155 = (f32[6,48]{1,0:T(8,128)S(1)}, f32[6,48]{1,0:T(8,128)}, u32[]{:S(2)}) copy-start(f32[6,48]{1,0:T(8,128)} %param.52) | copy-start | bytes 3460
  1095.6 970.0 %copy-start.83 = (f32[960,24]{0,1:T(8,128)S(1)}, f32[960,24]{0,1:T(8,128)}, u32[]{:S(2)}) copy-start(f32[960,24]{0,1:T(8,128)} %param.56) | copy-start | bytes 276484
  1095.7 970.0 %copy-start.100 = (f32[960,24]{0,1:T(8,128)S(1)}, f32[960,24]{0,1:T(8,128)}, u32[]{:S(2)}) copy-start(f32[960,24]{0,1:T(8,128)} %param.57) | copy-start | bytes 276484
  1095.7 970.0 %copy-start.101 = (f32[960,24]{0,1:T(8,128)S(1)}, f32[960,24]{0,1:T(8,128)}, u32[]{:S(2)}) copy-start(f32[960,24]{0,1:T(8,128)} %param.58) | copy-start | bytes 276484
  1097.1 969.3 %copy-start.78 = (f32[24,1344]{1,0:T(8,128)S(1)}, f32[24,1344]{1,0:T(8,128)}, u32[]{:S(2)}) copy-start(f32[24,1344]{1,0:T(8,128)} %param.53) | copy-start | bytes 387076
  1097.1 969.3 %copy-start.95 = (f32[24,1344]{1,0:T(8,128)S(1)}, f32[24,1344]{1,0:T(8,128)}, u32[]{:S(2)}) copy-start(f32[24,1344]{1,0:T(8,128)} %param.54) | copy-start | bytes 387076
  1097.1 969.3 %copy-start.96 = (f32[24,1344]{1,0:T(8,128)S(1)}, f32[24,1344]{1,0:T(8,128)}, u32[]{:S(2)}) copy-start(f32[24,1344]{1,0:T(8,128)} %param.55) | copy-start | bytes 387076
  (180 other events, 8165.9 us)
Sparse Core Ops, SparseCore 0:
  11.4 58.8 all-gather.10
  73.7 74.6 all-gather.12
  151.8 64.8 all-gather.14
  220.9 22.2 all-reduce.14
  246.8 57.2 all-gather.18
  307.8 76.0 all-gather.20
  387.7 73.8 all-gather.22
  464.0 22.2 all-reduce.16
  489.7 57.2 all-gather.16
  623.0 31.8 all-reduce.28
  723.0 34.9 all-reduce.26
  793.2 22.7 all-reduce.18
  906.6 22.7 all-reduce.20
  955.9 24.3 all-reduce.22
  1024.8 24.3 all-reduce.24
  1053.9 125.7 reduce-scatter.24
  1184.4 126.9 reduce-scatter.28
  1316.2 127.6 reduce-scatter.20
  1449.8 120.4 reduce-scatter.26
  1575.1 127.6 reduce-scatter.16
  1708.9 142.3 reduce-scatter.22
  1857.8 161.7 reduce-scatter.18
where the time goes:
time: 2090 us; the launch traced here: 2080 us
  waiting for transfers between devices  1050 us (50%)
  blocking collectives  335 us (16%)
  matrix products  315 us (15%)
  other arithmetic  219 us (10%)
  local copies, waits for them, and re-layouts  140 us (7%)
  between operations  25.1 us (1%)
    unnamed x26, waiting for transfers between devices  402 us
    reduce_scatter x1, waiting for transfers between devices, shards(): lax.psum_scatter(grad_enc_in, 'dp', scatter_dimension=0, tiled=True)  166 us
    psum x8, waiting for transfers between devices, across(): return lax.psum(partial_sum, 'mp')  159 us
    reduce_scatter x1, waiting for transfers between devices, shards(): lax.psum_scatter(grad_embed, 'dp', scatter_dimension=0, tiled=True)  131 us
    reduce_scatter x1, waiting for transfers between devices, shards(): lax.psum_scatter(grad_bridge, 'dp', scatter_dimension=0, tiled=True)  131 us
    unnamed x1, blocking collectives  77.6 us
    gather x5, local copies, waits for them, and re-layouts, pick_rows(): return jnp.take_along_axis(values, index[:, :, None], 1)  69 us
    all_gather x1, blocking collectives, shards(): lax.all_gather(pred_in.astype(LOW), 'dp', axis=0, tiled=True)  53.4 us
  transfers between devices with their start and end apart: 22, of which 16 were waited for; matrix products, arithmetic and copies ran while one was open for 16% of the time, Pallas kernels for 0%

commit v1 on v0

v1 whole, which is shorter than its diff:
```python
import functools

import jax
import jax.numpy as jnp
from jax import lax
from jax.experimental import pallas as pl
from jax.experimental.pallas import tpu as pltpu
from jax.sharding import PartitionSpec as P

D = 768
HEADS = 12
PW = 384
PHEADS = 12
SIDE = 14
SMALLP = 196
CTX = 512
TGT = 256
STEP = 10


LOW = jnp.bfloat16
WIDE = jnp.float32
CLIP_NORM = 0.0005
LEARN_RATE = 0.05
GAIN_RATE = 1.0
BETA_ONE = 0.9
BETA_TWO = 0.999
EPSILON = 1e-08
WEIGHT_DECAY = 0.05


LANES = 128


def norm_rows(values, gain_row, shift_row):
    centred = values - jnp.mean(values, -1, keepdims=True)
    spread = jnp.mean(centred * centred, -1, keepdims=True)
    return centred * lax.rsqrt(spread + 1e-06) * gain_row + shift_row


def norm_back(values, gain_row, grad):
    centred = values - jnp.mean(values, -1, keepdims=True)
    rstd = lax.rsqrt(jnp.mean(centred * centred, -1, keepdims=True) + 1e-06)
    unit = centred * rstd
    scaled = grad * gain_row
    d_values = rstd * (
        scaled
        - jnp.mean(scaled, -1, keepdims=True)
        - unit * jnp.mean(scaled * unit, -1, keepdims=True)
    )
    return d_values, jnp.sum(grad * unit, 0), jnp.sum(grad, 0)


def gelu_parts(pre):
    bell = jnp.exp(-0.5 * pre * pre)
    turn = 1.0 / (1.0 + 0.3275911 * 0.7071067811865476 * jnp.abs(pre))
    series = 0.5 * 1.061405429
    for factor in (-1.453152027, 1.421413741, -0.284496736, 0.254829592):
        series = series * turn + 0.5 * factor
    tail = series * turn * bell
    return jnp.where(pre < 0.0, tail, 1.0 - tail), bell * 0.3989422804014327


def gelu_both(pre):
    phi, density = gelu_parts(pre)
    return (pre * phi).astype(LOW), (phi + pre * density).astype(LOW)


def place(single, positions):
    image_id = jnp.where(single, 0, positions // SMALLP)
    within = jnp.where(single, positions, positions % SMALLP)
    side_len = jnp.where(single, 2 * SIDE, SIDE)
    return (image_id, within // side_len, within % side_len)


def three_parts(values):
    high = lax.reduce_precision(values, 8, 7)
    rest = values - high
    middle = lax.reduce_precision(rest, 8, 7)
    return jnp.concatenate([high, middle, rest - middle], 0).astype(LOW)


def sincos(row_pos, col_pos, width, order):
    quarter = width // 4
    omega = 10000.0 ** (-jnp.arange(quarter).astype(WIDE) / quarter)
    steps = jnp.arange(2 * SIDE)
    angle = steps.astype(WIDE)[:, None] * omega
    table = jnp.concatenate([jnp.sin(angle), jnp.cos(angle)], -1)
    blank = jnp.zeros_like(table)
    table = jnp.concatenate(
        [jnp.concatenate([table, blank], 1), jnp.concatenate([blank, table], 1)], 0
    )
    parts = three_parts(table)
    if order is not None:
        parts = mm(parts, order).astype(LOW)
    pick = jnp.concatenate([row_pos[:, None] == steps, col_pos[:, None] == steps], 1)
    pick = pick.astype(LOW)
    return mm(jnp.concatenate([pick, pick, pick], 1), parts)


def mm(left, right):
    return jnp.dot(left, right, preferred_element_type=WIDE)


def mm_t(left, right):
    return lax.dot_general(left, right, (((1,), (1,)), ((), ())), preferred_element_type=WIDE)


def t_mm(left, right):
    return lax.dot_general(left, right, (((0,), (0,)), ((), ())), preferred_element_type=WIDE)


def head_forward(query, keys, values, bias, size):
    scores = mm_t(keys, query) + bias
    soft = jnp.exp((scores - jnp.max(scores, 0, keepdims=True)) * size**-0.5)
    total = jnp.sum(soft, 0, keepdims=True)
    return (t_mm(values, soft.astype(LOW)) / total).T


def head_backward(query, keys, values, d_out, bias, size):
    scale = size**-0.5
    scores = mm_t(keys, query) + bias
    soft = jnp.exp((scores - jnp.max(scores, 0, keepdims=True)) * scale)
    soft = soft * (1.0 / jnp.sum(soft, 0, keepdims=True))
    d_soft = mm_t(values, d_out)
    row_sum = jnp.sum(d_soft * soft, 0, keepdims=True)
    d_scores = (soft * (d_soft - row_sum)).astype(LOW)
    d_values = mm(soft.astype(LOW), d_out)
    d_keys = mm(d_scores, query) * scale
    d_query = (t_mm(keys, d_scores) * scale).T
    return d_query.astype(LOW), d_keys.astype(LOW), d_values.astype(LOW)


WHOLE = pl.BlockSpec(memory_space=pltpu.VMEM)
CHUNK = 64


def on_chip(kernel, ins, outs, scratch, macs, exps=0):
    outs = [jax.ShapeDtypeStruct(shape, kind) for shape, kind in outs]
    moved = sum(value.size * value.dtype.itemsize for value in list(ins) + outs)
    return pl.pallas_call(
        kernel,
        in_specs=[WHOLE] * len(ins),
        out_specs=[WHOLE] * len(outs),
        out_shape=outs,
        scratch_shapes=[pltpu.VMEM(shape, kind) for shape, kind in scratch],
        cost_estimate=pl.CostEstimate(flops=2 * macs, bytes_accessed=moved, transcendentals=exps),
        compiler_params=pltpu.CompilerParams(vmem_limit_bytes=56 * 1024 * 1024),
    )(*ins)


def tiles(count, width, body):
    def step(at, carry):
        body(pl.ds(pl.multiple_of(at * width, width), width))
        return carry

    lax.fori_loop(0, count // width, step, 0)


def norm_back_rows(values_ref, grad_ref, gain, write, sums_ref, at):
    rows, width = values_ref.shape

    def step(number, carry):
        span = pl.ds(pl.multiple_of(number * CHUNK, CHUNK), CHUNK)
        values, grad = values_ref[span, :], grad_ref[span, :]
        centred = values - jnp.mean(values, -1, keepdims=True)
        rstd = lax.rsqrt(jnp.mean(centred * centred, -1, keepdims=True) + 1e-06)
        unit = centred * rstd
        scaled = grad * gain
        d_values = rstd * (
            scaled
            - jnp.mean(scaled, -1, keepdims=True)
            - unit * jnp.mean(scaled * unit, -1, keepdims=True)
        )
        write(span, d_values)
        return (
            carry[0] + jnp.sum(grad * unit, 0, keepdims=True),
            carry[1] + jnp.sum(grad, 0, keepdims=True),
        )

    blank = jnp.zeros((1, width), WIDE)
    gains, shifts = lax.fori_loop(0, rows // CHUNK, step, (blank, blank))
    sums_ref[at : at + 1, :] = gains
    sums_ref[at + 1 : at + 2, :] = shifts


def ff_back_kernel(*refs):
    (d_inward, bridge_in, hidden, middle, normed, order, gains) = refs[0:7]
    acts, slopes, ups, downs = refs[7:9], refs[9:11], refs[11:13], refs[13:15]
    grads, branch_out, d_middle, sums = refs[15:19], refs[19], refs[20], refs[21]
    grad, d_hidden, branch, branch_t, normed_t, d_pre = refs[22:28]
    ff = acts[0].shape[1]
    wide = 768

    def first(span):
        grad[:, span] = mm_t(d_inward[...], bridge_in[span, :])

    tiles(D, wide, first)

    def write_hidden(span, values):
        d_hidden[span, :] = values
        branch[span, :] = values.astype(LOW)

    norm_back_rows(hidden, grad, gains[4:5, :], write_hidden, sums, 0)
    branch_t[...] = mm_t(order[...], branch[...]).astype(LOW)
    normed_t[...] = mm_t(order[...], normed[...]).astype(LOW)
    for side in (0, 1):
        act, slope, down = acts[side], slopes[side], downs[side]
        out_up, out_down = grads[2 * side], grads[2 * side + 1]

        def second(
            span, act=act, slope=slope, down=down, out_up=out_up, out_down=out_down, side=side
        ):
            d_act = mm(branch[...], down[:, span])
            values = (d_act * slope[:, span].astype(WIDE)).astype(LOW)
            d_pre[side, :, span] = values
            out_up[:, span] = mm(normed_t[...], values).astype(LOW)
            out_down[:, span] = mm(branch_t[...], act[:, span]).astype(LOW)

        tiles(ff, wide, second)

    def third(span):
        grad[:, span] = mm_t(d_pre[0], ups[0][span, :]) + mm_t(d_pre[1], ups[1][span, :])

    tiles(D, wide, third)

    def write_middle(span, values):
        values = values + d_hidden[span, :]
        d_middle[span, :] = values
        branch_out[span, :] = values.astype(LOW)

    norm_back_rows(middle, grad, gains[2:3, :], write_middle, sums, 2)


def ff_back(d_inward, bridge_in, hidden, middle, normed, order, gains, acts, slopes, ups, downs):
    rows, ff = acts[0].shape
    return on_chip(
        ff_back_kernel,
        [d_inward, bridge_in, hidden, middle, normed, order, gains]
        + [*acts, *slopes, *ups, *downs],
        [((D, ff), LOW)] * 4 + [((rows, D), LOW), ((rows, D), WIDE), ((8, D), WIDE)],
        [((rows, D), WIDE)] * 2
        + [((rows, D), LOW), ((D, rows), LOW), ((D, rows), LOW), ((2, rows, ff), LOW)],
        8 * rows * D * ff,
    )


def attn_back_kernel(size, branch, ids_row, ids_col, *refs):
    rests, projs, d_projs, d_mixed = refs[0:2], refs[2:4], refs[4:6], refs[6]
    width = D // 2
    bias = jnp.where(ids_col[...] == ids_row[...], 0.0, -1e30)
    for rest, proj, d_proj in zip(rests, projs, d_projs):
        d_mixed[...] = mm(branch[...], rest[:, width : 2 * width]).astype(LOW)

        def step(block, carry, proj=proj, d_proj=d_proj):
            at = [pl.multiple_of(part * width + block * LANES, LANES) for part in range(3)]
            query, keys, values = [proj[:, pl.ds(col, LANES)] for col in at]
            d_out = d_mixed[:, pl.ds(at[0], LANES)]
            found = []
            for low in range(0, LANES, size):
                cols = slice(low, low + size)
                found.append(
                    head_backward(
                        query[:, cols], keys[:, cols], values[:, cols], d_out[:, cols], bias, size
                    )
                )
            for col, parts in zip(at, zip(*found)):
                d_proj[:, pl.ds(col, LANES)] = jnp.concatenate(parts, -1)
            return carry

        lax.fori_loop(0, width // LANES, step, 0)


def attn_back(size, branch, ids, rests, projs):
    rows = branch.shape[0]
    return on_chip(
        functools.partial(attn_back_kernel, size),
        [branch, ids[None, :], ids[:, None], *rests, *projs],
        [(projs[0].shape, LOW)] * 2,
        [((rows, D // 2), LOW)],
        rows * D * D + rows * rows * D * 5,
        rows * rows * D // size,
    )


def qkv_back_kernel(*refs):
    branch, d_middle, start, normed, seen, eye, gains, sums_ff, sums_p, spread = refs[0:10]
    d_projs, mixeds, qkvs, orders = refs[10:12], refs[12:14], refs[14:16], refs[16:18]
    out_qkv, out_rest = refs[18:20], refs[20:22]
    grad, flipped, d_start, sums = refs[22:26]
    width = D // 2
    flipped[...] = mm_t(eye[...], branch[...]).astype(LOW)
    for side in (0, 1):
        out_rest[side][:, width : 2 * width] = mm(flipped[...], mixeds[side][...]).astype(LOW)
    flipped[...] = mm_t(eye[...], normed[...]).astype(LOW)
    for side in (0, 1):
        out_qkv[side][...] = mm(flipped[...], d_projs[side][...]).astype(LOW)
    grad[...] = mm_t(d_projs[0][...], qkvs[0][...]) + mm_t(d_projs[1][...], qkvs[1][...])

    def write(span, values):
        d_start[span, :] = (values + d_middle[span, :]).astype(LOW)

    norm_back_rows(start, grad, gains[0:1, :], write, sums, 0)
    flipped[...] = mm_t(eye[...], seen[...]).astype(LOW)
    sums[2:4, :] = sums_ff[2:4, :]
    sums[4:6, :] = sums_ff[0:2, :]
    sums[6:8, :] = jnp.zeros((2, D), WIDE)
    rows = jnp.concatenate(
        [sums[...].astype(LOW), mm(sums_p[...].astype(LOW), spread[...]).astype(LOW)], 0
    )
    cols = t_mm(rows, eye[0:16, 0:LANES]).astype(LOW)
    for side in (0, 1):
        moved = mm_t(d_start[...], orders[side][...]).astype(LOW)
        out_rest[side][:, 0:width] = mm(flipped[...], moved).astype(LOW)
        out_rest[side][:, 2 * width :] = cols


def qkv_back(branch, d_middle, start, normed, seen, eye, gains, sums_ff, sums_p, spread, pairs):
    rows, width = branch.shape[0], D // 2
    return on_chip(
        qkv_back_kernel,
        [branch, d_middle, start, normed, seen, eye, gains, sums_ff, sums_p, spread]
        + [value for pair in pairs for value in pair],
        [((D, 3 * width), LOW)] * 2 + [((D, 2 * width + LANES), LOW)] * 2,
        [((rows, D), WIDE), ((D, rows), LOW), ((rows, D), LOW), ((8, D), WIDE)],
        rows * D * D * 10,
    )


def row_spans(rows, chunk, body):
    def step(number, carry):
        body(pl.ds(pl.multiple_of(number * chunk, chunk), chunk))
        return carry

    lax.fori_loop(0, rows // chunk, step, 0)


def heads_forward(query_ref, keys_ref, values_ref, out_ref, bias, size, at):
    width = out_ref.shape[1]

    def step(block, carry):
        cols = [pl.multiple_of(first + block * LANES, LANES) for first in at]
        query = query_ref[:, pl.ds(cols[0], LANES)]
        keys = keys_ref[:, pl.ds(cols[1], LANES)]
        values = values_ref[:, pl.ds(cols[2], LANES)]
        found = []
        for low in range(0, LANES, size):
            part = slice(low, low + size)
            found.append(head_forward(query[:, part], keys[:, part], values[:, part], bias, size))
        place_at = pl.ds(pl.multiple_of(block * LANES, LANES), LANES)
        out_ref[:, place_at] = jnp.concatenate(found, -1).astype(LOW)
        return carry

    lax.fori_loop(0, width // LANES, step, 0)


def ctx_kernel(size, *refs):
    seen, pos, gains, ids_row, ids_col = refs[0:5]
    orders, rests, qkvs = refs[5:7], refs[7:9], refs[9:11]
    start, normed, middle, normed_two = refs[11:15]
    projs, mixeds = refs[15:17], refs[17:19]
    embed_w = refs[19]
    width = orders[0].shape[0]
    rows = seen.shape[0]
    embed_w[...] = (
        mm(rests[0][:, 0:width], orders[0][...]) + mm(rests[1][:, 0:width], orders[1][...])
    ).astype(LOW)
    start[...] = mm(seen[...], embed_w[...]) + pos[...]

    def first_norm(span):
        normed[span, :] = norm_rows(start[span, :], gains[0:1, :], gains[1:2, :]).astype(LOW)

    row_spans(rows, CHUNK, first_norm)
    bias = jnp.where(ids_col[...] == ids_row[...], 0.0, -1e30)
    for side in (0, 1):
        projs[side][...] = mm(normed[...], qkvs[side][...]).astype(LOW)
        heads_forward(
            projs[side], projs[side], projs[side], mixeds[side], bias, size, (0, width, 2 * width)
        )
    middle[...] = (
        start[...]
        + mm_t(mixeds[0][...], rests[0][:, width : 2 * width])
        + mm_t(mixeds[1][...], rests[1][:, width : 2 * width])
    )

    def second_norm(span):
        normed_two[span, :] = norm_rows(middle[span, :], gains[2:3, :], gains[3:4, :]).astype(LOW)

    row_spans(rows, CHUNK, second_norm)


def ctx_forward(size, seen, pos, gains, ids, orders, rests, qkvs):
    rows, width = seen.shape[0], orders[0].shape[0]
    return on_chip(
        functools.partial(ctx_kernel, size),
        [seen, pos, gains, ids[None, :], ids[:, None], *orders, *rests, *qkvs],
        [((rows, D), WIDE), ((rows, D), LOW), ((rows, D), WIDE), ((rows, D), LOW)]
        + [((rows, 3 * width), LOW)] * 2
        + [((rows, width), LOW)] * 2,
        [((D, D), LOW)],
        rows * D * D * 6 + D * D * D + rows * rows * D * 2,
        rows * rows * D // size,
    )


def gelu_rows(pre_ref, act_ref, slope_ref, span):
    def body(rows):
        act, slope = gelu_both(pre_ref[rows, :])
        act_ref[rows, span] = act
        if slope_ref is not None:
            slope_ref[rows, span] = slope

    row_spans(pre_ref.shape[0], 32, body)


def ff_kernel(*refs):
    normed, middle, gains, ups, downs = *refs[0:3], refs[3:5], refs[5:7]
    hidden, context, acts, slopes, pre = refs[7], refs[8], refs[9:11], refs[11:13], refs[13]
    rows, ff = acts[0].shape
    for side in (0, 1):

        def first(span, side=side):
            pre[...] = mm(normed[...], ups[side][:, span])
            gelu_rows(pre, acts[side], slopes[side], span)

        tiles(ff, 512, first)
    hidden[...] = (
        middle[...] + mm_t(acts[0][...], downs[0][...]) + mm_t(acts[1][...], downs[1][...])
    )

    def last(span):
        context[span, :] = norm_rows(hidden[span, :], gains[4:5, :], gains[5:6, :]).astype(LOW)

    row_spans(rows, CHUNK, last)


def ff_forward(normed, middle, gains, ups, downs):
    rows, ff = normed.shape[0], ups[0].shape[1]
    return on_chip(
        ff_kernel,
        [normed, middle, gains, *ups, *downs],
        [((rows, D), WIDE), ((rows, D), LOW)] + [((rows, ff), LOW)] * 4,
        [((rows, 512), WIDE)],
        rows * D * ff * 4 + rows * D * D,
        rows * ff * 2,
    )


def target_kernel(size, *refs):
    patch, seen, pos_all, pos_tgt, gains, ids_row, ids_col = refs[0:7]
    orders, weights, (t_middle, t_two), (embed_w, hidden, normed, start, query, keys, mixed) = (
        refs[7:9],
        refs[9:11],
        refs[11:13],
        refs[13:],
    )
    width = D // 2
    own, other = [part[:, 3 * width : 4 * width] for part in weights]
    embed_w[...] = (mm(own, orders[0][...]) + mm(other, orders[1][...])).astype(LOW)
    hidden[...] = mm(patch[...], embed_w[...]) + pos_all[...]

    def first_norm(span):
        normed[span, :] = norm_rows(hidden[span, :], gains[0:1, :], gains[1:2, :]).astype(LOW)

    row_spans(patch.shape[0], 112, first_norm)
    start[...] = mm(seen[...], embed_w[...]) + pos_tgt[...]
    t_normed = norm_rows(start[...], gains[0:1, :], gains[1:2, :]).astype(LOW)
    bias = jnp.where(ids_col[...] == ids_row[...], 0.0, -1e30)
    total = start[...]
    for part in weights:
        query[...] = mm(t_normed, part[:, 0:width]).astype(LOW)
        keys[...] = mm(normed[...], part[:, width : 3 * width]).astype(LOW)
        heads_forward(query, keys, keys, mixed, bias, size, (0, 0, width))
        total = total + mm_t(mixed[...], part[:, 4 * width : 5 * width])
    t_middle[...] = total
    t_two[...] = norm_rows(total, gains[2:3, :], gains[3:4, :]).astype(LOW)


def target_forward(
    size, patch, seen, pos_all, pos_tgt, gains, idq, idk, orders, weights
):
    rows, count, width = seen.shape[0], patch.shape[0], D // 2
    return on_chip(
        functools.partial(target_kernel, size),
        [patch, seen, pos_all, pos_tgt, gains, idq[None, :], idk[:, None], *orders, *weights],
        [((rows, D), WIDE), ((rows, D), LOW)],
        [
            ((D, D), LOW),
            ((count, D), WIDE),
            ((count, D), LOW),
            ((rows, D), WIDE),
            ((rows, width), LOW),
            ((count, 2 * width), LOW),
            ((rows, width), LOW),
        ],
        count * D * D * 3 + rows * D * D * 3 + 2 * rows * count * D,
        rows * count * D // size,
    )


def pred_forward_kernel(size, *refs):
    context, bridge_in, bridge_out, pos, gains, ids_row, ids_col = refs[0:7]
    downs, ups, qks, rights = refs[7:9], refs[9:11], refs[11:13], refs[13:15]
    joined, normed, middle, normed_two, predicted, final, guess = refs[15:22]
    out_qk, out_v, mixeds, acts, slopes = (
        refs[22:24],
        refs[24:26],
        refs[26:28],
        refs[28:30],
        refs[30:32],
    )
    width = out_v[0].shape[1]
    rows = middle.shape[0]
    joined[0:CTX, :] = mm(context[...], bridge_in[...]) + pos[0:CTX, :]
    joined[CTX:, :] = gains[6:7, :] + pos[CTX:, :]

    def first(span):
        normed[span, :] = norm_rows(joined[span, :], gains[0:1, :], gains[1:2, :]).astype(LOW)

    row_spans(joined.shape[0], 128, first)
    bias = jnp.where(ids_col[...] == ids_row[...], 0.0, -1e30)
    total = joined[CTX:, :]
    for qk, right, qk_ref, v_ref, mixed in zip(qks, rights, out_qk, out_v, mixeds):
        qk_ref[...] = mm(normed[...], qk[...]).astype(LOW)
        v_ref[...] = mm(normed[...], right[:, 0:width]).astype(LOW)
        found = []
        for low in range(0, width, size):
            found.append(
                head_forward(
                    qk_ref[CTX:, low : low + size],
                    qk_ref[:, width + low : width + low + size],
                    v_ref[:, low : low + size],
                    bias,
                    size,
                )
            )
        mixed[...] = jnp.concatenate(found, -1).astype(LOW)
        total = total + mm_t(mixed[...], right[:, width:])
    middle[...] = total
    normed_two[...] = norm_rows(total, gains[2:3, :], gains[3:4, :]).astype(LOW)
    total = middle[...]
    for up, down, act, slope in zip(ups, downs, acts, slopes):
        values, tilt = gelu_both(mm(normed_two[...], up[...]))
        act[...] = values
        slope[...] = tilt
        total = total + mm_t(act[...], down[...])
    predicted[...] = total
    final[...] = norm_rows(total, gains[4:5, :], gains[5:6, :]).astype(LOW)
    guess[...] = mm_t(final[...], bridge_out[...])


def pred_forward(
    size, context, bridge_in, bridge_out, pos, gains, idq, idk, downs, ups, qks, rights
):
    rows, count, width, ff = idq.shape[0], idk.shape[0], qks[0].shape[1] // 2, ups[0].shape[1]
    low, wide = LOW, WIDE
    return on_chip(
        functools.partial(pred_forward_kernel, size),
        [context, bridge_in, bridge_out, pos, gains, idq[None, :], idk[:, None]]
        + [*downs, *ups, *qks, *rights],
        [((count, PW), wide), ((count, PW), low), ((rows, PW), wide), ((rows, PW), low)]
        + [((rows, PW), wide), ((rows, PW), low), ((rows, D), wide)]
        + [((count, 2 * width), low)] * 2
        + [((count, width), low)] * 2
        + [((rows, width), low)] * 2
        + [((rows, ff), low)] * 4,
        [],
        1_000_000_000,
        rows * count * PW // size,
    )


def target_ff_kernel(t_two, t_middle, gains, *refs):
    ups, downs, (target, pre, act, total) = refs[0:2], refs[2:4], refs[4:8]
    total[...] = t_middle[...]
    for up, down in zip(ups, downs):

        def first(span, up=up):
            pre[...] = mm(t_two[...], up[:, span])
            gelu_rows(pre, act, None, span)

        tiles(act.shape[1], 512, first)
        total[...] = total[...] + mm_t(act[...], down[...])
    chosen = norm_rows(total[...], gains[4:5, :], gains[5:6, :])
    target[...] = norm_rows(chosen, 1.0, 0.0)


def target_ff(t_two, t_middle, gains, ups, downs):
    rows, ff = t_two.shape[0], ups[0].shape[1]
    return on_chip(
        target_ff_kernel,
        [t_two, t_middle, gains, *ups, *downs],
        [((rows, D), WIDE)],
        [((rows, 512), WIDE), ((rows, ff), LOW), ((rows, D), WIDE)],
        rows * D * ff * 4,
        rows * ff * 2,
    )[0]


def pred_back_all_kernel(size, count_all, *refs):
    (guess, target, used, context, final, bridge_in, bridge_out, gains, ids_row, ids_col) = refs[
        0:10
    ]
    predicted, middle, joined, normed, normed_two = refs[10:15]
    downs, ups, qks, rights = refs[15:17], refs[17:19], refs[19:21], refs[21:23]
    acts, slopes, in_qk, in_v, mixeds = (
        refs[23:25],
        refs[25:27],
        refs[27:29],
        refs[29:31],
        refs[31:33],
    )
    loss, d_inward, g_bridge_in, g_bridge_out, sums = refs[33:38]
    g_left, g_right = refs[38:40], refs[40:42]
    d_qk, d_v, d_normed = refs[42:45]
    width = in_v[0].shape[1]
    ff = acts[0].shape[1]
    diff = guess[...] - target[...]
    size_abs = jnp.abs(diff)
    keep = lax.broadcasted_iota(jnp.int32, diff.shape, 0) < used[0]
    terms = jnp.where(
        keep, jnp.where(size_abs < 1.0, 0.5 * diff * diff, size_abs - 0.5), 0.0
    )
    loss[...] = jnp.sum(jnp.sum(terms, 0, keepdims=True), 1, keepdims=True)
    d_guess = jnp.where(keep, jnp.clip(diff, -1.0, 1.0) / count_all, 0.0).astype(LOW)
    g_bridge_out[...] = t_mm(d_guess, final[...]).astype(LOW)

    def back(values, gain, grad, at):
        d_values, gain_sum, shift_sum = norm_back(values, gain, grad)
        sums[at : at + 1, :] = gain_sum[None, :]
        sums[at + 1 : at + 2, :] = shift_sum[None, :]
        return d_values

    d_tail = back(predicted[...], gains[4:5, :], mm(d_guess, bridge_out[...]), 4)
    branch = d_tail.astype(LOW)
    total = None
    for side in (0, 1):
        d_pre = (mm(branch, downs[side][...]) * slopes[side][...].astype(WIDE)).astype(LOW)
        g_left[side][:, 0:ff] = t_mm(branch, acts[side][...]).astype(LOW)
        g_right[side][:, 0:ff] = t_mm(normed_two[...], d_pre).astype(LOW)
        part = mm_t(d_pre, ups[side][...])
        total = part if total is None else total + part
    d_middle = d_tail + back(middle[...], gains[2:3, :], total, 2)
    branch = d_middle.astype(LOW)
    bias = jnp.where(ids_col[...] == ids_row[...], 0.0, -1e30)
    total = None
    for side in (0, 1):
        qk_ref, v_ref, right = in_qk[side], in_v[side], rights[side]
        d_mixed = mm(branch, right[:, width:]).astype(LOW)
        g_right[side][:, ff + width :] = t_mm(branch, mixeds[side][...]).astype(LOW)
        found = []
        for low in range(0, width, size):
            found.append(
                head_backward(
                    qk_ref[CTX:, low : low + size],
                    qk_ref[:, width + low : width + low + size],
                    v_ref[:, low : low + size],
                    d_mixed[:, low : low + size],
                    bias,
                    size,
                )
            )
        d_query, d_keys, d_values = [jnp.concatenate(parts, -1) for parts in zip(*found)]
        d_qk[0:CTX, 0:width] = jnp.zeros((CTX, width), LOW)
        d_qk[CTX:, 0:width] = d_query
        d_qk[:, width:] = d_keys
        d_v[...] = d_values
        g_left[side][:, ff:] = t_mm(normed[...], d_qk[...]).astype(LOW)
        g_right[side][:, ff : ff + width] = t_mm(normed[...], d_v[...]).astype(LOW)
        part = mm_t(d_qk[...], qks[side][...]) + mm_t(d_v[...], right[:, 0:width])
        d_normed[...] = part if side == 0 else d_normed[...] + part
    d_joined = back(joined[...], gains[0:1, :], d_normed[...], 0)
    sums[6:7, :] = jnp.sum(d_joined[CTX:] + d_middle, 0, keepdims=True)
    sums[7:8, :] = jnp.zeros((1, PW), WIDE)
    d_inward[...] = d_joined[0:CTX].astype(LOW)
    g_bridge_in[...] = t_mm(context[...], d_inward[...]).astype(LOW)


def pred_back_all(size, count_all, used, values, pairs, idq, idk):
    (guess, target, context, final, bridge_in, bridge_out, gains) = values[:7]
    ff, width, count = pairs[0][0].shape[1], pairs[2][0].shape[1] // 2, idk.shape[0]
    ins = [guess, target, used, context, final, bridge_in, bridge_out, gains]
    ins += [idq[None, :], idk[:, None], *values[7:]] + [part for pair in pairs for part in pair]
    outs = [((1, 1), WIDE), ((CTX, PW), LOW), ((D, PW), LOW), ((D, PW), LOW), ((8, PW), WIDE)]
    outs += [((PW, ff + 2 * width), LOW)] * 4
    specs = [WHOLE] * len(ins)
    specs[2] = pl.BlockSpec(memory_space=pltpu.SMEM)
    return pl.pallas_call(
        functools.partial(pred_back_all_kernel, size, count_all),
        in_specs=specs,
        out_specs=[WHOLE] * len(outs),
        out_shape=[jax.ShapeDtypeStruct(shape, kind) for shape, kind in outs],
        scratch_shapes=[
            pltpu.VMEM((count, 2 * width), LOW),
            pltpu.VMEM((count, width), LOW),
            pltpu.VMEM((count, PW), WIDE),
        ],
        cost_estimate=pl.CostEstimate(
            flops=4_000_000_000, bytes_accessed=20_000_000, transcendentals=3_000_000
        ),
        compiler_params=pltpu.CompilerParams(vmem_limit_bytes=56 * 1024 * 1024),
    )(*ins)


class Lines:
    def __init__(self, count):
        self.count = count
        self.stride = count // 4
        bits = list(range(self.stride.bit_length() - 1))
        turn = len(bits) // 2
        self.bits = bits
        self.orders = (bits, bits[turn:] + bits[:turn])
        self.turn = turn

    def flip(self, values, bit):
        pairs = [(at, at ^ (1 << bit)) for at in range(self.count)]
        return lax.ppermute(values, "dp", pairs)

    def shift(self, values, steps):
        pairs = [(at, (at + steps * self.stride) % self.count) for at in range(self.count)]
        return lax.ppermute(values, "dp", pairs)

    def order(self, index, width):
        rows = width // self.count
        column = jnp.arange(width)
        block = column // rows
        far = (block // self.stride - index // self.stride) % 4
        near = (block ^ index) % self.stride
        target = (near * 4 + far) * rows + column % rows
        return (target[:, None] == column).astype(LOW)


def swap(values):
    return lax.ppermute(values, "mp", [(0, 1), (1, 0)])


def swap_all(values):
    return [swap(value) for value in values]


def gather_far(lines, shards):
    wide = jnp.concatenate(shards, 1)
    found = [wide] + [lines.shift(wide, -steps) for steps in (1, 2, 3)]
    cut = shards[0].shape[1]
    return [jnp.stack([block[:, :cut] for block in found]), jnp.stack([block[:, cut:] for block in found])]


def gather_near(lines, held, phase):
    results = []
    for values, order in zip(held, lines.orders):
        done = list(order[: lines.turn]) if phase else []
        for bit in order[lines.turn :] if phase else order[: lines.turn]:
            axis = sum(1 for other in done if other > bit)
            values = jnp.stack([values, lines.flip(values, bit)], axis)
            done.append(bit)
        results.append(values)
    return results


def flat(values):
    return values.reshape(-1, values.shape[-1])


class Terms:
    def __init__(self, lines, own, other, order, rows):
        self.lines, self.order, self.left, self.rows = lines, order, list(lines.bits), rows
        self.terms = [[own, []]]
        self.other = other

    def shaped(self, values):
        return values.reshape((2,) * len(self.lines.bits) + (4, self.rows, values.shape[-1]))

    def total(self, *last):
        found = None
        for values, axes, *_ in self.terms:
            for axis, at in [(axis, 0) for axis in axes] + list(last):
                values = lax.index_in_dim(values, at, axis, keepdims=False)
            values = values.astype(WIDE)
            found = values if found is None else found + values
        return found

    def swap(self):
        self.terms = [[self.shaped(self.terms[0][0]), [], True], [self.shaped(swap(self.other)), []]]
        self.other = None

    def near(self, phase):
        turn = self.lines.turn
        for bit in self.order[turn:] if phase else self.order[:turn]:
            axis = sum(1 for other in self.left if other > bit)
            self.left.remove(bit)
            got = self.lines.flip(self.total((axis, 1)).astype(LOW), bit)
            for term in self.terms:
                term[1].append(axis)
            self.terms.append([got, []])

    def far(self):
        got = [
            self.lines.shift(self.total((0, steps)).astype(LOW), steps) for steps in (1, 2, 3)
        ]
        for term in self.terms:
            term[1].append(0)
        self.terms += [[values, []] for values in got]

    def hold(self):
        self.fresh = [term for term in self.terms if len(term) == 2]
        return [term[0] for term in self.fresh] + ([] if self.other is None else [self.other])

    def keep(self, values):
        for term, value in zip(self.fresh, values):
            term[0] = value
            term.append(True)
        if self.other is not None:
            self.other = values[-1]


class Sums:
    def __init__(self, lines, own, other, rows):
        self.parts = [
            Terms(lines, mine, rest, order, rows)
            for mine, rest, order in zip(own, other, lines.orders)
        ]

    def swap(self):
        for part in self.parts:
            part.swap()

    def near(self, phase):
        for part in self.parts:
            part.near(phase)

    def far(self):
        for part in self.parts:
            part.far()

    def hold(self):
        return [part.hold() for part in self.parts]

    def keep(self, values):
        for part, value in zip(self.parts, values):
            part.keep(value)

    def results(self):
        return [part.total() for part in self.parts]


def fence_sums(sums, *values):
    held, values = lax.optimization_barrier(([one.hold() for one in sums], values))
    for one, value in zip(sums, held):
        one.keep(value)
    return values


def reduce_swap(own, other):
    return [
        (mine.astype(WIDE) + swap(rest).astype(WIDE)).astype(LOW)
        for mine, rest in zip(own, other)
    ]


def fence(*values):
    return lax.optimization_barrier(values)


def adam(weight, moment_one, moment_two, gradient, decay, rate):
    moment_one = BETA_ONE * moment_one + (1.0 - BETA_ONE) * gradient
    moment_two = BETA_TWO * moment_two + (1.0 - BETA_TWO) * gradient * gradient
    fixed_one = moment_one / (1.0 - BETA_ONE**STEP)
    fixed_two = moment_two / (1.0 - BETA_TWO**STEP)
    weight = weight - rate * (fixed_one / (jnp.sqrt(fixed_two) + EPSILON) + decay * weight)
    return [weight, moment_one, moment_two]


def two_parts(values):
    high = lax.reduce_precision(values, 8, 7)
    return jnp.concatenate([high, values - high], 1).astype(LOW)


def widen_rows(values, rows):
    return jnp.pad(values, ((0, rows - values.shape[0]), (0, 0)))


def shards(
    patches,
    ctx_index,
    tgt_index,
    group,
    tgt_count,
    embed,
    embed_m,
    embed_v,
    bridge,
    bridge_m,
    bridge_v,
    enc_in,
    enc_in_m,
    enc_in_v,
    enc_out,
    enc_out_m,
    enc_out_v,
    enc_gains,
    enc_gains_m,
    enc_gains_v,
    pred_in,
    pred_in_m,
    pred_in_v,
    pred_out,
    pred_out_m,
    pred_out_v,
    pred_gains,
    pred_gains_m,
    pred_gains_v,
    t_embed,
    t_in,
    t_out,
    t_gains,
):
    index = lax.axis_index("dp")
    side = lax.axis_index("mp")
    dp_count = lax.axis_size("dp")
    lines = Lines(dp_count)
    assert patches.shape[0] == lax.axis_size("mp")
    count = patches.shape[0] * dp_count * TGT * D
    rows = D // dp_count
    p_rows = PW // dp_count
    half_d = D // 2
    local = D // 2
    ff = enc_in.shape[1] - 3 * local
    p_local = PW // 2
    p_ff = pred_in.shape[1] - 3 * p_local
    first = side == 0
    size = D // HEADS
    p_size = PW // PHEADS

    def own_half(values):
        return lax.dynamic_slice_in_dim(values, side * half_d, half_d, 1).astype(LOW)

    gains_pack = jnp.concatenate(
        [
            two_parts(enc_gains.T),
            two_parts(t_gains.T),
            widen_rows(two_parts(pred_gains.T), rows),
            jnp.zeros((rows, LANES - 38), LOW),
        ],
        1,
    )
    enc_in_low, t_in_low = enc_in.astype(LOW), t_in.astype(LOW)
    enc_out_low, t_out_low = enc_out.T.astype(LOW), t_out.T.astype(LOW)
    pred_in_low, pred_out_low = pred_in.astype(LOW), pred_out.T.astype(LOW)
    pred_main = jnp.concatenate([pred_out_low[:, p_local:], pred_in_low[:, 3 * p_local :]], 0)
    pred_rest = jnp.concatenate(
        [
            pred_in_low[:, : 2 * p_local],
            jnp.concatenate(
                [pred_in_low[:, 2 * p_local : 3 * p_local], pred_out_low[:, :p_local]], 1
            ),
        ],
        0,
    )
    packs = [
        [
            enc_in_low[:, : 3 * local],
            jnp.concatenate([own_half(embed), enc_out_low[:, :local], gains_pack], 1),
        ],
        [enc_in_low[:, 3 * local :], enc_out_low[:, local:]],
        [
            jnp.concatenate(
                [t_in_low[:, : 3 * local], own_half(t_embed), t_out_low[:, :local]], 1
            ),
            jnp.concatenate([own_half(bridge), pred_main, pred_rest], 1),
        ],
        [t_in_low[:, 3 * local :], t_out_low[:, local:]],
    ]

    order = lines.order(index, D)
    p_order = lines.order(index, PW)
    eye = jnp.eye(D, dtype=LOW)
    patch = lax.dynamic_index_in_dim(patches, side, 0, keepdims=False)
    ctx = lax.dynamic_index_in_dim(ctx_index, side, 0, keepdims=False)
    tgt = lax.dynamic_index_in_dim(tgt_index, side, 0, keepdims=False)
    single = lax.dynamic_index_in_dim(group, side, 0, keepdims=False) == 1
    used = lax.dynamic_index_in_dim(tgt_count, side, 0, keepdims=False)
    positions = jnp.arange(patch.shape[0])
    chosen = jnp.concatenate([ctx, tgt])
    all_id, all_row, all_col = place(single, positions)
    joined_id, joined_row, joined_col = place(single, chosen)
    ctx_id, tgt_id = joined_id[:CTX], joined_id[CTX:]

    far_a = gather_far(lines, packs[0])
    pos_all = sincos(all_row, all_col, D, order)
    pos_joined = sincos(joined_row, joined_col, D, order)
    pos_small = sincos(joined_row, joined_col, PW, p_order)
    patch = mm(patch, order).astype(LOW)
    seen = mm((chosen[:, None] == positions).astype(LOW), patch).astype(LOW)
    far_a, packs[1] = fence(far_a, packs[1])
    near_a = gather_near(lines, far_a, 0)
    near_a, packs[1] = fence(near_a, packs[1])
    held_a = gather_near(lines, near_a, 1)
    far_b = gather_far(lines, packs[1])
    held_a, far_b, pos_all, pos_joined, pos_small, patch, seen, packs[2] = fence(
        held_a, far_b, pos_all, pos_joined, pos_small, patch, seen, packs[2]
    )
    other_a = swap_all(held_a)
    near_b = gather_near(lines, far_b, 0)
    held_a, other_a, near_b, packs[2] = fence(held_a, other_a, near_b, packs[2])

    def widths(values, *sizes):
        found, at = [], 0
        for wide in sizes:
            found.append(values[:, at : at + wide])
            at += wide
        return found

    enc_qkv = (flat(held_a[0]), flat(other_a[0]))
    enc_rest = (flat(held_a[1]), flat(other_a[1]))
    gains_w = enc_rest[0][:, 2 * local :]
    gains_wide = gains_w.astype(WIDE)
    enc_gain = (gains_wide[:, 0:6] + gains_wide[:, 6:12]).T
    target_gain = (gains_wide[:, 12:18] + gains_wide[:, 18:24]).T
    pred_wide = gains_wide.reshape(dp_count, rows, LANES)[:, :p_rows].reshape(PW, LANES)
    pred_gain = (pred_wide[:, 24:31] + pred_wide[:, 31:38]).T
    order_own = lax.dynamic_slice_in_dim(order, side * half_d, half_d, 0)
    order_other = lax.dynamic_slice_in_dim(order, (1 - side) * half_d, half_d, 0)

    held_b = gather_near(lines, near_b, 1)
    far_c = gather_far(lines, packs[2])
    start, normed_one, middle, normed_two, *pairs = ctx_forward(
        size,
        seen[:CTX],
        pos_joined[:CTX],
        enc_gain,
        ctx_id,
        (order_own, order_other),
        enc_rest,
        enc_qkv,
    )
    projected, mixed = pairs[:2], pairs[2:]
    held_b, far_c, normed_two, middle, packs[3] = fence(
        held_b, far_c, normed_two, middle, packs[3]
    )
    other_b = swap_all(held_b)
    near_c = gather_near(lines, far_c, 0)
    held_b, other_b, near_c, packs[3] = fence(held_b, other_b, near_c, packs[3])
    held_c = gather_near(lines, near_c, 1)
    far_d = gather_far(lines, packs[3])
    enc_up, enc_down = [(flat(own), flat(other)) for own, other in zip(held_b, other_b)]
    hidden, context, *pairs = ff_forward(
        normed_two, middle, enc_gain, enc_up, enc_down
    )
    activated, slope = pairs[:2], pairs[2:]
    held_c, far_d, hidden, context, activated, slope = fence(
        held_c, far_d, hidden, context, activated, slope
    )
    other_c = swap_all(held_c)
    near_d = gather_near(lines, far_d, 0)
    held_c, other_c, near_d = fence(held_c, other_c, near_d)
    held_d = gather_near(lines, near_d, 1)
    t_middle, t_two = target_forward(
        size,
        patch,
        seen[CTX:],
        pos_all,
        pos_joined[CTX:],
        target_gain,
        tgt_id,
        all_id,
        (order_own, order_other),
        (flat(held_c[0]), flat(other_c[0])),
    )
    held_d, t_two, t_middle = fence(held_d, t_two, t_middle)
    other_d = swap_all(held_d)

    pred_all = [flat(part[1]) for part in (held_c, other_c)]
    bridges = [part[:, :local] for part in pred_all]
    main = [part[:, local : 3 * local].reshape(dp_count, 2, p_rows, -1) for part in pred_all]
    rest = [part[:, 3 * local :].reshape(dp_count, 2, p_rows, -1) for part in pred_all]
    bridge_in = mm(jnp.where(first, bridges[0], bridges[1]), p_order).astype(LOW)
    bridge_out = mm(jnp.where(first, bridges[1], bridges[0]), p_order).astype(LOW)
    pred_down = [flat(part[:, 0]) for part in main]
    pred_up = [flat(part[:, 1]) for part in main]
    pred_qk = [flat(part[:, 0]) for part in rest]
    pred_right = [flat(part[:, 1]) for part in rest]
    (
        joined,
        p_normed_one,
        p_middle,
        p_normed_two,
        predicted,
        final,
        guess,
        *pairs,
    ) = pred_forward(
        p_size,
        context,
        bridge_in,
        bridge_out,
        pos_small,
        pred_gain,
        tgt_id,
        joined_id,
        pred_down,
        pred_up,
        pred_qk,
        pred_right,
    )
    p_qk, p_values, p_mixed, p_activated, p_slope = [
        pairs[at : at + 2] for at in range(0, 10, 2)
    ]
    other_d, guess = fence(other_d, guess)
    target = target_ff(
        t_two,
        t_middle,
        target_gain,
        (flat(held_d[0]), flat(other_d[0])),
        (flat(held_d[1]), flat(other_d[1])),
    )
    (
        loss_local,
        d_inward,
        grad_bridge_in,
        grad_bridge_out,
        sums_pred,
        *pairs,
    ) = pred_back_all(
        p_size,
        count,
        used[None],
        [
            guess,
            target,
            context,
            final,
            bridge_in,
            bridge_out,
            pred_gain,
            predicted,
            p_middle,
            joined,
            p_normed_one,
            p_normed_two,
        ],
        [
            pred_down,
            pred_up,
            pred_qk,
            pred_right,
            p_activated,
            p_slope,
            p_qk,
            p_values,
            p_mixed,
        ],
        tgt_id,
        joined_id,
    )
    loss_local = loss_local[0, 0]
    grads_left, grads_right = pairs[:2], pairs[2:]

    def blocks(values):
        return values.reshape(dp_count, p_rows, -1)

    bridge_pair = [
        mm_t(jnp.where(first, low, high), p_order).astype(LOW).reshape(dp_count, rows, -1)
        for low, high in (
            (grad_bridge_in, grad_bridge_out),
            (grad_bridge_out, grad_bridge_in),
        )
    ]
    pair_p = [
        [
            jnp.concatenate([blocks(grads_left[at]), bridge_pair[at][:, :p_rows]], 2),
            jnp.concatenate([blocks(grads_right[at]), bridge_pair[at][:, p_rows:]], 2),
        ]
        for at in (0, 1)
    ]
    sum_p = Sums(lines, *pair_p, p_rows)
    (d_inward,) = fence_sums([sum_p], d_inward)
    sum_p.swap()
    *pairs, branch, d_middle, sums_ff = ff_back(
        d_inward,
        bridge_in,
        hidden,
        middle,
        normed_two,
        eye,
        enc_gain,
        activated,
        slope,
        enc_up,
        enc_down,
    )
    sum_f = Sums(lines, pairs[0:2], pairs[2:4], rows)
    branch, d_middle = fence_sums([sum_p, sum_f], branch, d_middle)
    sum_p.near(0)
    sum_f.swap()
    d_proj = attn_back(size, branch, ctx_id, enc_rest, projected)
    (d_proj,) = fence_sums([sum_p, sum_f], d_proj)
    sum_p.near(1)
    sum_f.near(0)
    spread = jnp.arange(D) // rows * p_rows + jnp.arange(D) % rows
    spread = (jnp.arange(PW)[:, None] == spread) & (jnp.arange(D) % rows < p_rows)
    qkv_own, qkv_other, rest_own, rest_other = qkv_back(
        branch,
        d_middle,
        start,
        normed_one,
        seen[:CTX],
        eye,
        enc_gain,
        sums_ff,
        sums_pred,
        spread.astype(LOW),
        [d_proj, mixed, enc_qkv, (order_own, order_other)],
    )
    sum_a = Sums(lines, [qkv_own, rest_own], [qkv_other, rest_other], rows)
    fence_sums([sum_p, sum_f, sum_a])
    sum_p.far()
    sum_a.swap()
    sum_f.near(1)
    fence_sums([sum_p, sum_f, sum_a])
    sum_f.far()
    sum_a.near(0)
    fence_sums([sum_f, sum_a])
    sum_a.near(1)
    fence_sums([sum_a])
    sum_a.far()

    red_left, red_right = sum_p.results()
    red_p_down, red_p_qk, bridge_top = widths(red_left, p_ff, 2 * p_local, half_d)
    red_p_up, red_p_v, red_p_attn, bridge_low = widths(red_right, p_ff, p_local, p_local, half_d)
    red_bridge = jnp.concatenate([bridge_top, bridge_low], 0)
    red_up, red_down = sum_f.results()
    red_qkv, red_rest = sum_a.results()
    red_embed, red_attn, red_gains = widths(red_rest, half_d, local, 16)
    red_pred_gains = red_gains[:p_rows, 8:15]
    split_squares = sum(
        jnp.sum(part * part)
        for part in (red_left, red_right, red_down, red_up, red_attn, red_qkv, red_embed)
    )
    shared_squares = jnp.sum(red_gains * red_gains)
    sums = jnp.stack([split_squares + shared_squares * 0.5, loss_local])
    for bit in range(dp_count.bit_length() - 1):
        sums = sums + lines.flip(sums, bit)
    sums = sums + swap(sums)
    square_sum, loss_sum = sums[0], sums[1]
    both = jnp.concatenate([red_embed, red_bridge], 1)
    both_other = swap(both)
    low = jnp.where(first, both, both_other)
    high = jnp.where(first, both_other, both)
    full_embed = jnp.concatenate([low[:, :half_d], high[:, :half_d]], 1)
    full_bridge = jnp.concatenate([low[:, half_d:], high[:, half_d:]], 1)
    grad_norm = jnp.sqrt(square_sum)
    factor = jnp.minimum(1.0, CLIP_NORM / (grad_norm + 1e-06))
    reduced = (
        full_embed,
        full_bridge,
        jnp.concatenate([red_qkv, red_up], 1),
        jnp.concatenate([red_attn, red_down], 1).T,
        red_gains[:, :6].T,
        jnp.concatenate([red_p_qk, red_p_v, red_p_up], 1),
        jnp.concatenate([red_p_attn, red_p_down], 1).T,
        red_pred_gains.T,
    )
    masters = (embed, bridge, enc_in, enc_out, enc_gains, pred_in, pred_out, pred_gains)
    firsts = (
        embed_m,
        bridge_m,
        enc_in_m,
        enc_out_m,
        enc_gains_m,
        pred_in_m,
        pred_out_m,
        pred_gains_m,
    )
    seconds = (
        embed_v,
        bridge_v,
        enc_in_v,
        enc_out_v,
        enc_gains_v,
        pred_in_v,
        pred_out_v,
        pred_gains_v,
    )
    results = []
    for index_pos in range(8):
        is_gain = index_pos in (4, 7)
        decay = 0.0 if is_gain else WEIGHT_DECAY
        rate = GAIN_RATE if is_gain else LEARN_RATE
        results.extend(
            adam(
                masters[index_pos],
                firsts[index_pos],
                seconds[index_pos],
                reduced[index_pos] * factor,
                decay,
                rate,
            )
        )
    return (
        results[0],
        results[1],
        results[2],
        results[3],
        results[4],
        results[5],
        results[6],
        results[7],
        results[8],
        results[9],
        results[10],
        results[11],
        results[12],
        results[13],
        results[14],
        results[15],
        results[16],
        results[17],
        results[18],
        results[19],
        results[20],
        results[21],
        results[22],
        results[23],
        loss_sum,
        grad_norm,
    )


def solution(mesh):
    in_specs = (
        P("dp", None, None),
        P("dp", None),
        P("dp", None),
        P("dp"),
        P("dp"),
        P("dp", None),
        P("dp", None),
        P("dp", None),
        P("dp", None),
        P("dp", None),
        P("dp", None),
        P("dp", "mp"),
        P("dp", "mp"),
        P("dp", "mp"),
        P("mp", "dp"),
        P("mp", "dp"),
        P("mp", "dp"),
        P(None, "dp"),
        P(None, "dp"),
        P(None, "dp"),
        P("dp", "mp"),
        P("dp", "mp"),
        P("dp", "mp"),
        P("mp", "dp"),
        P("mp", "dp"),
        P("mp", "dp"),
        P(None, "dp"),
        P(None, "dp"),
        P(None, "dp"),
        P("dp", None),
        P("dp", "mp"),
        P("mp", "dp"),
        P(None, "dp"),
    )
    out_specs = (
        P("dp", None),
        P("dp", None),
        P("dp", None),
        P("dp", None),
        P("dp", None),
        P("dp", None),
        P("dp", "mp"),
        P("dp", "mp"),
        P("dp", "mp"),
        P("mp", "dp"),
        P("mp", "dp"),
        P("mp", "dp"),
        P(None, "dp"),
        P(None, "dp"),
        P(None, "dp"),
        P("dp", "mp"),
        P("dp", "mp"),
        P("dp", "mp"),
        P("mp", "dp"),
        P("mp", "dp"),
        P("mp", "dp"),
        P(None, "dp"),
        P(None, "dp"),
        P(None, "dp"),
        P(),
        P(),
    )
    return jax.shard_map(shards, mesh=mesh, in_specs=in_specs, out_specs=out_specs, check_vma=False)
```

time: 2090 us -> 597 us (0.29)
  waiting for transfers between devices: 1050 us -> 99.3 us
  blocking collectives: 335 us -> 0 us
  matrix products: 315 us -> 16.3 us
  Pallas kernels: 0 us -> 194 us
  other arithmetic: 219 us -> 97.7 us
  starting transfers between devices: 1.92 us -> 86 us
  local copies, waits for them, and re-layouts: 140 us -> 83.4 us
    reduce_scatter x3 -> x0, waiting for transfers between devices: 428 us -> none  [the longest x1 166 us: shards(): lax.psum_scatter(grad_enc_in, 'dp', scatter_dimension=0, tiled=True)]
    unnamed x26 -> x0, waiting for transfers between devices: 402 us -> none
    dot_general x51 -> x10, matrix products: 315 us -> 16.3 us  [the longest x8 13.9 us: mm(): return jnp.dot(left, right, preferred_element_type=WIDE)]
    all_gather x5 -> x0, blocking collectives: 218 us -> none  [the longest x1 53.4 us: shards(): lax.all_gather(pred_in.astype(LOW), 'dp', axis=0, tiled=True)]
    pallas_call x0 -> x9, Pallas kernels: none -> 194 us  [the longest x8 168 us: on_chip(): pl.pallas_call(kernel, in_specs=[WHOLE] * len(ins), out_specs=[WHOLE] * l...]
    psum x8 -> x0, waiting for transfers between devices: 159 us -> none  [across(): return lax.psum(partial_sum, 'mp')]
    ppermute x0 -> x78, waiting for transfers between devices: none -> 99.3 us  [the longest x32 64.3 us: flip(): return lax.ppermute(values, 'dp', pairs)]
    ppermute x0 -> x78, starting transfers between devices: none -> 86 us  [the longest x30 47.1 us: shift(): return lax.ppermute(values, 'dp', pairs)]
  transfers between devices with their start and end apart: 22 -> 78, of which waited for: 16 -> 23; matrix products, arithmetic and copies ran while one was open for 16% -> 24% of each run, Pallas kernels for 0% -> 27%
where the time goes in v1:
time: 597 us; the launch traced here: 587 us
  Pallas kernels  194 us (32%)
  waiting for transfers between devices  99.3 us (17%)
  other arithmetic  97.7 us (16%)
  starting transfers between devices  86 us (14%)
  local copies, waits for them, and re-layouts  83.4 us (14%)
  matrix products  16.3 us (3%)
  between operations  10.5 us (2%)
    pallas_call x8, Pallas kernels, on_chip(): pl.pallas_call(kernel, in_specs=[WHOLE] * len(ins), out_specs=[WHOLE] * l...  168 us
    ppermute x32, waiting for transfers between devices, flip(): return lax.ppermute(values, 'dp', pairs)  64.3 us
    ppermute x30, starting transfers between devices, shift(): return lax.ppermute(values, 'dp', pairs)  47.1 us
    ppermute x32, starting transfers between devices, flip(): return lax.ppermute(values, 'dp', pairs)  35.1 us
    ppermute x30, waiting for transfers between devices, shift(): return lax.ppermute(values, 'dp', pairs)  33.8 us
    pallas_call x1, Pallas kernels, pred_back_all(): pl.pallas_call(functools.partial(pred_back_all_kernel, size, count_all),...  25.3 us
    another operation x16, other arithmetic, gather_near(): values = jnp.stack([values, lines.flip(values, bit)], axis)  22 us
    unnamed x245, local copies, waits for them, and re-layouts  21.5 us
  transfers between devices with their start and end apart: 78, of which 23 were waited for; matrix products, arithmetic and copies ran while one was open for 24% of the time, Pallas kernels for 27%

profile of v1, /device:TPU:0, one launch (start us, length us, event | category | flops | bytes accessed | tf_op | source)
XLA Modules:
  0.0 586.7 jit_solution(17962530751159064735)
XLA Ops:
  6.4 3.0 collective-permute-start.2
  43.2 3.8 fusion.7
  59.7 3.3 collective-permute-done.9
  63.1 9.5 %collective-permute-done.8 = bf16[48,3072]{1,0:T(8,128)(2,1)S(1)} collective-permute-done((bf16[48,3072]{1,0:T(8,128)(2,1)S(1)}, bf16[48,3072]{1,0:T(8,128)(2,1)S(1)}, u32[]{:S(2)}, u32[]{:S(2)}) %collective-permute-start.8) | collective-permute-done | bytes 294944 | tf_op jit(solution)/shard_map/ppermute | solution.py:721
  87.2 6.1 %collective-permute-done.12 = bf16[4,48,1536]{2,1,0:T(8,128)(2,1)} collective-permute-done((bf16[4,48,1536]{2,1,0:T(8,128)(2,1)S(1)}, bf16[4,48,1536]{2,1,0:T(8,128)(2,1)}, u32[]{:S(2)}, u32[]{:S(2)}) %collective-permute-start.12) | collective-permute-done | bytes 589856 | tf_op jit(solution)/shard_map/ppermute | solution.py:717
  100.2 5.8 collective-permute-start.18
  115.7 24.5 %shard_map.512 = (f32[512,768]{1,0:T(8,128)}, bf16[512,768]{1,0:T(8,128)(2,1)}, f32[512,768]{1,0:T(8,128)}, bf16[512,768]{1,0:T(8,128)(2,1)}, bf16[512,1152]{1,0...) custom-call(bf16[512,768]{1,0:T(8,128)(2,1)} %slice.998.refs_0_.refs_4_, ...), custom_call_target="tpu_custom_call" | custom-call | flops 5335154688 | bytes 17717248 | tf_op jit(solution)/shard_map/pallas_call | solution.py:141
  152.8 13.4 %collective-permute-done.22 = bf16[4,48,1536]{2,1,0:T(8,128)(2,1)S(1)} collective-permute-done((bf16[4,48,1536]{2,1,0:T(8,128)(2,1)S(1)}, bf16[4,48,1536]{2,1,0:T(8,128)(2,1)S(1)}, u32[]{:S(2)}, u32[]{:S(2)}) %collective-permute-start.22) | collective-permute-done | bytes 589856 | tf_op jit(solution)/shard_map/ppermute | solution.py:717
  166.4 3.3 collective-permute-done.21
  181.8 21.5 %shard_map.513 = (f32[512,768]{1,0:T(8,128)}, bf16[512,768]{1,0:T(8,128)(2,1)}, bf16[512,1536]{1,0:T(8,128)(2,1)}, bf16[512,1536]{1,0:T(8,128)(2,1)}, bf16[512,1...) custom-call(bf16[512,768]{1,0:T(8,128)(2,1)} %get-tuple-element.230.refs_0_.refs_4_, ...), custom_call_target="tpu_custom_call" | custom-call | flops 5435817984 | bytes 20465664 | tf_op jit(solution)/shard_map/pallas_call | solution.py:141
  214.6 12.4 %collective-permute-done.30 = bf16[4,48,1536]{2,1,0:T(8,128)(2,1)S(1)} collective-permute-done((bf16[4,48,1536]{2,1,0:T(8,128)(2,1)S(1)}, bf16[4,48,1536]{2,1,0:T(8,128)(2,1)S(1)}, u32[]{:S(2)}, u32[]{:S(2)}) %collective-permute-start.30) | collective-permute-done | bytes 589856 | tf_op jit(solution)/shard_map/ppermute | solution.py:717
  240.5 23.0 %shard_map.514 = (f32[256,768]{1,0:T(8,128)}, bf16[256,768]{1,0:T(8,128)(2,1)}) custom-call(bf16[784,768]{1,0:T(8,128)(2,1)} %fusion.6.refs_0_, bf16[256,768]{1,0:T(8,128)(2,1)} %slice.1012.refs_1_, f32[784,768]{1,0:T(8,128)} %fusion.201.refs_2_, f32[256,768]{1,0:T(8,128)} %slice.1013.refs_3_, f32[6,768]{1,0:T(8,128)} %get-tuple-element.537.refs_4_.gains, ...), custom_call_target="tpu_custom_call" | custom-call | flops 4297064448 | bytes 13072448 | tf_op jit(solution)/shard_map/pallas_call | solution.py:141
  263.5 2.9 pad_maximum_fusion.4
  266.4 3.3 pad_maximum_fusion.5
  281.5 17.6 %shard_map.515 = (f32[768,384]{1,0:T(8,128)}, bf16[768,384]{1,0:T(8,128)(2,1)}, f32[256,384]{1,0:T(8,128)}, bf16[256,384]{1,0:T(8,128)(2,1)}, f32[256,384]{1,0:T...) custom-call(bf16[512,768]{1,0:T(8,128)(2,1)} %get-tuple-element.256., ...), custom_call_target="tpu_custom_call" | custom-call | flops 2000000000 | bytes 13974016 | tf_op jit(solution)/shard_map/pallas_call | solution.py:141
  299.1 3.3 copy.220
  302.4 3.3 copy.221
  305.7 12.5 %shard_map.516.refs_1_ = f32[256,768]{1,0:T(8,128)} custom-call(bf16[256,768]{1,0:T(8,128)(2,1)} %get-tuple-element.262.t_two, f32[256,768]{1,0:T(8,128)} %get-tuple-element.263.t_middle, f32[6,768]{1,0:T(8,128)} %get-tuple-element.537.refs_4_.gains, bf16[768,1536]{1,0:T(8,128)(2,1)} %bitcast.109.refs_0_, bf16[768,1536]{1,0:T(8,128)(2,1)} %bitcast.110.refs_1_, ...), custom_call_target="tpu_custom_call" | custom-call | flops 2415919104 | bytes 11421696 | tf_op jit(solution)/shard_map/pallas_call | solution.py:141
  318.2 25.3 %shard_map.517 = (f32[1,1]{1,0:T(1,128)}, bf16[512,384]{1,0:T(8,128)(2,1)}, bf16[768,384]{1,0:T(8,128)(2,1)}, bf16[768,384]{1,0:T(8,128)(2,1)}, f32[8,384]{1,0:T...) custom-call(f32[256,768]{1,0:T(8,128)} %get-tuple-element.261.refs_0, ...), custom_call_target="tpu_custom_call" | custom-call | flops 4000000000 | bytes 20000000 | tf_op jit(solution)/shard_map/pallas_call | solution.py:688
  350.5 29.1 %shard_map.518 = (bf16[768,1536]{1,0:T(8,128)(2,1)}, bf16[768,1536]{1,0:T(8,128)(2,1)}, bf16[768,1536]{1,0:T(8,128)(2,1)}, bf16[768,1536]{1,0:T(8,128)(2,1)}, bf...) custom-call(bf16[512,384]{1,0:T(8,128)(2,1)} %get-tuple-element.292.refs_0_, ...), custom_call_target="tpu_custom_call" | custom-call | flops 9663676416 | bytes 33662976 | tf_op jit(solution)/shard_map/pallas_call | solution.py:141
  385.0 20.7 %shard_map.519 = (bf16[512,1152]{1,0:T(8,128)(2,1)}, bf16[512,1152]{1,0:T(8,128)(2,1)}) custom-call(bf16[512,768]{1,0:T(8,128)(2,1)} %get-tuple-element.309.branch.refs_0_, s32[1,512]{1,0:T(1,128)} %bitcast.619, s32[512,1]{1,0:T(8,128)} %copy.199.refs_4_.ids_col, bf16[768,896]{1,0:T(8,128)(2,1)} %bitcast.51.refs_7_.refs_0_, ...), custom_call_target="tpu_custom_call" | custom-call | flops 2617245696 | bytes 8261632 | tf_op jit(solution)/shard_map/pallas_call | solution.py:141
  418.5 19.4 %shard_map.520 = (bf16[768,1152]{1,0:T(8,128)(2,1)}, bf16[768,1152]{1,0:T(8,128)(2,1)}, bf16[768,896]{1,0:T(8,128)(2,1)}, bf16[768,896]{1,0:T(8,128)(2,1)}) custom-call(bf16[512,768]{1,0:T(8,128)(2,1)} %get-tuple-element.309.branch.refs_0_, f32[512,768]{1,0:T(8,128)} %get-tuple-element.320.refs_1_, f32[512,768]{1,0:T(8,128)} %get-tuple-element.321.refs_2_, ...), custom_call_target="tpu_custom_call" | custom-call | flops 6039797760 | bytes 21485568 | tf_op jit(solution)/shard_map/pallas_call | solution.py:141
  437.9 7.9 %collective-permute-done.42 = bf16[4,24,1536]{2,1,0:T(8,128)(2,1)} collective-permute-done((bf16[4,24,1536]{2,1,0:T(8,128)(2,1)}, bf16[4,24,1536]{2,1,0:T(8,128)(2,1)}, u32[]{:S(2)}, u32[]{:S(2)}) %collective-permute-start.42) | collective-permute-done | bytes 294944 | tf_op jit(solution)/shard_map/ppermute | solution.py:717
  449.3 2.8 collective-permute-start.48
  459.8 4.7 collective-permute-done.49
  464.5 5.9 %collective-permute-done.50 = bf16[24,1536]{1,0:T(8,128)(2,1)S(1)} collective-permute-done((bf16[24,1536]{1,0:T(8,128)(2,1)S(1)}, bf16[24,1536]{1,0:T(8,128)(2,1)S(1)}, u32[]{:S(2)}, u32[]{:S(2)}) %collective-permute-start.50) | collective-permute-done | bytes 73760 | tf_op jit(solution)/shard_map/ppermute | solution.py:721
  506.7 4.1 collective-permute-done.60
  525.5 3.6 collective-permute-start.68
  532.8 3.9 collective-permute-start.72
  537.3 4.8 collective-permute-done.67
  560.9 3.5 collective-permute-done.75
  564.5 4.4 collective-permute-done.76
  (600 shorter events, 263.7 us)
Async XLA Ops:
  6.4 26.5 %collective-permute-start.2 = (bf16[48,2048]{1,0:T(8,128)(2,1)}, bf16[48,2048]{1,0:T(8,128)(2,1)}, u32[]{:S(2)}, u32[]{:S(2)}) collective-permute-start(bf16[48,2048]{1,0:T(8,128)(2,1)} %concatenate.178), channel_id=1, source_target_pairs={{0,8},{2,10},{4,12},{6,14},{8,16},{10,18},{12,20},{14,22},{16,24},... | collective-permute-start | bytes 589832 | tf_op jit(solution)/shard_map/ppermute | solution.py:721
  9.4 24.4 %collective-permute-start.1 = (bf16[48,2048]{1,0:T(8,128)(2,1)}, bf16[48,2048]{1,0:T(8,128)(2,1)}, u32[]{:S(2)}, u32[]{:S(2)}) collective-permute-start(bf16[48,2048]{1,0:T(8,128)(2,1)} %concatenate.178), channel_id=1, source_target_pairs={{0,16},{2,18},{4,20},{6,22},{8,24},{10,26},{12,28},{14,30},{16,0},... | collective-permute-start | bytes 589832 | tf_op jit(solution)/shard_map/ppermute | solution.py:721
  12.0 22.7 %collective-permute-start = (bf16[48,2048]{1,0:T(8,128)(2,1)}, bf16[48,2048]{1,0:T(8,128)(2,1)}, u32[]{:S(2)}, u32[]{:S(2)}) collective-permute-start(bf16[48,2048]{1,0:T(8,128)(2,1)} %concatenate.178), channel_id=1, source_target_pairs={{0,24},{2,26},{4,28},{6,30},{8,0},{10,2},{12,4},{14,6},{16,8},{18,... | collective-permute-start | bytes 589832 | tf_op jit(solution)/shard_map/ppermute | solution.py:721
  77.3 21.5 %collective-permute-start.10 = (bf16[2,2,4,48,1152]{4,3,2,1,0:T(8,128)(2,1)}, bf16[2,2,4,48,1152]{4,3,2,1,0:T(8,128)(2,1)}, u32[]{:S(2)}, u32[]{:S(2)}) collective-permute-start(bf16[2,2,4,48,1152]{4,3,2,1,0:T(8,128)(2,1)} %pad_maximum_fusion.6), channel_id=1, source_target_pairs={{0,1},{1,0},{2,3},{3,2},{4,5},{5,4},{6,7},{7,6},{8,9},{9,8},{10,11... | collective-permute-start | bytes 5308424 | tf_op jit(solution)/shard_map/ppermute | solution.py:734
  77.4 21.5 %collective-permute-start.11 = (bf16[2,2,4,48,896]{4,3,2,1,0:T(8,128)(2,1)}, bf16[2,2,4,48,896]{4,3,2,1,0:T(8,128)(2,1)}, u32[]{:S(2)}, u32[]{:S(2)}) collective-permute-start(bf16[2,2,4,48,896]{4,3,2,1,0:T(8,128)(2,1)} %pad_maximum_fusion.8), channel_id=1, source_target_pairs={{0,1},{1,0},{2,3},{3,2},{4,5},{5,4},{6,7},{7,6},{8,9},{9,8},{10,11... | collective-permute-start | bytes 4128776 | tf_op jit(solution)/shard_map/ppermute | solution.py:734
  100.2 40.0 %collective-permute-start.18 = (bf16[48,3456]{1,0:T(8,128)(2,1)}, bf16[48,3456]{1,0:T(8,128)(2,1)}, u32[]{:S(2)}, u32[]{:S(2)}) collective-permute-start(bf16[48,3456]{1,0:T(8,128)(2,1)} %constant_dynamic-update-slice_fusion.2), channel_id=1, source_target_pairs={{0,8},{2,10},{4,12},{6,14},{8,16},{10,18},{12,20},{14,22},{16,24},... | collective-permute-start | bytes 995336 | tf_op jit(solution)/shard_map/ppermute | solution.py:721
  106.1 36.1 %collective-permute-start.17 = (bf16[48,3456]{1,0:T(8,128)(2,1)}, bf16[48,3456]{1,0:T(8,128)(2,1)}, u32[]{:S(2)}, u32[]{:S(2)}) collective-permute-start(bf16[48,3456]{1,0:T(8,128)(2,1)} %constant_dynamic-update-slice_fusion.2), channel_id=1, source_target_pairs={{0,16},{2,18},{4,20},{6,22},{8,24},{10,26},{12,28},{14,30},{16,0},... | collective-permute-start | bytes 995336 | tf_op jit(solution)/shard_map/ppermute | solution.py:721
  106.1 38.0 %collective-permute-start.16 = (bf16[48,3456]{1,0:T(8,128)(2,1)}, bf16[48,3456]{1,0:T(8,128)(2,1)}, u32[]{:S(2)}, u32[]{:S(2)}) collective-permute-start(bf16[48,3456]{1,0:T(8,128)(2,1)} %constant_dynamic-update-slice_fusion.2), channel_id=1, source_target_pairs={{0,24},{2,26},{4,28},{6,30},{8,0},{10,2},{12,4},{14,6},{16,8},{18,... | collective-permute-start | bytes 995336 | tf_op jit(solution)/shard_map/ppermute | solution.py:721
  108.6 37.5 %collective-permute-start.14 = (bf16[2,4,48,1536]{3,2,1,0:T(8,128)(2,1)S(1)}, bf16[2,4,48,1536]{3,2,1,0:T(8,128)(2,1)}, u32[]{:S(2)}, u32[]{:S(2)}) collective-permute-start(bf16[2,4,48,1536]{3,2,1,0:T(8,128)(2,1)S(1)} %pad_maximum_fusion.9), channel_id=1, source_target_pairs={{0,4},{2,6},{4,0},{6,2},{8,12},{10,14},{12,8},{14,10},{16,20},{18,... | collective-permute-start | bytes 3538952 | tf_op jit(solution)/shard_map/ppermute | solution.py:717
  110.1 37.5 %collective-permute-start.15 = (bf16[2,4,48,1536]{3,2,1,0:T(8,128)(2,1)}, bf16[2,4,48,1536]{3,2,1,0:T(8,128)(2,1)}, u32[]{:S(2)}, u32[]{:S(2)}) collective-permute-start(bf16[2,4,48,1536]{3,2,1,0:T(8,128)(2,1)} %pad_maximum_fusion.10), channel_id=1, source_target_pairs={{0,2},{2,0},{4,6},{6,4},{8,10},{10,8},{12,14},{14,12},{16,18},{18,... | collective-permute-start | bytes 3538952 | tf_op jit(solution)/shard_map/ppermute | solution.py:717
  171.9 31.4 %collective-permute-start.27 = (bf16[48,3072]{1,0:T(8,128)(2,1)}, bf16[48,3072]{1,0:T(8,128)(2,1)}, u32[]{:S(2)}, u32[]{:S(2)}) collective-permute-start(bf16[48,3072]{1,0:T(8,128)(2,1)} %constant_dynamic-update-slice_fusion.4), channel_id=1, source_target_pairs={{0,8},{2,10},{4,12},{6,14},{8,16},{10,18},{12,20},{14,22},{16,24},... | collective-permute-start | bytes 884744 | tf_op jit(solution)/shard_map/ppermute | solution.py:721
  171.9 32.4 %collective-permute-start.26 = (bf16[48,3072]{1,0:T(8,128)(2,1)}, bf16[48,3072]{1,0:T(8,128)(2,1)}, u32[]{:S(2)}, u32[]{:S(2)}) collective-permute-start(bf16[48,3072]{1,0:T(8,128)(2,1)} %constant_dynamic-update-slice_fusion.4), channel_id=1, source_target_pairs={{0,16},{2,18},{4,20},{6,22},{8,24},{10,26},{12,28},{14,30},{16,0},... | collective-permute-start | bytes 884744 | tf_op jit(solution)/shard_map/ppermute | solution.py:721
  174.5 30.9 %collective-permute-start.25 = (bf16[48,3072]{1,0:T(8,128)(2,1)}, bf16[48,3072]{1,0:T(8,128)(2,1)}, u32[]{:S(2)}, u32[]{:S(2)}) collective-permute-start(bf16[48,3072]{1,0:T(8,128)(2,1)} %constant_dynamic-update-slice_fusion.4), channel_id=1, source_target_pairs={{0,24},{2,26},{4,28},{6,30},{8,0},{10,2},{12,4},{14,6},{16,8},{18,... | collective-permute-start | bytes 884744 | tf_op jit(solution)/shard_map/ppermute | solution.py:721
  175.7 32.6 %collective-permute-start.23 = (bf16[2,4,48,1920]{3,2,1,0:T(8,128)(2,1)S(1)}, bf16[2,4,48,1920]{3,2,1,0:T(8,128)(2,1)S(1)}, u32[]{:S(2)}, u32[]{:S(2)}) collective-permute-start(bf16[2,4,48,1920]{3,2,1,0:T(8,128)(2,1)S(1)} %pad_maximum_fusion.7), channel_id=1, source_target_pairs={{0,4},{2,6},{4,0},{6,2},{8,12},{10,14},{12,8},{14,10},{16,20},{18,... | collective-permute-start | bytes 4423688 | tf_op jit(solution)/shard_map/ppermute | solution.py:717
  177.3 29.3 %collective-permute-start.24 = (bf16[2,4,48,1536]{3,2,1,0:T(8,128)(2,1)S(1)}, bf16[2,4,48,1536]{3,2,1,0:T(8,128)(2,1)S(1)}, u32[]{:S(2)}, u32[]{:S(2)}) collective-permute-start(bf16[2,4,48,1536]{3,2,1,0:T(8,128)(2,1)S(1)} %pad_maximum_fusion.11), channel_id=1, source_target_pairs={{0,2},{2,0},{4,6},{6,4},{8,10},{10,8},{12,14},{14,12},{16,18},{18,... | collective-permute-start | bytes 3538952 | tf_op jit(solution)/shard_map/ppermute | solution.py:717
  230.7 32.8 %collective-permute-start.32 = (bf16[2,4,48,1536]{3,2,1,0:T(8,128)(2,1)S(1)}, bf16[2,4,48,1536]{3,2,1,0:T(8,128)(2,1)}, u32[]{:S(2)}, u32[]{:S(2)}) collective-permute-start(bf16[2,4,48,1536]{3,2,1,0:T(8,128)(2,1)S(1)} %pad_maximum_fusion.12), channel_id=1, source_target_pairs={{0,4},{2,6},{4,0},{6,2},{8,12},{10,14},{12,8},{14,10},{16,20},{18,... | collective-permute-start | bytes 3538952 | tf_op jit(solution)/shard_map/ppermute | solution.py:717
  232.3 34.1 %collective-permute-start.33 = (bf16[2,4,48,1536]{3,2,1,0:T(8,128)(2,1)}, bf16[2,4,48,1536]{3,2,1,0:T(8,128)(2,1)}, u32[]{:S(2)}, u32[]{:S(2)}) collective-permute-start(bf16[2,4,48,1536]{3,2,1,0:T(8,128)(2,1)} %pad_maximum_fusion.13), channel_id=1, source_target_pairs={{0,2},{2,0},{4,6},{6,4},{8,10},{10,8},{12,14},{14,12},{16,18},{18,... | collective-permute-start | bytes 3538952 | tf_op jit(solution)/shard_map/ppermute | solution.py:717
  269.7 32.7 %collective-permute-start.34 = (bf16[2,2,4,48,1536]{4,3,2,1,0:T(8,128)(2,1)}, bf16[2,2,4,48,1536]{4,3,2,1,0:T(8,128)(2,1)}, u32[]{:S(2)}, u32[]{:S(2)}) collective-permute-start(bf16[2,2,4,48,1536]{4,3,2,1,0:T(8,128)(2,1)} %pad_maximum_fusion.4), channel_id=1, source_target_pairs={{0,1},{1,0},{2,3},{3,2},{4,5},{5,4},{6,7},{7,6},{8,9},{9,8},{10,11... | collective-permute-start | bytes 7077896 | tf_op jit(solution)/shard_map/ppermute | solution.py:734
  269.7 32.7 %collective-permute-start.35 = (bf16[2,2,4,48,1536]{4,3,2,0,1:T(8,128)(2,1)}, bf16[2,2,4,48,1536]{4,3,2,0,1:T(8,128)(2,1)}, u32[]{:S(2)}, u32[]{:S(2)}) collective-permute-start(bf16[2,2,4,48,1536]{4,3,2,0,1:T(8,128)(2,1)} %pad_maximum_fusion.5), channel_id=1, source_target_pairs={{0,1},{1,0},{2,3},{3,2},{4,5},{5,4},{6,7},{7,6},{8,9},{9,8},{10,11... | collective-permute-start | bytes 7077896 | tf_op jit(solution)/shard_map/ppermute | solution.py:734
  348.8 30.8 %collective-permute-start.36 = (bf16[16,24,1536]{2,1,0:T(8,128)(2,1)S(1)}, bf16[16,24,1536]{2,1,0:T(8,128)(2,1)S(1)}, u32[]{:S(2)}, u32[]{:S(2)}) collective-permute-start(bf16[16,24,1536]{2,1,0:T(8,128)(2,1)S(1)} %pad_maximum_fusion.15), channel_id=1, source_target_pairs={{0,1},{1,0},{2,3},{3,2},{4,5},{5,4},{6,7},{7,6},{8,9},{9,8},{10,11... | collective-permute-start | bytes 3538952 | tf_op jit(solution)/shard_map/ppermute | solution.py:734
  348.9 30.8 %collective-permute-start.37 = (bf16[16,24,1536]{2,1,0:T(8,128)(2,1)S(1)}, bf16[16,24,1536]{2,1,0:T(8,128)(2,1)S(1)}, u32[]{:S(2)}, u32[]{:S(2)}) collective-permute-start(bf16[16,24,1536]{2,1,0:T(8,128)(2,1)S(1)} %pad_maximum_fusion.17), channel_id=1, source_target_pairs={{0,1},{1,0},{2,3},{3,2},{4,5},{5,4},{6,7},{7,6},{8,9},{9,8},{10,11... | collective-permute-start | bytes 3538952 | tf_op jit(solution)/shard_map/ppermute | solution.py:734
  379.7 26.0 %collective-permute-start.40 = (bf16[768,1536]{1,0:T(8,128)(2,1)}, bf16[768,1536]{1,0:T(8,128)(2,1)}, u32[]{:S(2)}, u32[]{:S(2)}) collective-permute-start(bf16[768,1536]{1,0:T(8,128)(2,1)} %get-tuple-element.307), channel_id=1, source_target_pairs={{0,1},{1,0},{2,3},{3,2},{4,5},{5,4},{6,7},{7,6},{8,9},{9,8},{10,11... | collective-permute-start | bytes 7077896 | tf_op jit(solution)/shard_map/ppermute | solution.py:734
  379.8 25.9 %collective-permute-start.41 = (bf16[768,1536]{1,0:T(8,128)(2,1)}, bf16[768,1536]{1,0:T(8,128)(2,1)}, u32[]{:S(2)}, u32[]{:S(2)}) collective-permute-start(bf16[768,1536]{1,0:T(8,128)(2,1)} %get-tuple-element.308), channel_id=1, source_target_pairs={{0,1},{1,0},{2,3},{3,2},{4,5},{5,4},{6,7},{7,6},{8,9},{9,8},{10,11... | collective-permute-start | bytes 7077896 | tf_op jit(solution)/shard_map/ppermute | solution.py:734
  380.7 25.0 %collective-permute-start.38 = (bf16[2,4,24,1536]{3,2,1,0:T(8,128)(2,1)S(1)}, bf16[2,4,24,1536]{3,2,1,0:T(8,128)(2,1)S(1)}, u32[]{:S(2)}, u32[]{:S(2)}) collective-permute-start(bf16[2,4,24,1536]{3,2,1,0:T(8,128)(2,1)S(1)} %fusion.25), channel_id=1, source_target_pairs={{0,2},{2,0},{4,6},{6,4},{8,10},{10,8},{12,14},{14,12},{16,18},{18,... | collective-permute-start | bytes 1769480 | tf_op jit(solution)/shard_map/ppermute | solution.py:717
  382.2 23.4 %collective-permute-start.39 = (bf16[2,4,24,1536]{3,2,1,0:T(8,128)(2,1)S(1)}, bf16[2,4,24,1536]{3,2,1,0:T(8,128)(2,1)S(1)}, u32[]{:S(2)}, u32[]{:S(2)}) collective-permute-start(bf16[2,4,24,1536]{3,2,1,0:T(8,128)(2,1)S(1)} %fusion.16), channel_id=1, source_target_pairs={{0,4},{2,6},{4,0},{6,2},{8,12},{10,14},{12,8},{14,10},{16,20},{18,... | collective-permute-start | bytes 1769480 | tf_op jit(solution)/shard_map/ppermute | solution.py:717
  408.1 37.7 %collective-permute-start.44 = (bf16[2,4,48,1536]{3,2,1,0:T(8,128)(2,1)S(1)}, bf16[2,4,48,1536]{3,2,1,0:T(8,128)(2,1)}, u32[]{:S(2)}, u32[]{:S(2)}) collective-permute-start(bf16[2,4,48,1536]{3,2,1,0:T(8,128)(2,1)S(1)} %fusion.13), channel_id=1, source_target_pairs={{0,2},{2,0},{4,6},{6,4},{8,10},{10,8},{12,14},{14,12},{16,18},{18,... | collective-permute-start | bytes 3538952 | tf_op jit(solution)/shard_map/ppermute | solution.py:717
  411.7 34.0 %collective-permute-start.45 = (bf16[2,4,48,1536]{3,2,1,0:T(8,128)(2,1)}, bf16[2,4,48,1536]{3,2,1,0:T(8,128)(2,1)S(1)}, u32[]{:S(2)}, u32[]{:S(2)}) collective-permute-start(bf16[2,4,48,1536]{3,2,1,0:T(8,128)(2,1)} %fusion.1), channel_id=1, source_target_pairs={{0,4},{2,6},{4,0},{6,2},{8,12},{10,14},{12,8},{14,10},{16,20},{18,... | collective-permute-start | bytes 3538952 | tf_op jit(solution)/shard_map/ppermute | solution.py:717
  414.0 31.7 %collective-permute-start.42 = (bf16[4,24,1536]{2,1,0:T(8,128)(2,1)}, bf16[4,24,1536]{2,1,0:T(8,128)(2,1)}, u32[]{:S(2)}, u32[]{:S(2)}) collective-permute-start(bf16[4,24,1536]{2,1,0:T(8,128)(2,1)} %fusion.27), channel_id=1, source_target_pairs={{0,4},{2,6},{4,0},{6,2},{8,12},{10,14},{12,8},{14,10},{16,20},{18,... | collective-permute-start | bytes 884744 | tf_op jit(solution)/shard_map/ppermute | solution.py:717
  417.3 28.4 %collective-permute-start.43 = (bf16[4,24,1536]{2,1,0:T(8,128)(2,1)}, bf16[4,24,1536]{2,1,0:T(8,128)(2,1)}, u32[]{:S(2)}, u32[]{:S(2)}) collective-permute-start(bf16[4,24,1536]{2,1,0:T(8,128)(2,1)} %fusion.26), channel_id=1, source_target_pairs={{0,2},{2,0},{4,6},{6,4},{8,10},{10,8},{12,14},{14,12},{16,18},{18,... | collective-permute-start | bytes 884744 | tf_op jit(solution)/shard_map/ppermute | solution.py:717
  452.1 24.0 %collective-permute-start.54 = (bf16[768,1152]{1,0:T(8,128)(2,1)}, bf16[768,1152]{1,0:T(8,128)(2,1)}, u32[]{:S(2)}, u32[]{:S(2)}) collective-permute-start(bf16[768,1152]{1,0:T(8,128)(2,1)} %get-tuple-element.338), channel_id=1, source_target_pairs={{0,1},{1,0},{2,3},{3,2},{4,5},{5,4},{6,7},{7,6},{8,9},{9,8},{10,11... | collective-permute-start | bytes 5308424 | tf_op jit(solution)/shard_map/ppermute | solution.py:734
  454.4 21.7 %collective-permute-start.55 = (bf16[768,896]{1,0:T(8,128)(2,1)}, bf16[768,896]{1,0:T(8,128)(2,1)}, u32[]{:S(2)}, u32[]{:S(2)}) collective-permute-start(bf16[768,896]{1,0:T(8,128)(2,1)} %get-tuple-element.339), channel_id=1, source_target_pairs={{0,1},{1,0},{2,3},{3,2},{4,5},{5,4},{6,7},{7,6},{8,9},{9,8},{10,11... | collective-permute-start | bytes 4128776 | tf_op jit(solution)/shard_map/ppermute | solution.py:734
  545.2 37.4 %collective-permute-start.69 = (f32[48,768]{1,0:T(8,128)}, f32[48,768]{1,0:T(8,128)}, u32[]{:S(2)}, u32[]{:S(2)}) collective-permute-start(f32[48,768]{1,0:T(8,128)} %maximum_maximum_fusion.2), channel_id=1, source_target_pairs={{0,1},{1,0},{2,3},{3,2},{4,5},{5,4},{6,7},{7,6},{8,9},{9,8},{10,11... | collective-permute-start | bytes 442376 | tf_op jit(solution)/shard_map/ppermute | solution.py:734
  (166 other events, 1355.3 us)

commit v2 on v1

v2 whole, which is shorter than its diff:
```python
import functools
import itertools

import jax
import jax.numpy as jnp
from jax import lax
from jax.experimental import pallas as pl
from jax.experimental.pallas import tpu as pltpu
from jax.sharding import PartitionSpec as P

D = 768
HEADS = 12
PW = 384
PHEADS = 12
SIDE = 14
SMALLP = 196
CTX = 512
TGT = 256
STEP = 10


LOW = jnp.bfloat16
WIDE = jnp.float32
CLIP_NORM = 0.0005
LEARN_RATE = 0.05
GAIN_RATE = 1.0
BETA_ONE = 0.9
BETA_TWO = 0.999
EPSILON = 1e-08
WEIGHT_DECAY = 0.05


LANES = 128


def norm_rows(values, gain_row, shift_row):
    centred = values - jnp.mean(values, -1, keepdims=True)
    spread = jnp.mean(centred * centred, -1, keepdims=True)
    return centred * lax.rsqrt(spread + 1e-06) * gain_row + shift_row


def norm_back(values, gain_row, grad):
    centred = values - jnp.mean(values, -1, keepdims=True)
    rstd = lax.rsqrt(jnp.mean(centred * centred, -1, keepdims=True) + 1e-06)
    unit = centred * rstd
    scaled = grad * gain_row
    d_values = rstd * (
        scaled
        - jnp.mean(scaled, -1, keepdims=True)
        - unit * jnp.mean(scaled * unit, -1, keepdims=True)
    )
    return d_values, jnp.sum(grad * unit, 0), jnp.sum(grad, 0)


def gelu_parts(pre):
    bell = jnp.exp(-0.5 * pre * pre)
    turn = 1.0 / (1.0 + 0.3275911 * 0.7071067811865476 * jnp.abs(pre))
    series = 0.5 * 1.061405429
    for factor in (-1.453152027, 1.421413741, -0.284496736, 0.254829592):
        series = series * turn + 0.5 * factor
    tail = series * turn * bell
    return jnp.where(pre < 0.0, tail, 1.0 - tail), bell * 0.3989422804014327


def gelu_both(pre):
    phi, density = gelu_parts(pre)
    return (pre * phi).astype(LOW), (phi + pre * density).astype(LOW)


def place(single, positions):
    image_id = jnp.where(single, 0, positions // SMALLP)
    within = jnp.where(single, positions, positions % SMALLP)
    side_len = jnp.where(single, 2 * SIDE, SIDE)
    return (image_id, within // side_len, within % side_len)


def three_parts(values):
    high = lax.reduce_precision(values, 8, 7)
    rest = values - high
    middle = lax.reduce_precision(rest, 8, 7)
    return jnp.concatenate([high, middle, rest - middle], 0).astype(LOW)


def sincos(row_pos, col_pos, width, order):
    quarter = width // 4
    omega = 10000.0 ** (-jnp.arange(quarter).astype(WIDE) / quarter)
    steps = jnp.arange(2 * SIDE)
    angle = steps.astype(WIDE)[:, None] * omega
    table = jnp.concatenate([jnp.sin(angle), jnp.cos(angle)], -1)
    blank = jnp.zeros_like(table)
    table = jnp.concatenate(
        [jnp.concatenate([table, blank], 1), jnp.concatenate([blank, table], 1)], 0
    )
    parts = three_parts(table)
    if order is not None:
        parts = mm(parts, order).astype(LOW)
    pick = jnp.concatenate([row_pos[:, None] == steps, col_pos[:, None] == steps], 1)
    pick = pick.astype(LOW)
    return mm(jnp.concatenate([pick, pick, pick], 1), parts)


def mm(left, right):
    return jnp.dot(left, right, preferred_element_type=WIDE)


def mm_t(left, right):
    return lax.dot_general(left, right, (((1,), (1,)), ((), ())), preferred_element_type=WIDE)


def t_mm(left, right):
    return lax.dot_general(left, right, (((0,), (0,)), ((), ())), preferred_element_type=WIDE)


SPAN = 64


def head_forward(query, keys, values, bias_ref, size):
    scale = size**-0.5
    scores = mm_t(keys, query) + bias_ref[...]
    highest = jnp.max(scores, 0, keepdims=True)
    soft = jnp.exp((scores - highest) * scale)
    total = jnp.sum(soft, 0, keepdims=True)
    return (t_mm(values, soft.astype(LOW)) / total).T, highest * scale + jnp.log(total)


def head_backward(query, keys, values, d_out, mixed, logs, bias_ref, soft_ref, ds_ref, size):
    scale = size**-0.5
    count = keys.shape[0]
    row_sum = jnp.sum((d_out.astype(WIDE) * mixed.astype(WIDE)).T, 0, keepdims=True)
    for low in range(0, count, SPAN):
        high = low + SPAN
        scores = mm_t(keys[low:high], query) + bias_ref[low:high, :]
        soft = jnp.exp(scores * scale - logs)
        d_soft = mm_t(values[low:high], d_out)
        soft_ref[low:high, :] = soft.astype(LOW)
        ds_ref[low:high, :] = (soft * (d_soft - row_sum)).astype(LOW)
    d_values = mm(soft_ref[...], d_out)
    d_keys = mm(ds_ref[...], query) * scale
    d_query = (t_mm(keys, ds_ref[...]) * scale).T
    return d_query.astype(LOW), d_keys.astype(LOW), d_values.astype(LOW)


WHOLE = pl.BlockSpec(memory_space=pltpu.VMEM)
CHUNK = 64
MARGIN = 6 * 2**20


def room(values, margin=MARGIN):
    total = 0
    for value in values:
        rows, cols = value.shape[-2], value.shape[-1]
        cells = value.size // (rows * cols) * (-(-rows // 16) * 16) * (-(-cols // LANES) * LANES)
        total += cells * jnp.dtype(value.dtype).itemsize
    return min(total + margin, 58 * 2**20)


def streamed(kernel, counts, late, early, *refs):
    n_in, n_out, n_scratch = counts
    ins, outs = list(refs[:n_in]), list(refs[n_in : n_in + n_out])
    scratch = refs[n_in + n_out : n_in + n_out + n_scratch]
    extra = refs[n_in + n_out + n_scratch :]
    arriving, leaving, left = {}, {}, []
    for at, which in enumerate(late):
        arriving[which] = pltpu.make_async_copy(ins[which], extra[at], extra[-1].at[at])
        arriving[which].start()
        ins[which] = extra[at]
    for at, which in enumerate(early, len(late)):
        leaving[which] = pltpu.make_async_copy(extra[at], outs[which], extra[-1].at[at])
        outs[which] = extra[at]

    def need(*those):
        for which in those:
            arriving.pop(which).wait()

    def ship(*those):
        for which in those:
            copy = leaving.pop(which)
            copy.start()
            left.append(copy)

    kernel(need, ship, *ins, *outs, *scratch)
    need(*list(arriving))
    ship(*list(leaving))
    for copy in left:
        copy.wait()


def on_chip(kernel, ins, outs, scratch, macs, exps=0, ahead=False, late=(), early=()):
    outs = [jax.ShapeDtypeStruct(shape, kind) for shape, kind in outs]
    held = [jax.ShapeDtypeStruct(shape, kind) for shape, kind in scratch]
    moved = sum(value.size * value.dtype.itemsize for value in list(ins) + outs)
    buffers = [pltpu.VMEM(shape, kind) for shape, kind in scratch]
    in_specs, out_specs = [WHOLE] * len(ins), [WHOLE] * len(outs)
    if late or early:
        counts = len(ins), len(outs), len(scratch)
        kernel = functools.partial(streamed, kernel, counts, late, early)
        for which in late:
            in_specs[which] = pl.BlockSpec(memory_space=pl.ANY)
            buffers.append(pltpu.VMEM(ins[which].shape, ins[which].dtype))
        for which in early:
            out_specs[which] = pl.BlockSpec(memory_space=pl.ANY)
            buffers.append(pltpu.VMEM(outs[which].shape, outs[which].dtype))
        buffers.append(pltpu.SemaphoreType.DMA((len(late) + len(early),)))
    return pl.pallas_call(
        kernel,
        in_specs=in_specs,
        out_specs=out_specs,
        out_shape=outs,
        scratch_shapes=buffers,
        cost_estimate=pl.CostEstimate(flops=2 * macs, bytes_accessed=moved, transcendentals=exps),
        compiler_params=pltpu.CompilerParams(
            vmem_limit_bytes=room(list(ins) + outs + held) if ahead else 58 * 2**20
        ),
    )(*ins)


def tiles(count, width, body):
    def step(at, carry):
        body(pl.ds(pl.multiple_of(at * width, width), width))
        return carry

    lax.fori_loop(0, count // width, step, 0)


def norm_back_rows(values_ref, grad_ref, gain, write, sums_ref, at):
    rows, width = values_ref.shape

    def step(number, carry):
        span = pl.ds(pl.multiple_of(number * CHUNK, CHUNK), CHUNK)
        values, grad = values_ref[span, :], grad_ref[span, :]
        centred = values - jnp.mean(values, -1, keepdims=True)
        rstd = lax.rsqrt(jnp.mean(centred * centred, -1, keepdims=True) + 1e-06)
        unit = centred * rstd
        scaled = grad * gain
        d_values = rstd * (
            scaled
            - jnp.mean(scaled, -1, keepdims=True)
            - unit * jnp.mean(scaled * unit, -1, keepdims=True)
        )
        write(span, d_values)
        return (
            carry[0] + jnp.sum(grad * unit, 0, keepdims=True),
            carry[1] + jnp.sum(grad, 0, keepdims=True),
        )

    blank = jnp.zeros((1, width), WIDE)
    gains, shifts = lax.fori_loop(0, rows // CHUNK, step, (blank, blank))
    sums_ref[at : at + 1, :] = gains
    sums_ref[at + 1 : at + 2, :] = shifts


def ff_back_kernel(need, ship, *refs):
    (d_inward, bridge_in, hidden, middle, normed, order, gains) = refs[0:7]
    acts, slopes, ups, downs = refs[7:9], refs[9:11], refs[11:13], refs[13:15]
    grads, branch_out, d_middle, sums = refs[15:17], refs[17], refs[18], refs[19]
    grad, d_hidden, branch, branch_t, normed_t, d_pre = refs[20:26]
    ff = acts[0].shape[1]
    wide = 768

    def first(span):
        grad[:, span] = mm_t(d_inward[...], bridge_in[span, :])

    tiles(D, wide, first)

    def write_hidden(span, values):
        d_hidden[span, :] = values
        branch[span, :] = values.astype(LOW)

    norm_back_rows(hidden, grad, gains[4:5, :], write_hidden, sums, 0)
    need(5, 4)
    branch_t[...] = mm_t(order[...], branch[...]).astype(LOW)
    normed_t[...] = mm_t(order[...], normed[...]).astype(LOW)
    for side in (0, 1):
        need(7 + side, 9 + side, 13 + side)
        act, slope, down = acts[side], slopes[side], downs[side]
        out = grads[side]

        def second(span, act=act, slope=slope, down=down, out=out, side=side):
            d_act = mm(branch[...], down[:, span])
            values = (d_act * slope[:, span].astype(WIDE)).astype(LOW)
            d_pre[side, :, span] = values
            out[:, span] = mm(normed_t[...], values).astype(LOW)
            lower = pl.ds(pl.multiple_of(span.start + ff, LANES), span.size)
            out[:, lower] = mm(branch_t[...], act[:, span]).astype(LOW)

        tiles(ff, wide, second)
        ship(side)

    need(11, 12)

    def third(span):
        grad[:, span] = mm_t(d_pre[0], ups[0][span, :]) + mm_t(d_pre[1], ups[1][span, :])

    tiles(D, wide, third)

    def write_middle(span, values):
        values = values + d_hidden[span, :]
        d_middle[span, :] = values
        branch_out[span, :] = values.astype(LOW)

    need(3)
    norm_back_rows(middle, grad, gains[2:3, :], write_middle, sums, 2)


def ff_back(d_inward, bridge_in, hidden, middle, normed, order, gains, acts, slopes, ups, downs):
    rows, ff = acts[0].shape
    return on_chip(
        ff_back_kernel,
        [d_inward, bridge_in, hidden, middle, normed, order, gains]
        + [*acts, *slopes, *ups, *downs],
        [((D, 2 * ff), LOW)] * 2 + [((rows, D), LOW), ((rows, D), WIDE), ((8, D), WIDE)],
        [((rows, D), WIDE)] * 2
        + [((rows, D), LOW), ((D, rows), LOW), ((D, rows), LOW), ((2, rows, ff), LOW)],
        8 * rows * D * ff,
        late=(5, 4, 13, 9, 7, 14, 10, 8, 11, 12, 3),
        early=(0, 1),
    )


def attn_back_kernel(size, branch, ids_row, ids_col, *refs):
    rests, projs, mixeds, logs, d_projs = refs[0:2], refs[2:4], refs[4:6], refs[6:8], refs[8:10]
    d_mixed, bias, soft, d_scores = refs[10:14]
    width = D // 2
    bias[...] = jnp.where(ids_col[...] == ids_row[...], 0.0, -1e30)
    for side in (0, 1):
        proj, mixed, log, d_proj = projs[side], mixeds[side], logs[side], d_projs[side]
        d_mixed[...] = mm(branch[...], rests[side][:, width : 2 * width]).astype(LOW)

        def step(block, carry, proj=proj, mixed=mixed, log=log, d_proj=d_proj):
            at = [pl.multiple_of(part * width + block * LANES, LANES) for part in range(3)]
            query, keys, values = [proj[:, pl.ds(col, LANES)] for col in at]
            d_out = d_mixed[:, pl.ds(at[0], LANES)]
            out = mixed[:, pl.ds(at[0], LANES)]
            found = []
            for number, low in enumerate(range(0, LANES, size)):
                cols = slice(low, low + size)
                found.append(
                    head_backward(
                        query[:, cols],
                        keys[:, cols],
                        values[:, cols],
                        d_out[:, cols],
                        out[:, cols],
                        log[number, pl.ds(block, 1), :],
                        bias,
                        soft,
                        d_scores,
                        size,
                    )
                )
            for col, parts in zip(at, zip(*found)):
                d_proj[:, pl.ds(col, LANES)] = jnp.concatenate(parts, -1)
            return carry

        lax.fori_loop(0, width // LANES, step, 0)


def attn_back(size, branch, ids, rests, projs, mixeds, logs):
    rows = branch.shape[0]
    return on_chip(
        functools.partial(attn_back_kernel, size),
        [branch, ids[None, :], ids[:, None], *rests, *projs, *mixeds, *logs],
        [(projs[0].shape, LOW)] * 2,
        [
            ((rows, D // 2), LOW),
            ((rows, rows), WIDE),
            ((rows, rows), LOW),
            ((rows, rows), LOW),
        ],
        rows * D * D + rows * rows * D * 5,
        rows * rows * D // size,
        ahead=True,
    )


def qkv_back_kernel(need, ship, *refs):
    branch, d_middle, start, normed, seen, eye, gains, sums_ff, sums_p, spread = refs[0:10]
    d_projs, mixeds, qkvs, orders = refs[10:12], refs[12:14], refs[14:16], refs[16:18]
    outs = refs[18:20]
    grad, flipped, d_start, sums = refs[20:24]
    width = D // 2
    rest = 3 * width
    flipped[...] = mm_t(eye[...], branch[...]).astype(LOW)
    need(12, 13)
    for side in (0, 1):
        outs[side][:, rest + width : rest + 2 * width] = mm(
            flipped[...], mixeds[side][...]
        ).astype(LOW)
    need(3)
    flipped[...] = mm_t(eye[...], normed[...]).astype(LOW)
    need(10, 11)
    for side in (0, 1):
        outs[side][:, 0:rest] = mm(flipped[...], d_projs[side][...]).astype(LOW)
    need(14, 15)
    grad[...] = mm_t(d_projs[0][...], qkvs[0][...]) + mm_t(d_projs[1][...], qkvs[1][...])

    def write(span, values):
        d_start[span, :] = (values + d_middle[span, :]).astype(LOW)

    need(1, 2)
    norm_back_rows(start, grad, gains[0:1, :], write, sums, 0)
    need(4)
    flipped[...] = mm_t(eye[...], seen[...]).astype(LOW)
    sums[2:4, :] = sums_ff[2:4, :]
    sums[4:6, :] = sums_ff[0:2, :]
    sums[6:8, :] = jnp.zeros((2, D), WIDE)
    rows = jnp.concatenate(
        [sums[...].astype(LOW), mm(sums_p[...].astype(LOW), spread[...]).astype(LOW)], 0
    )
    cols = t_mm(rows, eye[0:16, 0:LANES]).astype(LOW)
    need(16, 17)
    for side in (0, 1):
        moved = mm_t(d_start[...], orders[side][...]).astype(LOW)
        outs[side][:, rest : rest + width] = mm(flipped[...], moved).astype(LOW)
        outs[side][:, rest + 2 * width :] = cols


def qkv_back(branch, d_middle, start, normed, seen, eye, gains, sums_ff, sums_p, spread, pairs):
    rows, width = branch.shape[0], D // 2
    return on_chip(
        qkv_back_kernel,
        [branch, d_middle, start, normed, seen, eye, gains, sums_ff, sums_p, spread]
        + [value for pair in pairs for value in pair],
        [((D, 5 * width + LANES), LOW)] * 2,
        [((rows, D), WIDE), ((D, rows), LOW), ((rows, D), LOW), ((8, D), WIDE)],
        rows * D * D * 10,
        late=(12, 13, 3, 10, 11, 14, 15, 1, 2, 4, 16, 17),
    )


def row_spans(rows, chunk, body):
    def step(number, carry):
        body(pl.ds(pl.multiple_of(number * chunk, chunk), chunk))
        return carry

    lax.fori_loop(0, rows // chunk, step, 0)


def heads_forward(query_ref, keys_ref, values_ref, out_ref, logs_ref, bias, size, at):
    width = out_ref.shape[1]

    def step(block, carry):
        cols = [pl.multiple_of(first + block * LANES, LANES) for first in at]
        query = query_ref[:, pl.ds(cols[0], LANES)]
        keys = keys_ref[:, pl.ds(cols[1], LANES)]
        values = values_ref[:, pl.ds(cols[2], LANES)]
        found = []
        for number, low in enumerate(range(0, LANES, size)):
            part = slice(low, low + size)
            out, logs = head_forward(
                query[:, part], keys[:, part], values[:, part], bias, size
            )
            found.append(out)
            if logs_ref is not None:
                logs_ref[number, pl.ds(block, 1), :] = logs
        place_at = pl.ds(pl.multiple_of(block * LANES, LANES), LANES)
        out_ref[:, place_at] = jnp.concatenate(found, -1).astype(LOW)
        return carry

    lax.fori_loop(0, width // LANES, step, 0)


def ctx_first_kernel(need, ship, seen, pos, spread, *refs):
    orders, rests, qkvs = refs[0:2], refs[2:4], refs[4:6]
    start, normed, projs, outs, embed_w = refs[6], refs[7], refs[8:10], refs[10:13], refs[13]
    gains = outs[0]
    width = orders[0].shape[0]
    parts = rests[0][:, 2 * width :].astype(WIDE).T
    outs[0][...] = parts[0:8] + parts[8:16]
    outs[1][...] = parts[16:24] + parts[24:32]
    low = parts[32:48].astype(LOW)
    low = mm_t(low, spread[...])
    outs[2][...] = low[0:8] + low[8:16]
    embed_w[...] = (
        mm(rests[0][:, 0:width], orders[0][...]) + mm(rests[1][:, 0:width], orders[1][...])
    ).astype(LOW)
    need(0, 1)
    start[...] = mm(seen[...], embed_w[...]) + pos[...]
    ship(0)

    def first_norm(span):
        normed[span, :] = norm_rows(start[span, :], gains[0:1, :], gains[1:2, :]).astype(LOW)

    row_spans(seen.shape[0], CHUNK, first_norm)
    ship(1)
    for side in (0, 1):
        need(7 + side)
        projs[side][...] = mm(normed[...], qkvs[side][...]).astype(LOW)
        ship(2 + side)


def ctx_first(seen, pos, spread, orders, rests, qkvs):
    rows, width = seen.shape[0], orders[0].shape[0]
    return on_chip(
        ctx_first_kernel,
        [seen, pos, spread, *orders, *rests, *qkvs],
        [((rows, D), WIDE), ((rows, D), LOW)]
        + [((rows, 3 * width), LOW)] * 2
        + [((8, D), WIDE), ((8, D), WIDE), ((8, PW), WIDE)],
        [((D, D), LOW)],
        rows * D * D * 4 + D * D * D,
        late=(0, 1, 7, 8),
        early=(0, 1, 2, 3),
    )


def ctx_second_kernel(size, need, ship, start, gains, ids_row, ids_col, *refs):
    rests, projs = refs[0:2], refs[2:4]
    middle, normed_two, mixeds, logs, bias = refs[4], refs[5], refs[6:8], refs[8:10], refs[10]
    width = mixeds[0].shape[1]
    bias[...] = jnp.where(ids_col[...] == ids_row[...], 0.0, -1e30)
    for side in (0, 1):
        need(6 + side)
        proj = projs[side]
        heads_forward(
            proj, proj, proj, mixeds[side], logs[side], bias, size, (0, width, 2 * width)
        )
        ship(2 + side)
    need(4, 5, 0)
    middle[...] = (
        start[...]
        + mm_t(mixeds[0][...], rests[0][:, width : 2 * width])
        + mm_t(mixeds[1][...], rests[1][:, width : 2 * width])
    )

    def second_norm(span):
        normed_two[span, :] = norm_rows(middle[span, :], gains[2:3, :], gains[3:4, :]).astype(LOW)

    row_spans(start.shape[0], CHUNK, second_norm)


def ctx_second(size, start, gains, ids, rests, projs):
    rows, width = start.shape[0], D // 2
    return on_chip(
        functools.partial(ctx_second_kernel, size),
        [start, gains, ids[None, :], ids[:, None], *rests, *projs],
        [((rows, D), WIDE), ((rows, D), LOW)]
        + [((rows, width), LOW)] * 2
        + [((LANES // size, 8, rows), WIDE)] * 2,
        [((rows, rows), WIDE)],
        rows * D * D + rows * rows * D * 2,
        rows * rows * D // size,
        late=(6, 7, 4, 5, 0),
        early=(2, 3),
    )


def gelu_rows(pre_ref, act_ref, slope_ref, span):
    def body(rows):
        act, slope = gelu_both(pre_ref[rows, :])
        act_ref[rows, span] = act
        if slope_ref is not None:
            slope_ref[rows, span] = slope

    row_spans(pre_ref.shape[0], 32, body)


def ff_kernel(need, ship, *refs):
    normed, middle, gains, ups, downs = *refs[0:3], refs[3:5], refs[5:7]
    hidden, context, acts, slopes, pre = refs[7], refs[8], refs[9:11], refs[11:13], refs[13]
    rows, ff = acts[0].shape
    for side in (0, 1):
        need(3 + side)

        def first(span, side=side):
            pre[...] = mm(normed[...], ups[side][:, span])
            gelu_rows(pre, acts[side], slopes[side], span)

        tiles(ff, 512, first)
        ship(2 + side, 4 + side)
    need(5, 6, 1)
    hidden[...] = (
        middle[...] + mm_t(acts[0][...], downs[0][...]) + mm_t(acts[1][...], downs[1][...])
    )

    def last(span):
        context[span, :] = norm_rows(hidden[span, :], gains[4:5, :], gains[5:6, :]).astype(LOW)

    row_spans(rows, CHUNK, last)


def ff_forward(normed, middle, gains, ups, downs):
    rows, ff = normed.shape[0], ups[0].shape[1]
    return on_chip(
        ff_kernel,
        [normed, middle, gains, *ups, *downs],
        [((rows, D), WIDE), ((rows, D), LOW)] + [((rows, ff), LOW)] * 4,
        [((rows, 512), WIDE)],
        rows * D * ff * 4 + rows * D * D,
        rows * ff * 2,
        late=(3, 4, 5, 6, 1),
        early=(2, 3, 4, 5),
    )


def target_kernel(size, *refs):
    patch, seen, pos_all, pos_tgt, gains, ids_row, ids_col = refs[0:7]
    orders, weights, (t_middle, t_two) = refs[7:9], refs[9:11], refs[11:13]
    embed_w, hidden, normed, start, query, keys, mixed, bias = refs[13:]
    width = D // 2
    own, other = [part[:, 3 * width : 4 * width] for part in weights]
    embed_w[...] = (mm(own, orders[0][...]) + mm(other, orders[1][...])).astype(LOW)
    hidden[...] = mm(patch[...], embed_w[...]) + pos_all[...]

    def first_norm(span):
        normed[span, :] = norm_rows(hidden[span, :], gains[0:1, :], gains[1:2, :]).astype(LOW)

    row_spans(patch.shape[0], 112, first_norm)
    start[...] = mm(seen[...], embed_w[...]) + pos_tgt[...]
    t_normed = norm_rows(start[...], gains[0:1, :], gains[1:2, :]).astype(LOW)
    bias[...] = jnp.where(ids_col[...] == ids_row[...], 0.0, -1e30)
    total = start[...]
    for part in weights:
        query[...] = mm(t_normed, part[:, 0:width]).astype(LOW)
        keys[...] = mm(normed[...], part[:, width : 3 * width]).astype(LOW)
        heads_forward(query, keys, keys, mixed, None, bias, size, (0, 0, width))
        total = total + mm_t(mixed[...], part[:, 4 * width : 5 * width])
    t_middle[...] = total
    t_two[...] = norm_rows(total, gains[2:3, :], gains[3:4, :]).astype(LOW)


def target_forward(
    size, patch, seen, pos_all, pos_tgt, gains, idq, idk, orders, weights
):
    rows, count, width = seen.shape[0], patch.shape[0], D // 2
    return on_chip(
        functools.partial(target_kernel, size),
        [patch, seen, pos_all, pos_tgt, gains, idq[None, :], idk[:, None], *orders, *weights],
        [((rows, D), WIDE), ((rows, D), LOW)],
        [
            ((D, D), LOW),
            ((count, D), WIDE),
            ((count, D), LOW),
            ((rows, D), WIDE),
            ((rows, width), LOW),
            ((count, 2 * width), LOW),
            ((rows, width), LOW),
            ((count, rows), WIDE),
        ],
        count * D * D * 3 + rows * D * D * 3 + 2 * rows * count * D,
        rows * count * D // size,
        ahead=True,
    )


def pred_forward_kernel(size, *refs):
    context, bridge_in, bridge_out, pos, gains, ids_row, ids_col = refs[0:7]
    downs, ups, qks, rights = refs[7:9], refs[9:11], refs[11:13], refs[13:15]
    joined, normed, middle, normed_two, predicted, final, guess = refs[15:22]
    out_qk, out_v, mixeds, acts, slopes = (
        refs[22:24],
        refs[24:26],
        refs[26:28],
        refs[28:30],
        refs[30:32],
    )
    logs, bias = refs[32], refs[33]
    width = out_v[0].shape[1]
    joined[0:CTX, :] = mm(context[...], bridge_in[...]) + pos[0:CTX, :]
    joined[CTX:, :] = gains[6:7, :] + pos[CTX:, :]

    def first(span):
        normed[span, :] = norm_rows(joined[span, :], gains[0:1, :], gains[1:2, :]).astype(LOW)

    row_spans(joined.shape[0], 128, first)
    bias[...] = jnp.where(ids_col[...] == ids_row[...], 0.0, -1e30)
    total = joined[CTX:, :]
    head = 0
    for qk, right, qk_ref, v_ref, mixed in zip(qks, rights, out_qk, out_v, mixeds):
        qk_ref[...] = mm(normed[...], qk[...]).astype(LOW)
        v_ref[...] = mm(normed[...], right[:, 0:width]).astype(LOW)
        found = []
        for low in range(0, width, size):
            out, log = head_forward(
                qk_ref[CTX:, low : low + size],
                qk_ref[:, width + low : width + low + size],
                v_ref[:, low : low + size],
                bias,
                size,
            )
            found.append(out)
            logs[head : head + 1, :] = log
            head += 1
        mixed[...] = jnp.concatenate(found, -1).astype(LOW)
        total = total + mm_t(mixed[...], right[:, width:])
    middle[...] = total
    normed_two[...] = norm_rows(total, gains[2:3, :], gains[3:4, :]).astype(LOW)
    total = middle[...]
    for up, down, act, slope in zip(ups, downs, acts, slopes):
        values, tilt = gelu_both(mm(normed_two[...], up[...]))
        act[...] = values
        slope[...] = tilt
        total = total + mm_t(act[...], down[...])
    predicted[...] = total
    final[...] = norm_rows(total, gains[4:5, :], gains[5:6, :]).astype(LOW)
    guess[...] = mm_t(final[...], bridge_out[...])


def pred_forward(
    size, context, bridge_in, bridge_out, pos, gains, idq, idk, downs, ups, qks, rights
):
    rows, count, width, ff = idq.shape[0], idk.shape[0], qks[0].shape[1] // 2, ups[0].shape[1]
    low, wide = LOW, WIDE
    return on_chip(
        functools.partial(pred_forward_kernel, size),
        [context, bridge_in, bridge_out, pos, gains, idq[None, :], idk[:, None]]
        + [*downs, *ups, *qks, *rights],
        [((count, PW), wide), ((count, PW), low), ((rows, PW), wide), ((rows, PW), low)]
        + [((rows, PW), wide), ((rows, PW), low), ((rows, D), wide)]
        + [((count, 2 * width), low)] * 2
        + [((count, width), low)] * 2
        + [((rows, width), low)] * 2
        + [((rows, ff), low)] * 4
        + [((16, rows), wide)],
        [((count, rows), wide)],
        1_000_000_000,
        rows * count * PW // size,
    )


def target_ff_kernel(need, ship, t_two, t_middle, gains, *refs):
    ups, downs, (target, pre, act, total) = refs[0:2], refs[2:4], refs[4:8]
    total[...] = t_middle[...]
    for side in (0, 1):
        up, down = ups[side], downs[side]
        need(3 + side)

        def first(span, up=up):
            pre[...] = mm(t_two[...], up[:, span])
            gelu_rows(pre, act, None, span)

        tiles(act.shape[1], 512, first)
        need(5 + side)
        total[...] = total[...] + mm_t(act[...], down[...])
    chosen = norm_rows(total[...], gains[4:5, :], gains[5:6, :])
    target[...] = norm_rows(chosen, 1.0, 0.0)


def target_ff(t_two, t_middle, gains, ups, downs):
    rows, ff = t_two.shape[0], ups[0].shape[1]
    return on_chip(
        target_ff_kernel,
        [t_two, t_middle, gains, *ups, *downs],
        [((rows, D), WIDE)],
        [((rows, 512), WIDE), ((rows, ff), LOW), ((rows, D), WIDE)],
        rows * D * ff * 4,
        rows * ff * 2,
        late=(3, 5, 4, 6),
    )[0]


def pred_back_all_kernel(size, count_all, *refs):
    (guess, target, used, context, final, bridge_in, bridge_out, gains, ids_row, ids_col) = refs[
        0:10
    ]
    predicted, middle, joined, normed, normed_two = refs[10:15]
    downs, ups, qks, rights = refs[15:17], refs[17:19], refs[19:21], refs[21:23]
    acts, slopes, in_qk, in_v, mixeds = (
        refs[23:25],
        refs[25:27],
        refs[27:29],
        refs[29:31],
        refs[31:33],
    )
    logs = refs[33]
    loss, d_inward, g_bridge_in, g_bridge_out, sums = refs[34:39]
    g_left, g_right = refs[39:41], refs[41:43]
    d_qk, d_v, d_normed, bias, soft, d_scores = refs[43:49]
    width = in_v[0].shape[1]
    ff = acts[0].shape[1]
    diff = guess[...] - target[...]
    size_abs = jnp.abs(diff)
    keep = lax.broadcasted_iota(jnp.int32, diff.shape, 0) < used[0]
    terms = jnp.where(
        keep, jnp.where(size_abs < 1.0, 0.5 * diff * diff, size_abs - 0.5), 0.0
    )
    loss[...] = jnp.sum(jnp.sum(terms, 0, keepdims=True), 1, keepdims=True)
    d_guess = jnp.where(keep, jnp.clip(diff, -1.0, 1.0) / count_all, 0.0).astype(LOW)
    g_bridge_out[...] = t_mm(d_guess, final[...]).astype(LOW)

    def back(values, gain, grad, at):
        d_values, gain_sum, shift_sum = norm_back(values, gain, grad)
        sums[at : at + 1, :] = gain_sum[None, :]
        sums[at + 1 : at + 2, :] = shift_sum[None, :]
        return d_values

    d_tail = back(predicted[...], gains[4:5, :], mm(d_guess, bridge_out[...]), 4)
    branch = d_tail.astype(LOW)
    total = None
    for side in (0, 1):
        d_pre = (mm(branch, downs[side][...]) * slopes[side][...].astype(WIDE)).astype(LOW)
        g_left[side][:, 0:ff] = t_mm(branch, acts[side][...]).astype(LOW)
        g_right[side][:, 0:ff] = t_mm(normed_two[...], d_pre).astype(LOW)
        part = mm_t(d_pre, ups[side][...])
        total = part if total is None else total + part
    d_middle = d_tail + back(middle[...], gains[2:3, :], total, 2)
    branch = d_middle.astype(LOW)
    bias[...] = jnp.where(ids_col[...] == ids_row[...], 0.0, -1e30)
    total = None
    head = 0
    for side in (0, 1):
        qk_ref, v_ref, right = in_qk[side], in_v[side], rights[side]
        d_mixed = mm(branch, right[:, width:]).astype(LOW)
        g_right[side][:, ff + width :] = t_mm(branch, mixeds[side][...]).astype(LOW)
        found = []
        for low in range(0, width, size):
            found.append(
                head_backward(
                    qk_ref[CTX:, low : low + size],
                    qk_ref[:, width + low : width + low + size],
                    v_ref[:, low : low + size],
                    d_mixed[:, low : low + size],
                    mixeds[side][:, low : low + size],
                    logs[head : head + 1, :],
                    bias,
                    soft,
                    d_scores,
                    size,
                )
            )
            head += 1
        d_query, d_keys, d_values = [jnp.concatenate(parts, -1) for parts in zip(*found)]
        d_qk[0:CTX, 0:width] = jnp.zeros((CTX, width), LOW)
        d_qk[CTX:, 0:width] = d_query
        d_qk[:, width:] = d_keys
        d_v[...] = d_values
        g_left[side][:, ff:] = t_mm(normed[...], d_qk[...]).astype(LOW)
        g_right[side][:, ff : ff + width] = t_mm(normed[...], d_v[...]).astype(LOW)
        part = mm_t(d_qk[...], qks[side][...]) + mm_t(d_v[...], right[:, 0:width])
        d_normed[...] = part if side == 0 else d_normed[...] + part
    d_joined = back(joined[...], gains[0:1, :], d_normed[...], 0)
    sums[6:7, :] = jnp.sum(d_joined[CTX:] + d_middle, 0, keepdims=True)
    sums[7:8, :] = jnp.zeros((1, PW), WIDE)
    d_inward[...] = d_joined[0:CTX].astype(LOW)
    g_bridge_in[...] = t_mm(context[...], d_inward[...]).astype(LOW)


def pred_back_all(size, count_all, used, values, pairs, logs, idq, idk):
    (guess, target, context, final, bridge_in, bridge_out, gains) = values[:7]
    ff, width, count = pairs[0][0].shape[1], pairs[2][0].shape[1] // 2, idk.shape[0]
    ins = [guess, target, used, context, final, bridge_in, bridge_out, gains]
    ins += [idq[None, :], idk[:, None], *values[7:]] + [part for pair in pairs for part in pair]
    ins.append(logs)
    outs = [((1, 1), WIDE), ((CTX, PW), LOW), ((D, PW), LOW), ((D, PW), LOW), ((8, PW), WIDE)]
    outs += [((PW, ff + 2 * width), LOW)] * 4
    specs = [WHOLE] * len(ins)
    specs[2] = pl.BlockSpec(memory_space=pltpu.SMEM)
    return pl.pallas_call(
        functools.partial(pred_back_all_kernel, size, count_all),
        in_specs=specs,
        out_specs=[WHOLE] * len(outs),
        out_shape=[jax.ShapeDtypeStruct(shape, kind) for shape, kind in outs],
        scratch_shapes=[
            pltpu.VMEM((count, 2 * width), LOW),
            pltpu.VMEM((count, width), LOW),
            pltpu.VMEM((count, PW), WIDE),
            pltpu.VMEM((count, idq.shape[0]), WIDE),
            pltpu.VMEM((count, idq.shape[0]), LOW),
            pltpu.VMEM((count, idq.shape[0]), LOW),
        ],
        cost_estimate=pl.CostEstimate(
            flops=4_000_000_000, bytes_accessed=20_000_000, transcendentals=3_000_000
        ),
        compiler_params=pltpu.CompilerParams(vmem_limit_bytes=58 * 2**20),
    )(*ins)


def pred_parts_kernel(dp_count, side_ref, own, other, order, *outs):
    width, half = PW // 2, D // 2
    ff = D
    flip = side_ref[0] != 0
    low = jnp.where(flip, other[:, 0:half], own[:, 0:half])
    high = jnp.where(flip, own[:, 0:half], other[:, 0:half])
    outs[0][...] = mm(low, order[...]).astype(LOW)
    outs[1][...] = mm(high, order[...]).astype(LOW)
    rows = PW // dp_count
    for at, ref in enumerate((own, other)):
        for start, wide, out in ((half, ff, 2), (half + ff, 2 * width, 6)):
            blocks = ref[:, start : start + wide].astype(WIDE).reshape(dp_count, 2 * rows, wide)
            outs[out + at][...] = blocks[:, :rows].reshape(PW, wide).astype(LOW)
            outs[out + 2 + at][...] = blocks[:, rows:].reshape(PW, wide).astype(LOW)


def pred_parts(dp_count, side, own, other, order):
    width, half = PW // 2, D // 2
    if PW // dp_count % 8:
        bridges = [part[:, :half] for part in (own, other)]
        first = side == 0
        found = [
            mm(jnp.where(first, bridges[at], bridges[1 - at]), order).astype(LOW) for at in (0, 1)
        ]
        for start, wide in ((half, D), (half + D, 2 * width)):
            cols = [part[:, start : start + wide] for part in (own, other)]
            cols = [part.reshape(dp_count, 2, PW // dp_count, wide) for part in cols]
            found += [flat(part[:, which]) for which in (0, 1) for part in cols]
    else:
        ins = [side[None], own, other, order]
        shapes = [(D, PW)] * 2 + [(PW, D)] * 4 + [(PW, 2 * width)] * 4
        outs = [jax.ShapeDtypeStruct(shape, LOW) for shape in shapes]
        found = pl.pallas_call(
            functools.partial(pred_parts_kernel, dp_count),
            in_specs=[pl.BlockSpec(memory_space=pltpu.SMEM)] + [WHOLE] * 3,
            out_specs=[WHOLE] * len(outs),
            out_shape=outs,
            cost_estimate=pl.CostEstimate(
                flops=1_000_000_000, bytes_accessed=9_000_000, transcendentals=0
            ),
            compiler_params=pltpu.CompilerParams(vmem_limit_bytes=58 * 2**20),
        )(*ins)
    return found[0], found[1], [found[at : at + 2] for at in range(2, 10, 2)]


class Lines:
    def __init__(self, count):
        self.count = count
        self.stride = count // 4
        bits = list(range(self.stride.bit_length() - 1))
        turn = len(bits) // 2
        self.bits = bits
        self.orders = (bits, bits[turn:] + bits[:turn])
        self.turn = turn

    def flip(self, values, bit):
        pairs = [(at, at ^ (1 << bit)) for at in range(self.count)]
        return lax.ppermute(values, "dp", pairs)

    def shift(self, values, steps):
        pairs = [(at, (at + steps * self.stride) % self.count) for at in range(self.count)]
        return lax.ppermute(values, "dp", pairs)

    def add_all(self, values, low, high):
        total = values
        for change in range(1, 1 << (high - low)):
            pairs = [(at, at ^ (change << low)) for at in range(2 * self.count)]
            total = total + lax.ppermute(values, ("dp", "mp"), pairs)
        return total

    def order(self, index, width):
        rows = width // self.count
        column = jnp.arange(width)
        block = column // rows
        far = (block // self.stride - index // self.stride) % 4
        near = (block ^ index) % self.stride
        target = (near * 4 + far) * rows + column % rows
        return (target[:, None] == column).astype(LOW)


def swap(values):
    return lax.ppermute(values, "mp", [(0, 1), (1, 0)])


def swap_all(values):
    return [swap(value) for value in values]


def far_kernel(*refs):
    outs = refs[4:]
    cut = outs[0].shape[-1]
    for at, block in enumerate(refs[:4]):
        outs[0][at] = block[:, :cut]
        outs[1][at] = block[:, cut:]


def gather_far(lines, shards):
    wide = jnp.concatenate(shards, 1)
    found = [wide] + [lines.shift(wide, -steps) for steps in (1, 2, 3)]
    rows, cut = shards[0].shape
    cols = [slice(0, cut), slice(cut, wide.shape[1])]
    if rows % 16:
        return [jnp.stack([block[:, part] for block in found]) for part in cols]
    return on_chip(
        far_kernel,
        found,
        [((4, rows, part.stop - part.start), LOW) for part in cols],
        [],
        0,
    )


def stack_kernel(axes, *refs):
    count = len(axes)
    ins, outs, bufs, sems = refs[: 2 * count], refs[2 * count : 3 * count], refs[3 * count : -1], refs[-1]
    arriving = [
        pltpu.make_async_copy(ins[at], bufs[at], sems.at[at]) for at in range(2 * count)
    ]
    for copy in arriving:
        copy.start()
    leaving = []
    for at, copy in enumerate(arriving):
        copy.wait()
        where = (slice(None),) * axes[at % count] + (at // count,)
        out = pltpu.make_async_copy(
            bufs[at], outs[at % count].at[where], sems.at[2 * count + at]
        )
        out.start()
        leaving.append(out)
    for copy in leaving:
        copy.wait()


def stack_pairs(held, got, axes):
    anywhere = pl.BlockSpec(memory_space=pl.ANY)
    ins = [*held, *got]
    outs = [
        jax.ShapeDtypeStruct(values.shape[:axis] + (2,) + values.shape[axis:], LOW)
        for values, axis in zip(held, axes)
    ]
    return pl.pallas_call(
        functools.partial(stack_kernel, axes),
        in_specs=[anywhere] * len(ins),
        out_specs=[anywhere] * len(outs),
        out_shape=outs,
        scratch_shapes=[pltpu.VMEM(value.shape, LOW) for value in ins]
        + [pltpu.SemaphoreType.DMA((2 * len(ins),))],
        cost_estimate=pl.CostEstimate(
            flops=0, bytes_accessed=8 * sum(value.size for value in ins), transcendentals=0
        ),
        compiler_params=pltpu.CompilerParams(vmem_limit_bytes=58 * 2**20),
    )(*ins)


def gather_near(lines, held, phase):
    done = [list(order[: lines.turn]) if phase else [] for order in lines.orders]
    steps = [order[lines.turn :] if phase else order[: lines.turn] for order in lines.orders]
    for bits in zip(*steps):
        got = [lines.flip(values, bit) for values, bit in zip(held, bits)]
        axes = [sum(1 for other in had if other > bit) for had, bit in zip(done, bits)]
        if phase and held[0].shape[-2] % 16 == 0:
            held = stack_pairs(held, got, axes)
        else:
            held = [
                jnp.stack([values, other], axis) for values, other, axis in zip(held, got, axes)
            ]
        for had, bit in zip(done, bits):
            had.append(bit)
    return list(held)


def flat(values):
    return values.reshape(-1, values.shape[-1])


class Box:
    def __init__(self, value):
        self.value, self.held = value, False


def sum_kernel(plan, squares, *refs):
    operands = 1 + max(term[0] for pieces in plan for piece in pieces for term in piece)
    if squares:
        refs[-1][...] = jnp.zeros((1, LANES), WIDE)
    for pieces, out in zip(plan, refs[operands:]):
        for lead in itertools.product(*[range(size) for size in out.shape[:-2]]):
            at = 0
            for piece in pieces:
                total = None
                for operand, low, high in piece:
                    part = refs[operand][lead + (slice(None), slice(low, high))].astype(WIDE)
                    total = part if total is None else total + part
                wide = high - low
                out[lead + (slice(None), slice(at, at + wide))] = total.astype(out.dtype)
                if squares:
                    for col in range(0, wide, LANES):
                        part = total[:, col : col + LANES]
                        weight = 0.5 if at + col == squares[1] and wide == squares[0] else 1.0
                        refs[-1][...] += weight * jnp.sum(part * part, 0, keepdims=True)
                at += wide


def sum_parts(outs, kind, squares=None):
    operands, specs, plan, shapes = [], [], [], []
    known = {}
    for pieces in outs:
        row = []
        for piece in pieces:
            terms = []
            for box, taken, (low, high) in piece:
                if (id(box), taken) not in known:
                    known[id(box), taken] = len(operands)
                    value = box.value
                    block = [
                        size if pick is None else None for size, pick in zip(value.shape, taken)
                    ]
                    where = tuple(0 if pick is None else pick for pick in taken) + (0, 0)
                    operands.append(value)
                    specs.append(
                        pl.BlockSpec(
                            tuple(block) + value.shape[-2:], lambda step, where=where: where
                        )
                    )
                terms.append((known[id(box), taken], low, high))
            row.append(tuple(terms))
        plan.append(tuple(row))
        box, taken, cols = pieces[0][0]
        lead = tuple(size for size, pick in zip(box.value.shape, taken) if pick is None)
        wide = sum(piece[0][2][1] - piece[0][2][0] for piece in pieces)
        shapes.append(
            jax.ShapeDtypeStruct(lead + (box.value.shape[-2], wide), kind)
        )
    moved = 8 * sum(shape.size for shape in shapes)
    if squares:
        shapes.append(jax.ShapeDtypeStruct((1, LANES), WIDE))
    return pl.pallas_call(
        functools.partial(sum_kernel, tuple(plan), squares),
        grid=(1,),
        in_specs=specs,
        out_specs=[
            pl.BlockSpec(shape.shape, lambda step, rank=len(shape.shape): (0,) * rank)
            for shape in shapes
        ],
        out_shape=shapes,
        cost_estimate=pl.CostEstimate(flops=moved, bytes_accessed=moved, transcendentals=0),
        compiler_params=pltpu.CompilerParams(vmem_limit_bytes=58 * 2**20),
    )(*operands)


class Terms:
    def __init__(self, lines, order, cols):
        self.lines, self.order, self.cols, self.left = lines, order, cols, list(lines.bits)
        self.terms = []

    def take(self, axis, at):
        found = []
        for box, taken, cols in self.terms:
            open_axes = [place_at for place_at, pick in enumerate(taken) if pick is None]
            picked = list(taken)
            picked[open_axes[axis]] = at
            found.append((box, tuple(picked), cols))
        return found

    def near_job(self, phase):
        turn = self.lines.turn
        (self.bit,) = self.order[turn:] if phase else self.order[:turn]
        self.axis = sum(1 for other in self.left if other > self.bit)
        return self.take(self.axis, 1)

    def near_send(self, send):
        got = self.lines.flip(send, self.bit)
        self.left.remove(self.bit)
        self.terms = self.take(self.axis, 0)
        self.terms.append((Box(got), (None,) * (got.ndim - 2), (0, got.shape[-1])))


class Sums:
    def __init__(self, lines, own, other, cut, rows):
        self.lines, self.rows, self.cut = lines, rows, cut
        self.plain = len(lines.bits) != 2
        self.own, self.other = Box(own), Box(other)
        self.lead = (2,) * len(lines.bits) + (4,)
        self.wide = own.shape[-1]
        self.parts = [
            Terms(lines, order, cols)
            for order, cols in zip(lines.orders, ((0, cut), (cut, self.wide)))
        ]

    def shaped(self, values):
        return values.reshape(self.lead + (self.rows, self.wide))

    def boxes(self):
        found = [self.own, self.other]
        for part in self.parts:
            found += [term[0] for term in part.terms]
        return found

    def swap(self):
        if self.plain:
            return
        mine = Box(self.shaped(self.own.value))
        mine.held = True
        got = Box(self.shaped(swap(self.other.value)))
        for part in self.parts:
            blank = (None,) * len(self.lead)
            part.terms = [(mine, blank, part.cols), (got, blank, part.cols)]

    def far_jobs(self):
        return [[part.take(0, steps) for part in self.parts] for steps in (1, 2, 3)]

    def far_send(self, sends):
        got = [Box(self.lines.shift(send, steps)) for send, steps in zip(sends, (1, 2, 3))]
        for part in self.parts:
            part.terms = part.take(0, 0) + [(box, (), part.cols) for box in got]

    def results(self, halved=(0, -1)):
        if not self.plain:
            return sum_parts([[part.terms] for part in self.parts], WIDE, halved)
        results = []
        both = self.own.value.astype(WIDE) + swap(self.other.value).astype(WIDE)
        for part in self.parts:
            total = self.shaped(both)[..., part.cols[0] : part.cols[1]]
            for bit in part.order:
                axis = sum(1 for other in part.left if other > bit)
                part.left.remove(bit)
                sent = lax.index_in_dim(total, 1, axis, keepdims=False).astype(LOW)
                total = lax.index_in_dim(total, 0, axis, keepdims=False)
                total = total + self.lines.flip(sent, bit).astype(WIDE)
            result = total[0]
            for steps in (1, 2, 3):
                got = self.lines.shift(total[steps].astype(LOW), steps)
                result = result + got.astype(WIDE)
            results.append(result)
        squares = sum(jnp.sum(result * result) for result in results)
        for result in results:
            if result.shape[1] == halved[0]:
                part = result[:, halved[1] : halved[1] + LANES]
                squares = squares - 0.5 * jnp.sum(part * part)
        return results + [jnp.pad(squares.reshape(1, 1), ((0, 0), (0, LANES - 1)))]


def move(*steps):
    work = []
    for total, kind in steps:
        if total.plain:
            continue
        if kind == 2:
            work.append((total.far_send, total.far_jobs()))
        else:
            for part in total.parts:
                work.append((part.near_send, [[part.near_job(kind)]]))
    if not work:
        return
    sends = sum_parts([job for send, jobs in work for job in jobs], LOW)
    at = 0
    for send, jobs in work:
        found = sends[at : at + len(jobs)]
        at += len(jobs)
        send(found if len(jobs) > 1 else found[0])


def fence_sums(sums, *values):
    boxes = {id(box): box for one in sums for box in one.boxes() if not box.held}
    boxes = list(boxes.values())
    held, values = lax.optimization_barrier(([box.value for box in boxes], values))
    for box, value in zip(boxes, held):
        box.value, box.held = value, True
    return values


def fence(*values):
    return lax.optimization_barrier(values)


def adam(weight, moment_one, moment_two, gradient, decay, rate):
    moment_one = BETA_ONE * moment_one + (1.0 - BETA_ONE) * gradient
    moment_two = BETA_TWO * moment_two + (1.0 - BETA_TWO) * gradient * gradient
    fixed_one = moment_one / (1.0 - BETA_ONE**STEP)
    fixed_two = moment_two / (1.0 - BETA_TWO**STEP)
    weight = weight - rate * (fixed_one / (jnp.sqrt(fixed_two) + EPSILON) + decay * weight)
    return [weight, moment_one, moment_two]


def adam_kernel(plan, scalars, side, *refs):
    count = len(plan)
    grads = refs[3 * count : -3 * count]
    factor = jnp.minimum(1.0, CLIP_NORM / (jnp.sqrt(scalars[0]) + 1e-06))
    for at, (rate, decay, pieces) in enumerate(plan):
        ins = refs[3 * at : 3 * at + 3]
        outs = refs[len(refs) - 3 * count + 3 * at :][:3]
        for grad, rows_from, cols_from, rows, cols in pieces:
            if isinstance(cols[0], bool):
                half = side[0] if cols[0] else 1 - side[0]
                span = pl.ds(pl.multiple_of(half * cols[1], LANES), cols[1])
            else:
                span = slice(*cols)
            where = (slice(*rows), span)
            gradient = grads[grad][slice(*rows_from), slice(*cols_from)] * factor
            results = adam(*[ref[where] for ref in ins], gradient, decay, rate)
            for out, result in zip(outs, results):
                out[where] = result


def adam_all(scalars, side, groups, grads, plan):
    outs = [jax.ShapeDtypeStruct(group[0].shape, WIDE) for group in groups for at in range(3)]
    scalar = pl.BlockSpec(memory_space=pltpu.SMEM)
    ins = [value for group in groups for value in group] + list(grads)
    found = pl.pallas_call(
        functools.partial(adam_kernel, plan),
        in_specs=[scalar, scalar] + [WHOLE] * len(ins),
        out_specs=[WHOLE] * len(outs),
        out_shape=outs,
        cost_estimate=pl.CostEstimate(
            flops=20_000_000, bytes_accessed=10_000_000, transcendentals=400_000
        ),
        compiler_params=pltpu.CompilerParams(vmem_limit_bytes=58 * 2**20),
    )(scalars, side, *ins)
    return [found[at : at + 3] for at in range(0, len(found), 3)]


def two_parts(values):
    high = lax.reduce_precision(values, 8, 7)
    fill = ((0, 0), (0, 8 - values.shape[1]))
    return jnp.concatenate([jnp.pad(high, fill), jnp.pad(values - high, fill)], 1).astype(LOW)


def widen_rows(values, rows):
    return jnp.pad(values, ((0, rows - values.shape[0]), (0, 0)))


def shards(
    patches,
    ctx_index,
    tgt_index,
    group,
    tgt_count,
    embed,
    embed_m,
    embed_v,
    bridge,
    bridge_m,
    bridge_v,
    enc_in,
    enc_in_m,
    enc_in_v,
    enc_out,
    enc_out_m,
    enc_out_v,
    enc_gains,
    enc_gains_m,
    enc_gains_v,
    pred_in,
    pred_in_m,
    pred_in_v,
    pred_out,
    pred_out_m,
    pred_out_v,
    pred_gains,
    pred_gains_m,
    pred_gains_v,
    t_embed,
    t_in,
    t_out,
    t_gains,
):
    index = lax.axis_index("dp")
    side = lax.axis_index("mp")
    dp_count = lax.axis_size("dp")
    lines = Lines(dp_count)
    assert patches.shape[0] == lax.axis_size("mp")
    count = patches.shape[0] * dp_count * TGT * D
    rows = D // dp_count
    p_rows = PW // dp_count
    half_d = D // 2
    local = D // 2
    ff = enc_in.shape[1] - 3 * local
    p_local = PW // 2
    p_ff = pred_in.shape[1] - 3 * p_local
    first = side == 0
    size = D // HEADS
    p_size = PW // PHEADS

    def own_half(values):
        return lax.dynamic_slice_in_dim(values, side * half_d, half_d, 1).astype(LOW)

    gains_pack = jnp.concatenate(
        [
            two_parts(enc_gains.T),
            two_parts(t_gains.T),
            widen_rows(two_parts(pred_gains.T), rows),
            jnp.zeros((rows, LANES - 48), LOW),
        ],
        1,
    )
    enc_in_low, t_in_low = enc_in.astype(LOW), t_in.astype(LOW)
    enc_out_low, t_out_low = enc_out.T.astype(LOW), t_out.T.astype(LOW)
    pred_in_low, pred_out_low = pred_in.astype(LOW), pred_out.T.astype(LOW)
    pred_main = jnp.concatenate([pred_out_low[:, p_local:], pred_in_low[:, 3 * p_local :]], 0)
    pred_rest = jnp.concatenate(
        [
            pred_in_low[:, : 2 * p_local],
            jnp.concatenate(
                [pred_in_low[:, 2 * p_local : 3 * p_local], pred_out_low[:, :p_local]], 1
            ),
        ],
        0,
    )
    packs = [
        [
            enc_in_low[:, : 3 * local],
            jnp.concatenate([own_half(embed), enc_out_low[:, :local], gains_pack], 1),
        ],
        [
            jnp.concatenate(
                [t_in_low[:, : 3 * local], own_half(t_embed), t_out_low[:, :local]], 1
            ),
            jnp.concatenate([own_half(bridge), pred_main, pred_rest], 1),
        ],
        [enc_in_low[:, 3 * local :], enc_out_low[:, local:]],
        [t_in_low[:, 3 * local :], t_out_low[:, local:]],
    ]

    far_a = gather_far(lines, packs[0])
    far_a, packs[1] = fence(far_a, packs[1])
    near_a = gather_near(lines, far_a, 0)
    near_a, packs[1], patches, ctx_index, tgt_index, group, tgt_count = fence(
        near_a, packs[1], patches, ctx_index, tgt_index, group, tgt_count
    )
    order = lines.order(index, D)
    p_order = lines.order(index, PW)
    eye = jnp.eye(D, dtype=LOW)
    patch = lax.dynamic_index_in_dim(patches, side, 0, keepdims=False)
    ctx = lax.dynamic_index_in_dim(ctx_index, side, 0, keepdims=False)
    tgt = lax.dynamic_index_in_dim(tgt_index, side, 0, keepdims=False)
    single = lax.dynamic_index_in_dim(group, side, 0, keepdims=False) == 1
    used = lax.dynamic_index_in_dim(tgt_count, side, 0, keepdims=False)
    positions = jnp.arange(patch.shape[0])
    chosen = jnp.concatenate([ctx, tgt])
    all_id, all_row, all_col = place(single, positions)
    joined_id, joined_row, joined_col = place(single, chosen)
    ctx_id, tgt_id = joined_id[:CTX], joined_id[CTX:]

    spread = jnp.arange(D) // rows * p_rows + jnp.arange(D) % rows
    spread = (jnp.arange(PW)[:, None] == spread) & (jnp.arange(D) % rows < p_rows)
    spread = spread.astype(LOW)
    pos_all = sincos(all_row, all_col, D, order)
    pos_ctx = sincos(joined_row[:CTX], joined_col[:CTX], D, order)
    pos_tgt = sincos(joined_row[CTX:], joined_col[CTX:], D, order)
    pos_small = sincos(joined_row, joined_col, PW, p_order)
    patch = mm(patch, order).astype(LOW)
    seen_ctx = mm((ctx[:, None] == positions).astype(LOW), patch).astype(LOW)
    seen_tgt = mm((tgt[:, None] == positions).astype(LOW), patch).astype(LOW)
    order_own = lax.dynamic_slice_in_dim(order, side * half_d, half_d, 0)
    order_other = lax.dynamic_slice_in_dim(order, (1 - side) * half_d, half_d, 0)
    held_a = gather_near(lines, near_a, 1)
    far_b = gather_far(lines, packs[1])
    (
        held_a,
        far_b,
        pos_all,
        pos_ctx,
        pos_tgt,
        pos_small,
        patch,
        seen_ctx,
        seen_tgt,
        order_own,
        order_other,
        spread,
        order,
        p_order,
        eye,
        all_id,
        ctx_id,
        tgt_id,
        joined_id,
        used,
        packs[2],
    ) = fence(
        held_a,
        far_b,
        pos_all,
        pos_ctx,
        pos_tgt,
        pos_small,
        patch,
        seen_ctx,
        seen_tgt,
        order_own,
        order_other,
        spread,
        order,
        p_order,
        eye,
        all_id,
        ctx_id,
        tgt_id,
        joined_id,
        used,
        packs[2],
    )
    other_a = swap_all(held_a)
    near_b = gather_near(lines, far_b, 0)
    held_a, other_a, near_b, packs[2] = fence(held_a, other_a, near_b, packs[2])

    def widths(values, *sizes):
        found, at = [], 0
        for wide in sizes:
            found.append(values[:, at : at + wide])
            at += wide
        return found

    enc_qkv = (flat(held_a[0]), flat(other_a[0]))
    enc_rest = (flat(held_a[1]), flat(other_a[1]))
    held_b = gather_near(lines, near_b, 1)
    far_c = gather_far(lines, packs[2])
    start, normed_one, *projected, enc_gain, target_gain, pred_gain = ctx_first(
        seen_ctx,
        pos_ctx,
        spread,
        (order_own, order_other),
        enc_rest,
        enc_qkv,
    )
    held_b, far_c, start, projected, packs[3] = fence(
        held_b, far_c, start, projected, packs[3]
    )
    other_b = swap_all(held_b)
    near_c = gather_near(lines, far_c, 0)
    middle, normed_two, *pairs = ctx_second(
        size, start, enc_gain, ctx_id, enc_rest, projected
    )
    mixed, logs = pairs[:2], pairs[2:]
    held_b, other_b, near_c, normed_two, middle, packs[3] = fence(
        held_b, other_b, near_c, normed_two, middle, packs[3]
    )
    held_c = gather_near(lines, near_c, 1)
    far_d = gather_far(lines, packs[3])
    t_middle, t_two = target_forward(
        size,
        patch,
        seen_tgt,
        pos_all,
        pos_tgt,
        target_gain,
        tgt_id,
        all_id,
        (order_own, order_other),
        (flat(held_b[0]), flat(other_b[0])),
    )
    held_c, far_d, t_middle, t_two = fence(held_c, far_d, t_middle, t_two)
    other_c = swap_all(held_c)
    near_d = gather_near(lines, far_d, 0)
    bridge_in, bridge_out, pairs = pred_parts(
        dp_count, side.astype(jnp.int32), flat(held_b[1]), flat(other_b[1]), p_order
    )
    pred_down, pred_up, pred_qk, pred_right = pairs
    held_c, other_c, near_d, bridge_in, bridge_out, pred_down, pred_up, pred_qk, pred_right = fence(
        held_c, other_c, near_d, bridge_in, bridge_out, pred_down, pred_up, pred_qk, pred_right
    )
    held_d = gather_near(lines, near_d, 1)
    enc_up, enc_down = [(flat(own), flat(other)) for own, other in zip(held_c, other_c)]
    hidden, context, *pairs = ff_forward(
        normed_two, middle, enc_gain, enc_up, enc_down
    )
    activated, slope = pairs[:2], pairs[2:]
    held_d, hidden, context, activated, slope = fence(held_d, hidden, context, activated, slope)
    other_d = swap_all(held_d)
    (
        joined,
        p_normed_one,
        p_middle,
        p_normed_two,
        predicted,
        final,
        guess,
        *pairs,
    ) = pred_forward(
        p_size,
        context,
        bridge_in,
        bridge_out,
        pos_small,
        pred_gain,
        tgt_id,
        joined_id,
        pred_down,
        pred_up,
        pred_qk,
        pred_right,
    )
    p_qk, p_values, p_mixed, p_activated, p_slope = [
        pairs[at : at + 2] for at in range(0, 10, 2)
    ]
    p_logs = pairs[10]
    other_d, guess = fence(other_d, guess)
    target = target_ff(
        t_two,
        t_middle,
        target_gain,
        (flat(held_d[0]), flat(other_d[0])),
        (flat(held_d[1]), flat(other_d[1])),
    )
    (
        loss_local,
        d_inward,
        grad_bridge_in,
        grad_bridge_out,
        sums_pred,
        *pairs,
    ) = pred_back_all(
        p_size,
        count,
        used[None],
        [
            guess,
            target,
            context,
            final,
            bridge_in,
            bridge_out,
            pred_gain,
            predicted,
            p_middle,
            joined,
            p_normed_one,
            p_normed_two,
        ],
        [
            pred_down,
            pred_up,
            pred_qk,
            pred_right,
            p_activated,
            p_slope,
            p_qk,
            p_values,
            p_mixed,
        ],
        p_logs,
        tgt_id,
        joined_id,
    )
    grads_left, grads_right = pairs[:2], pairs[2:]

    def blocks(values):
        return values.reshape(dp_count, p_rows, -1)

    bridge_pair = [
        mm_t(jnp.where(first, low, high), p_order).astype(LOW).reshape(dp_count, rows, -1)
        for low, high in (
            (grad_bridge_in, grad_bridge_out),
            (grad_bridge_out, grad_bridge_in),
        )
    ]
    pair_p = [
        jnp.concatenate(
            [
                blocks(grads_left[at]),
                bridge_pair[at][:, :p_rows],
                blocks(grads_right[at]),
                bridge_pair[at][:, p_rows:],
            ],
            2,
        )
        for at in (0, 1)
    ]
    sum_p = Sums(lines, *pair_p, 4 * local, p_rows)
    (d_inward,) = fence_sums([sum_p], d_inward)
    sum_p.swap()
    (d_inward,) = fence_sums([sum_p], d_inward)
    move((sum_p, 0))
    grads_own, grads_other, branch, d_middle, sums_ff = ff_back(
        d_inward,
        bridge_in,
        hidden,
        middle,
        normed_two,
        eye,
        enc_gain,
        activated,
        slope,
        enc_up,
        enc_down,
    )
    sum_f = Sums(lines, grads_own, grads_other, ff, rows)
    branch, d_middle = fence_sums([sum_p, sum_f], branch, d_middle)
    sum_f.swap()
    move((sum_p, 1))
    branch, d_middle = fence_sums([sum_p, sum_f], branch, d_middle)
    move((sum_f, 0), (sum_p, 2))
    d_proj = attn_back(size, branch, ctx_id, enc_rest, projected, mixed, logs)
    (d_proj,) = fence_sums([sum_p, sum_f], d_proj)
    move((sum_f, 1))
    grads_own, grads_other = qkv_back(
        branch,
        d_middle,
        start,
        normed_one,
        seen_ctx,
        eye,
        enc_gain,
        sums_ff,
        sums_pred,
        spread,
        [d_proj, mixed, enc_qkv, (order_own, order_other)],
    )
    sum_a = Sums(lines, grads_own, grads_other, 3 * local, rows)
    fence_sums([sum_f, sum_a])
    sum_a.swap()
    fence_sums([sum_f, sum_a])
    move((sum_f, 2), (sum_a, 0))
    fence_sums([sum_f, sum_a])
    move((sum_a, 1))
    fence_sums([sum_a])
    move((sum_a, 2))

    red_left, red_right, squares_p = sum_p.results()
    red_up, red_down, squares_f = sum_f.results()
    red_qkv, red_rest, squares_a = sum_a.results((2 * local + LANES, 2 * local))
    low_one = p_ff + 2 * p_local
    bridge_other = swap(jnp.concatenate([red_left[:, low_one:], red_right[:, low_one:]], 0))
    embed_other = swap(red_rest[:, :local])
    gains_t = red_rest[:, 2 * local :].T
    sums = jnp.concatenate([squares_p + squares_f + squares_a, loss_local], 1)
    sums = jnp.stack([jnp.sum(sums[:, :LANES]), sums[0, LANES]])
    for step in range(0, dp_count.bit_length(), 2):
        sums = lines.add_all(sums, step, min(step + 2, dp_count.bit_length()))
    groups = [
        (embed, embed_m, embed_v),
        (bridge, bridge_m, bridge_v),
        (enc_in, enc_in_m, enc_in_v),
        (enc_out.T, enc_out_m.T, enc_out_v.T),
        (enc_gains, enc_gains_m, enc_gains_v),
        (pred_in, pred_in_m, pred_in_v),
        (pred_out.T, pred_out_m.T, pred_out_v.T),
        (pred_gains, pred_gains_m, pred_gains_v),
    ]
    grads = [
        red_left,
        red_right,
        red_up,
        red_down,
        red_qkv,
        red_rest,
        bridge_other,
        embed_other,
        gains_t,
    ]
    every, part = (0, rows), (0, p_rows)
    lower = (p_rows, 2 * p_rows)
    qk_end, v_end = p_ff + 2 * p_local, p_ff + p_local
    learn, gain = (LEARN_RATE, WEIGHT_DECAY), (GAIN_RATE, 0.0)
    plan = (
        (
            *learn,
            (
                (5, every, (0, local), every, (True, half_d)),
                (7, every, (0, local), every, (False, half_d)),
            ),
        ),
        (
            *learn,
            (
                (0, part, (qk_end, qk_end + half_d), part, (True, half_d)),
                (1, part, (qk_end, qk_end + half_d), lower, (True, half_d)),
                (6, every, (0, half_d), every, (False, half_d)),
            ),
        ),
        (
            *learn,
            (
                (4, every, (0, 3 * local), every, (0, 3 * local)),
                (2, every, (0, ff), every, (3 * local, 3 * local + ff)),
            ),
        ),
        (
            *learn,
            (
                (5, every, (local, 2 * local), every, (0, local)),
                (3, every, (0, ff), every, (local, local + ff)),
            ),
        ),
        (*gain, ((8, (0, 6), every, (0, 6), every),)),
        (
            *learn,
            (
                (0, part, (p_ff, qk_end), part, (0, 2 * p_local)),
                (1, part, (p_ff, v_end), part, (2 * p_local, 3 * p_local)),
                (1, part, (0, p_ff), part, (3 * p_local, 3 * p_local + p_ff)),
            ),
        ),
        (
            *learn,
            (
                (1, part, (v_end, qk_end), part, (0, p_local)),
                (0, part, (0, p_ff), part, (p_local, p_local + p_ff)),
            ),
        ),
        (*gain, ((8, (8, 15), part, (0, 7), part),)),
    )
    results = adam_all(sums, side[None].astype(jnp.int32), groups, grads, plan)
    for at in (3, 6):
        results[at] = [value.T for value in results[at]]
    return (*[value for result in results for value in result], sums[1], jnp.sqrt(sums[0]))


def solution(mesh):
    in_specs = (
        P("dp", None, None),
        P("dp", None),
        P("dp", None),
        P("dp"),
        P("dp"),
        P("dp", None),
        P("dp", None),
        P("dp", None),
        P("dp", None),
        P("dp", None),
        P("dp", None),
        P("dp", "mp"),
        P("dp", "mp"),
        P("dp", "mp"),
        P("mp", "dp"),
        P("mp", "dp"),
        P("mp", "dp"),
        P(None, "dp"),
        P(None, "dp"),
        P(None, "dp"),
        P("dp", "mp"),
        P("dp", "mp"),
        P("dp", "mp"),
        P("mp", "dp"),
        P("mp", "dp"),
        P("mp", "dp"),
        P(None, "dp"),
        P(None, "dp"),
        P(None, "dp"),
        P("dp", None),
        P("dp", "mp"),
        P("mp", "dp"),
        P(None, "dp"),
    )
    out_specs = (
        P("dp", None),
        P("dp", None),
        P("dp", None),
        P("dp", None),
        P("dp", None),
        P("dp", None),
        P("dp", "mp"),
        P("dp", "mp"),
        P("dp", "mp"),
        P("mp", "dp"),
        P("mp", "dp"),
        P("mp", "dp"),
        P(None, "dp"),
        P(None, "dp"),
        P(None, "dp"),
        P("dp", "mp"),
        P("dp", "mp"),
        P("dp", "mp"),
        P("mp", "dp"),
        P("mp", "dp"),
        P("mp", "dp"),
        P(None, "dp"),
        P(None, "dp"),
        P(None, "dp"),
        P(),
        P(),
    )
    return jax.shard_map(shards, mesh=mesh, in_specs=in_specs, out_specs=out_specs, check_vma=False)
```

time: 597 us -> 547 us (0.916)
  other arithmetic: 97.7 us -> 32.5 us
  Pallas kernels: 194 us -> 243 us
  local copies, waits for them, and re-layouts: 83.4 us -> 47 us
  waiting for transfers between devices: 99.3 us -> 116 us
  starting transfers between devices: 86 us -> 80 us
    pallas_call x8 -> x29, Pallas kernels: 168 us -> 219 us  [the longest x13 158 us: on_chip(): pl.pallas_call(kernel, in_specs=in_specs, out_specs=out_specs, out_shape=...]
    convert_element_type x21 -> x1, other arithmetic: 35.4 us -> 1.04 us  [shards(): spread = spread.astype(LOW)]
    another operation x20 -> x1, local copies, waits for them, and re-layouts: 14.8 us -> 0.01 us  [the longest x12 8.52 us: gather_far(): jnp.stack([block[:, cut:] for block in found])]
    slice x31 -> x11, local copies, waits for them, and re-layouts: 16.7 us -> 3.16 us  [the longest x1 0.89 us: shards(): embed_other = swap(red_rest[:, :local])]
    ppermute x30 -> x21, starting transfers between devices: 47.1 us -> 35.5 us  [shift(): return lax.ppermute(values, 'dp', pairs)]
    another operation x29 -> x14, other arithmetic: 24.5 us -> 13.3 us  [the longest x8 11.1 us: gather_near(): jnp.stack([values, other], axis)]
    ppermute x0 -> x7, starting transfers between devices: none -> 10.3 us  [add_all(): total = total + lax.ppermute(values, ('dp', 'mp'), pairs)]
    optimization_barrier x6 -> x0, local copies, waits for them, and re-layouts: 10.1 us -> none  [fence(): return lax.optimization_barrier(values)]
  transfers between devices with their start and end apart: 78 -> 69, of which waited for: 23 -> 27; matrix products, arithmetic and copies ran while one was open for 24% -> 10% of each run, Pallas kernels for 27% -> 30%
where the time goes in v2:
time: 547 us; the launch traced here: 537 us
  Pallas kernels  243 us (44%)
  waiting for transfers between devices  116 us (21%)
  starting transfers between devices  80 us (15%)
  local copies, waits for them, and re-layouts  47 us (9%)
  other arithmetic  32.5 us (6%)
  matrix products  14.1 us (3%)
    pallas_call x13, Pallas kernels, on_chip(): pl.pallas_call(kernel, in_specs=in_specs, out_specs=out_specs, out_shape=...  158 us
    ppermute x28, waiting for transfers between devices, flip(): return lax.ppermute(values, 'dp', pairs)  58.9 us
    ppermute x21, waiting for transfers between devices, shift(): return lax.ppermute(values, 'dp', pairs)  41.5 us
    ppermute x21, starting transfers between devices, shift(): return lax.ppermute(values, 'dp', pairs)  35.5 us
    pallas_call x10, Pallas kernels, sum_parts(): pl.pallas_call(functools.partial(sum_kernel, tuple(plan), squares), grid=...  34.6 us
    ppermute x28, starting transfers between devices, flip(): return lax.ppermute(values, 'dp', pairs)  31.3 us
    unnamed x224, local copies, waits for them, and re-layouts  27.1 us
    pallas_call x1, Pallas kernels, pred_back_all(): pl.pallas_call(functools.partial(pred_back_all_kernel, size, count_all),...  23.7 us
  transfers between devices with their start and end apart: 69, of which 27 were waited for; matrix products, arithmetic and copies ran while one was open for 10% of the time, Pallas kernels for 30%

profile of v2, /device:TPU:0, one launch (start us, length us, event | category | flops | bytes accessed | tf_op | source)
XLA Modules:
  0.0 537.3 jit_solution(11379144675736985694)
XLA Ops:
  5.3 5.1 collective-permute-start
  33.4 5.3 collective-permute-done.4
  89.4 13.3 %collective-permute-done.13 = bf16[4,48,1536]{2,1,0:T(8,128)(2,1)S(1)} collective-permute-done((bf16[4,48,1536]{2,1,0:T(8,128)(2,1)S(1)}, bf16[4,48,1536]{2,1,0:T(8,128)(2,1)S(1)}, u32[]{:S(2)}, u32[]{:S(2)}) %collective-permute-start.13) | collective-permute-done | bytes 589856 | tf_op jit(solution)/shard_map/ppermute | solution.py:925
  114.8 11.1 %shard_map.517 = (f32[512,768]{1,0:T(8,128)}, bf16[512,768]{1,0:T(8,128)(2,1)}, bf16[512,1152]{1,0:T(8,128)(2,1)}, bf16[512,1152]{1,0:T(8,128)(2,1)}, f32[8,768]...) custom-call(bf16[512,768]{1,0:T(8,128)(2,1)} %fusion.6.refs_0_.refs_4_, f32[512,768]{1,0:T(8,128)} %fusion.106.refs_1_, ...), custom_call_target="tpu_custom_call" | custom-call | flops 3321888768 | bytes 15200256 | tf_op jit(solution)/shard_map/pallas_call | solution.py:204
  126.0 12.0 %collective-permute-done.17.refs_2_ = bf16[48,3072]{1,0:T(8,128)(2,1)} collective-permute-done((bf16[48,3072]{1,0:T(8,128)(2,1)S(1)}, bf16[48,3072]{1,0:T(8,128)(2,1)}, u32[]{:S(2)}, u32[]{:S(2)}) %collective-permute-start.17) | collective-permute-done | bytes 294944 | tf_op jit(solution)/shard_map/ppermute | solution.py:929
  142.2 4.1 shard_map.515
  150.8 14.9 %shard_map.518 = (f32[512,768]{1,0:T(8,128)}, bf16[512,768]{1,0:T(8,128)(2,1)}, bf16[512,384]{1,0:T(8,128)(2,1)}, bf16[512,384]{1,0:T(8,128)(2,1)}, f32[2,8,512]{2,1,0:T(8,128)}, /*index=5*/f32[2,8,512]{2,1,0:T(8,128)}) custom-call(f32[512,768]{1,0:T(8,128)} %get-tuple-element.342.refs_0_.refs_2_, f32[8,768]{1,0:T(8,128)} %get-tuple-element.343.refs_1_.refs_2_.refs_6_, ...), custom_call_target="tpu_custom_call" | custom-call | flops 1409286144 | bytes 9924608 | tf_op jit(solution)/shard_map/pallas_call | solution.py:204
  174.3 19.4 %shard_map.521 = (f32[256,768]{1,0:T(8,128)S(1)}, bf16[256,768]{1,0:T(8,128)(2,1)S(1)}) custom-call(bf16[784,768]{1,0:T(8,128)(2,1)S(1)} %copy-done.23, bf16[256,768]{1,0:T(8,128)(2,1)S(1)} %copy-done.24, f32[784,768]{1,0:T(8,128)S(1)} %fusion.105.refs_2_, f32[256,768]{1,0:T(8,128)S(1)} %fusion.107.refs_3_, f32[8,768]{1,0:T(8,128)S(1)} %copy-done.12, ...), custom_call_target="tpu_custom_call" | custom-call | flops 4297064448 | bytes 13078592 | tf_op jit(solution)/shard_map/pallas_call | solution.py:204
  201.8 3.9 shard_map.519
  209.3 5.2 shard_map.522
  214.5 7.1 %collective-permute-done.31 = bf16[4,48,1536]{2,1,0:T(8,128)(2,1)S(1)} collective-permute-done((bf16[4,48,1536]{2,1,0:T(8,128)(2,1)S(1)}, bf16[4,48,1536]{2,1,0:T(8,128)(2,1)S(1)}, u32[]{:S(2)}, u32[]{:S(2)}) %collective-permute-start.31) | collective-permute-done | bytes 589856 | tf_op jit(solution)/shard_map/ppermute | solution.py:925
  225.0 17.9 %shard_map.524 = (f32[512,768]{1,0:T(8,128)}, bf16[512,768]{1,0:T(8,128)(2,1)}, bf16[512,1536]{1,0:T(8,128)(2,1)}, bf16[512,1536]{1,0:T(8,128)(2,1)}, bf16[512,1...) custom-call(bf16[512,768]{1,0:T(8,128)(2,1)} %get-tuple-element.391.refs_0_.refs_4_, ...), custom_call_target="tpu_custom_call" | custom-call | flops 5435817984 | bytes 20471808 | tf_op jit(solution)/shard_map/pallas_call | solution.py:204
  243.0 6.9 %collective-permute-done.32.refs_2_ = bf16[2,4,48,1536]{3,2,1,0:T(8,128)(2,1)S(1)} collective-permute-done((bf16[2,4,48,1536]{3,2,1,0:T(8,128)(2,1)S(1)}, bf16[2,4,48,1536]{3,2,1,0:T(8,128)(2,1)S(1)}, u32[]{:S(2)}, u32[]{:S(2)}) %collective-permute-start.32) | collective-permute-done | bytes 1179680 | tf_op jit(solution)/shard_map/ppermute | solution.py:925
  251.9 3.7 shard_map.523
  257.2 18.0 %shard_map.525 = (f32[768,384]{1,0:T(8,128)}, bf16[768,384]{1,0:T(8,128)(2,1)}, f32[256,384]{1,0:T(8,128)}, bf16[256,384]{1,0:T(8,128)(2,1)}, f32[256,384]{1,0:T...) custom-call(bf16[512,768]{1,0:T(8,128)(2,1)} %get-tuple-element.405., ...), custom_call_target="tpu_custom_call" | custom-call | flops 2000000000 | bytes 13991936 | tf_op jit(solution)/shard_map/pallas_call | solution.py:204
  276.5 11.0 %shard_map.526.refs_1_ = f32[256,768]{1,0:T(8,128)} custom-call(bf16[256,768]{1,0:T(8,128)(2,1)} %copy-done.11, f32[256,768]{1,0:T(8,128)} %copy-done.8, f32[8,768]{1,0:T(8,128)} %get-tuple-element.363.refs_4_.refs_2_, bf16[768,1536]{1,0:T(8,128)(2,1)} %bitcast.160, bf16[768,1536]{1,0:T(8,128)(2,1)} %bitcast.162, bf16[768,1536]{1,0:T(8,128)(2,1)} %bitcast.161, ...), custom_call_target="tpu_custom_call" | custom-call | flops 2415919104 | bytes 11427840 | tf_op jit(solution)/shard_map/pallas_call | solution.py:204
  287.6 23.7 %shard_map.527 = (f32[1,1]{1,0:T(1,128)}, bf16[512,384]{1,0:T(8,128)(2,1)}, bf16[768,384]{1,0:T(8,128)(2,1)}, bf16[768,384]{1,0:T(8,128)(2,1)}, f32[8,384]{1,0:T...) custom-call(f32[256,768]{1,0:T(8,128)} %get-tuple-element.420.refs_0, ...), custom_call_target="tpu_custom_call" | custom-call | flops 4000000000 | bytes 20000000 | tf_op jit(solution)/shard_map/pallas_call | solution.py:848
  318.3 4.4 collective-permute-done.36
  329.9 21.3 %shard_map.529 = (bf16[768,3072]{1,0:T(8,128)(2,1)}, bf16[768,3072]{1,0:T(8,128)(2,1)}, bf16[512,768]{1,0:T(8,128)(2,1)}, f32[512,768]{1,0:T(8,128)}, f32[8,768]{1,0:T(8,128)}) custom-call(bf16[512,384]{1,0:T(8,128)(2,1)} %get-tuple-element.456.refs_0_, bf16[768,384]{1,0:T(8,128)(2,1)} %get-tuple-element.406.refs_1_.refs_5_, ...), custom_call_target="tpu_custom_call" | custom-call | flops 9663676416 | bytes 33669120 | tf_op jit(solution)/shard_map/pallas_call | solution.py:204
  356.8 6.9 %collective-permute-done.39.refs_7_.refs_13_.refs_19_.refs_3_ = bf16[4,24,1536]{2,1,0:T(8,128)(2,1)S(1)} collective-permute-done((bf16[4,24,1536]{2,1,0:T(8,128)(2,1)}, bf16[4,24,1536]{2,1,0:T(8,128)(2,1)S(1)}, u32[]{:S(2)}, u32[]{:S(2)}) %collective-permute-start.39) | collective-permute-done | bytes 294944 | tf_op jit(solution)/shard_map/ppermute | solution.py:925
  367.0 6.1 %shard_map.531 = (bf16[2,4,48,1536]{3,2,1,0:T(8,128)(2,1)}, bf16[2,4,48,1536]{3,2,1,0:T(8,128)(2,1)}, bf16[24,3072]{1,0:T(8,128)(2,1)}, bf16[24,3072]{1,0:T(8,128)(2,1)}, bf16[24,3072]{1,0:T(8,128)(2,1)}) custom-call(bf16[2,2,4,48,3072]{4,3,2,1,0:T(8,128)(2,1)} %bitcast.111, bf16[2,2,4,48,3072]{4,3,2,1,0:T(8,128)(2,1)} %bitcast.119, ...), custom_call_target="tpu_custom_call" | custom-call | flops 11206656 | bytes 11206656 | tf_op jit(solution)/shard_map/pallas_call | solution.py:1103
  381.1 16.5 %shard_map.532 = (bf16[512,1152]{1,0:T(8,128)(2,1)S(1)}, bf16[512,1152]{1,0:T(8,128)(2,1)S(1)}) custom-call(bf16[512,768]{1,0:T(8,128)(2,1)S(1)} %copy-done.27, s32[1,512]{1,0:T(1,128)S(1)} %bitcast.106, s32[512,1]{1,0:T(8,128)S(1)} %copy-done.7, bf16[768,896]{1,0:T(8,128)(2,1)S(1)} %bitcast.100, bf16[768,896]{1,0:T(8,128)(2,1)S(1)} %bitcast.103, ...), custom_call_target="tpu_custom_call" | custom-call | flops 2617245696 | bytes 9113600 | tf_op jit(solution)/shard_map/pallas_call | solution.py:204
  400.0 3.9 shard_map.534
  406.5 18.9 %shard_map.535 = (bf16[768,2048]{1,0:T(8,128)(2,1)}, bf16[768,2048]{1,0:T(8,128)(2,1)}) custom-call(bf16[512,768]{1,0:T(8,128)(2,1)} %get-tuple-element.483.branch.refs_0_, f32[512,768]{1,0:T(8,128)} %get-tuple-element.498.refs_1_, f32[512,768]{1,0:T(8,128)} %get-tuple-element.342.refs_0_.refs_2_, bf16[512,768]{1,0:T(8,128)(2,1)} %get-tuple-element.499.refs_3_, ...), custom_call_target="tpu_custom_call" | custom-call | flops 6039797760 | bytes 21491712 | tf_op jit(solution)/shard_map/pallas_call | solution.py:204
  425.6 5.9 %collective-permute-done.49 = bf16[768,2048]{1,0:T(8,128)(2,1)S(1)} collective-permute-done((bf16[768,2048]{1,0:T(8,128)(2,1)}, bf16[768,2048]{1,0:T(8,128)(2,1)S(1)}, u32[]{:S(2)}, u32[]{:S(2)}) %collective-permute-start.49) | collective-permute-done | bytes 3145760 | tf_op jit(solution)/shard_map/ppermute | solution.py:949
  433.1 5.6 %shard_map.536 = (bf16[48,3072]{1,0:T(8,128)(2,1)}, bf16[48,3072]{1,0:T(8,128)(2,1)}, bf16[48,3072]{1,0:T(8,128)(2,1)}, bf16[2,4,48,1152]{3,2,1,0:T(8,128)(2,1)}, bf16[2,4,48,896]{3,2,1,0:T(8,128)(2,1)}) custom-call(bf16[2,2,4,48,3072]{4,3,2,1,0:T(8,128)(2,1)} %bitcast.115, bf16[2,2,4,48,3072]{4,3,2,1,0:T(8,128)(2,1)} %bitcast.123, ...), custom_call_target="tpu_custom_call" | custom-call | flops 9830400 | bytes 9830400 | tf_op jit(solution)/shard_map/pallas_call | solution.py:1103
  445.0 7.3 %collective-permute-done.50.refs_4_ = bf16[48,3072]{1,0:T(8,128)(2,1)S(1)} collective-permute-done((bf16[48,3072]{1,0:T(8,128)(2,1)}, bf16[48,3072]{1,0:T(8,128)(2,1)S(1)}, u32[]{:S(2)}, u32[]{:S(2)}) %collective-permute-start.50) | collective-permute-done | bytes 294944 | tf_op jit(solution)/shard_map/ppermute | solution.py:929
  452.3 11.3 %collective-permute-done.51.refs_5_ = bf16[48,3072]{1,0:T(8,128)(2,1)S(1)} collective-permute-done((bf16[48,3072]{1,0:T(8,128)(2,1)}, bf16[48,3072]{1,0:T(8,128)(2,1)S(1)}, u32[]{:S(2)}, u32[]{:S(2)}) %collective-permute-start.51) | collective-permute-done | bytes 294944 | tf_op jit(solution)/shard_map/ppermute | solution.py:929
  471.2 6.4 %collective-permute-done.56.refs_5_.refs_11_.refs_17_.refs_8_ = bf16[4,48,896]{2,1,0:T(8,128)(2,1)S(1)} collective-permute-done((bf16[4,48,896]{2,1,0:T(8,128)(2,1)}, bf16[4,48,896]{2,1,0:T(8,128)(2,1)S(1)}, u32[]{:S(2)}, u32[]{:S(2)}) %collective-permute-start.56) | collective-permute-done | bytes 344096 | tf_op jit(solution)/shard_map/ppermute | solution.py:925
  482.3 6.9 %collective-permute-start.57 = (bf16[48,2048]{1,0:T(8,128)(2,1)}, bf16[48,2048]{1,0:T(8,128)(2,1)S(1)}, u32[]{:S(2)}, u32[]{:S(2)}) collective-permute-start(bf16[48,2048]{1,0:T(8,128)(2,1)} %get-tuple-element.525), channel_id=1, source_target_pairs={{0,8},{2,10},{4,12},{6,14},{8,16},{10,18},{12,20},{14,22},{16,24},... | collective-permute-start | bytes 589832 | tf_op jit(solution)/shard_map/ppermute | solution.py:929
  514.9 4.0 collective-permute-start.64
  529.8 6.1 %shard_map.541 = (f32[48,768]{1,0:T(8,128)}, f32[48,768]{1,0:T(8,128)}, f32[48,768]{1,0:T(8,128)}, f32[48,768]{1,0:T(8,128)}, f32[48,768]{1,0:T(8,128)}, /*index...) custom-call(f32[2]{0:T(128)} %copy-done.95, ...), custom_call_target="tpu_custom_call" | custom-call | flops 20000000 | bytes 10000000 | tf_op jit(solution)/shard_map/pallas_call | solution.py:1275
  (485 shorter events, 217.9 us)
Async XLA Ops:
  5.3 20.4 %collective-permute-start = (bf16[48,2048]{1,0:T(8,128)(2,1)S(1)}, bf16[48,2048]{1,0:T(8,128)(2,1)}, u32[]{:S(2)}, u32[]{:S(2)}) collective-permute-start(bf16[48,2048]{1,0:T(8,128)(2,1)S(1)} %concatenate.139.refs_0_), channel_id=1, source_target_pairs={{0,24},{2,26},{4,28},{6,30},{8,0},{10,2},{12,4},{14,6},{16,8},{18,... | collective-permute-start | bytes 589832 | tf_op jit(solution)/shard_map/ppermute | solution.py:929
  47.8 27.4 %collective-permute-start.7 = (bf16[48,3456]{1,0:T(8,128)(2,1)}, bf16[48,3456]{1,0:T(8,128)(2,1)}, u32[]{:S(2)}, u32[]{:S(2)}) collective-permute-start(bf16[48,3456]{1,0:T(8,128)(2,1)} %constant_dynamic-update-slice_fusion.refs_0_), channel_id=1, source_target_pairs={{0,24},{2,26},{4,28},{6,30},{8,0},{10,2},{12,4},{14,6},{16,8},{18,... | collective-permute-start | bytes 995336 | tf_op jit(solution)/shard_map/ppermute | solution.py:929
  49.3 29.0 %collective-permute-start.8 = (bf16[48,3456]{1,0:T(8,128)(2,1)}, bf16[48,3456]{1,0:T(8,128)(2,1)}, u32[]{:S(2)}, u32[]{:S(2)}) collective-permute-start(bf16[48,3456]{1,0:T(8,128)(2,1)} %constant_dynamic-update-slice_fusion.refs_0_), channel_id=1, source_target_pairs={{0,16},{2,18},{4,20},{6,22},{8,24},{10,26},{12,28},{14,30},{16,0},... | collective-permute-start | bytes 995336 | tf_op jit(solution)/shard_map/ppermute | solution.py:929
  50.6 27.6 %collective-permute-start.9 = (bf16[48,3456]{1,0:T(8,128)(2,1)}, bf16[48,3456]{1,0:T(8,128)(2,1)}, u32[]{:S(2)}, u32[]{:S(2)}) collective-permute-start(bf16[48,3456]{1,0:T(8,128)(2,1)} %constant_dynamic-update-slice_fusion.refs_0_), channel_id=1, source_target_pairs={{0,8},{2,10},{4,12},{6,14},{8,16},{10,18},{12,20},{14,22},{16,24},... | collective-permute-start | bytes 995336 | tf_op jit(solution)/shard_map/ppermute | solution.py:929
  86.8 21.9 %collective-permute-start.10 = (bf16[2,2,4,48,1152]{4,3,2,1,0:T(8,128)(2,1)}, bf16[2,2,4,48,1152]{4,3,2,1,0:T(8,128)(2,1)S(1)}, u32[]{:S(2)}, u32[]{:S(2)}) collective-permute-start(bf16[2,2,4,48,1152]{4,3,2,1,0:T(8,128)(2,1)} %get-tuple-element.333), channel_id=1, source_target_pairs={{0,1},{1,0},{2,3},{3,2},{4,5},{5,4},{6,7},{7,6},{8,9},{9,8},{10,11... | collective-permute-start | bytes 5308424 | tf_op jit(solution)/shard_map/ppermute | solution.py:949
  86.9 21.8 %collective-permute-start.11 = (bf16[2,2,4,48,896]{4,3,2,1,0:T(8,128)(2,1)}, bf16[2,2,4,48,896]{4,3,2,1,0:T(8,128)(2,1)S(1)}, u32[]{:S(2)}, u32[]{:S(2)}) collective-permute-start(bf16[2,2,4,48,896]{4,3,2,1,0:T(8,128)(2,1)} %get-tuple-element.331), channel_id=1, source_target_pairs={{0,1},{1,0},{2,3},{3,2},{4,5},{5,4},{6,7},{7,6},{8,9},{9,8},{10,11... | collective-permute-start | bytes 4128776 | tf_op jit(solution)/shard_map/ppermute | solution.py:949
  108.7 33.5 %collective-permute-start.14 = (bf16[2,4,48,1920]{3,2,1,0:T(8,128)(2,1)}, bf16[2,4,48,1920]{3,2,1,0:T(8,128)(2,1)}, u32[]{:S(2)}, u32[]{:S(2)}) collective-permute-start(bf16[2,4,48,1920]{3,2,1,0:T(8,128)(2,1)} %pad_maximum_fusion.2.refs_0_), channel_id=1, source_target_pairs={{0,4},{2,6},{4,0},{6,2},{8,12},{10,14},{12,8},{14,10},{16,20},{18,... | collective-permute-start | bytes 4423688 | tf_op jit(solution)/shard_map/ppermute | solution.py:925
  110.3 30.0 %collective-permute-start.15 = (bf16[2,4,48,1536]{3,2,1,0:T(8,128)(2,1)S(1)}, bf16[2,4,48,1536]{3,2,1,0:T(8,128)(2,1)}, u32[]{:S(2)}, u32[]{:S(2)}) collective-permute-start(bf16[2,4,48,1536]{3,2,1,0:T(8,128)(2,1)S(1)} %pad_maximum_fusion.3.refs_1_), channel_id=1, source_target_pairs={{0,2},{2,0},{4,6},{6,4},{8,10},{10,8},{12,14},{14,12},{16,18},{18,... | collective-permute-start | bytes 3538952 | tf_op jit(solution)/shard_map/ppermute | solution.py:925
  114.0 24.0 %collective-permute-start.17 = (bf16[48,3072]{1,0:T(8,128)(2,1)S(1)}, bf16[48,3072]{1,0:T(8,128)(2,1)}, u32[]{:S(2)}, u32[]{:S(2)}) collective-permute-start(bf16[48,3072]{1,0:T(8,128)(2,1)S(1)} %constant_dynamic-update-slice_fusion.2.refs_0_), channel_id=1, source_target_pairs={{0,16},{2,18},{4,20},{6,22},{8,24},{10,26},{12,28},{14,30},{16,0},... | collective-permute-start | bytes 884744 | tf_op jit(solution)/shard_map/ppermute | solution.py:929
  114.0 24.0 %collective-permute-start.18 = (bf16[48,3072]{1,0:T(8,128)(2,1)S(1)}, bf16[48,3072]{1,0:T(8,128)(2,1)}, u32[]{:S(2)}, u32[]{:S(2)}) collective-permute-start(bf16[48,3072]{1,0:T(8,128)(2,1)S(1)} %constant_dynamic-update-slice_fusion.2.refs_0_), channel_id=1, source_target_pairs={{0,8},{2,10},{4,12},{6,14},{8,16},{10,18},{12,20},{14,22},{16,24},... | collective-permute-start | bytes 884744 | tf_op jit(solution)/shard_map/ppermute | solution.py:929
  146.3 23.8 %collective-permute-start.19 = (bf16[2,2,4,48,1920]{4,3,2,1,0:T(8,128)(2,1)}, bf16[2,2,4,48,1920]{4,3,2,1,0:T(8,128)(2,1)}, u32[]{:S(2)}, u32[]{:S(2)}) collective-permute-start(bf16[2,2,4,48,1920]{4,3,2,1,0:T(8,128)(2,1)} %get-tuple-element.366), channel_id=1, source_target_pairs={{0,1},{1,0},{2,3},{3,2},{4,5},{5,4},{6,7},{7,6},{8,9},{9,8},{10,11... | collective-permute-start | bytes 8847368 | tf_op jit(solution)/shard_map/ppermute | solution.py:949
  146.4 23.7 %collective-permute-start.20 = (bf16[2,2,4,48,1536]{4,3,2,1,0:T(8,128)(2,1)}, bf16[2,2,4,48,1536]{4,3,2,1,0:T(8,128)(2,1)}, u32[]{:S(2)}, u32[]{:S(2)}) collective-permute-start(bf16[2,2,4,48,1536]{4,3,2,1,0:T(8,128)(2,1)} %get-tuple-element.374), channel_id=1, source_target_pairs={{0,1},{1,0},{2,3},{3,2},{4,5},{5,4},{6,7},{7,6},{8,9},{9,8},{10,11... | collective-permute-start | bytes 7077896 | tf_op jit(solution)/shard_map/ppermute | solution.py:949
  170.2 31.7 %collective-permute-start.23 = (bf16[2,4,48,1536]{3,2,1,0:T(8,128)(2,1)}, bf16[2,4,48,1536]{3,2,1,0:T(8,128)(2,1)}, u32[]{:S(2)}, u32[]{:S(2)}) collective-permute-start(bf16[2,4,48,1536]{3,2,1,0:T(8,128)(2,1)} %pad_maximum_fusion.4.refs_0_), channel_id=1, source_target_pairs={{0,4},{2,6},{4,0},{6,2},{8,12},{10,14},{12,8},{14,10},{16,20},{18,... | collective-permute-start | bytes 3538952 | tf_op jit(solution)/shard_map/ppermute | solution.py:925
  170.7 31.2 %collective-permute-start.24 = (bf16[2,4,48,1536]{3,2,1,0:T(8,128)(2,1)S(1)}, bf16[2,4,48,1536]{3,2,1,0:T(8,128)(2,1)}, u32[]{:S(2)}, u32[]{:S(2)}) collective-permute-start(bf16[2,4,48,1536]{3,2,1,0:T(8,128)(2,1)S(1)} %pad_maximum_fusion.5.refs_1_), channel_id=1, source_target_pairs={{0,2},{2,0},{4,6},{6,4},{8,10},{10,8},{12,14},{14,12},{16,18},{18,... | collective-permute-start | bytes 3538952 | tf_op jit(solution)/shard_map/ppermute | solution.py:925
  171.5 23.9 %collective-permute-start.25 = (bf16[48,3072]{1,0:T(8,128)(2,1)S(1)}, bf16[48,3072]{1,0:T(8,128)(2,1)S(1)}, u32[]{:S(2)}, u32[]{:S(2)}) collective-permute-start(bf16[48,3072]{1,0:T(8,128)(2,1)S(1)} %constant_dynamic-update-slice_fusion.4.refs_0_), channel_id=1, source_target_pairs={{0,24},{2,26},{4,28},{6,30},{8,0},{10,2},{12,4},{14,6},{16,8},{18,... | collective-permute-start | bytes 884744 | tf_op jit(solution)/shard_map/ppermute | solution.py:929
  173.6 24.5 %collective-permute-start.26 = (bf16[48,3072]{1,0:T(8,128)(2,1)S(1)}, bf16[48,3072]{1,0:T(8,128)(2,1)S(1)}, u32[]{:S(2)}, u32[]{:S(2)}) collective-permute-start(bf16[48,3072]{1,0:T(8,128)(2,1)S(1)} %constant_dynamic-update-slice_fusion.4.refs_0_), channel_id=1, source_target_pairs={{0,16},{2,18},{4,20},{6,22},{8,24},{10,26},{12,28},{14,30},{16,0},... | collective-permute-start | bytes 884744 | tf_op jit(solution)/shard_map/ppermute | solution.py:929
  173.6 24.5 %collective-permute-start.27 = (bf16[48,3072]{1,0:T(8,128)(2,1)S(1)}, bf16[48,3072]{1,0:T(8,128)(2,1)S(1)}, u32[]{:S(2)}, u32[]{:S(2)}) collective-permute-start(bf16[48,3072]{1,0:T(8,128)(2,1)S(1)} %constant_dynamic-update-slice_fusion.4.refs_0_), channel_id=1, source_target_pairs={{0,8},{2,10},{4,12},{6,14},{8,16},{10,18},{12,20},{14,22},{16,24},... | collective-permute-start | bytes 884744 | tf_op jit(solution)/shard_map/ppermute | solution.py:929
  223.0 26.9 %collective-permute-start.32 = (bf16[2,4,48,1536]{3,2,1,0:T(8,128)(2,1)S(1)}, bf16[2,4,48,1536]{3,2,1,0:T(8,128)(2,1)S(1)}, u32[]{:S(2)}, u32[]{:S(2)}) collective-permute-start(bf16[2,4,48,1536]{3,2,1,0:T(8,128)(2,1)S(1)} %pad_maximum_fusion.6.refs_0_), channel_id=1, source_target_pairs={{0,4},{2,6},{4,0},{6,2},{8,12},{10,14},{12,8},{14,10},{16,20},{18,... | collective-permute-start | bytes 3538952 | tf_op jit(solution)/shard_map/ppermute | solution.py:925
  223.6 26.7 %collective-permute-start.33 = (bf16[2,4,48,1536]{3,2,1,0:T(8,128)(2,1)S(1)}, bf16[2,4,48,1536]{3,2,1,0:T(8,128)(2,1)S(1)}, u32[]{:S(2)}, u32[]{:S(2)}) collective-permute-start(bf16[2,4,48,1536]{3,2,1,0:T(8,128)(2,1)S(1)} %pad_maximum_fusion.7.refs_1_), channel_id=1, source_target_pairs={{0,2},{2,0},{4,6},{6,4},{8,10},{10,8},{12,14},{14,12},{16,18},{18,... | collective-permute-start | bytes 3538952 | tf_op jit(solution)/shard_map/ppermute | solution.py:925
  327.7 23.6 %collective-permute-start.37 = (bf16[2,4,24,1536]{3,2,1,0:T(8,128)(2,1)}, bf16[2,4,24,1536]{3,2,1,0:T(8,128)(2,1)S(1)}, u32[]{:S(2)}, u32[]{:S(2)}) collective-permute-start(bf16[2,4,24,1536]{3,2,1,0:T(8,128)(2,1)} %get-tuple-element.454), channel_id=1, source_target_pairs={{0,2},{2,0},{4,6},{6,4},{8,10},{10,8},{12,14},{14,12},{16,18},{18,... | collective-permute-start | bytes 1769480 | tf_op jit(solution)/shard_map/ppermute | solution.py:925
  329.2 22.1 %collective-permute-start.38 = (bf16[2,4,24,1536]{3,2,1,0:T(8,128)(2,1)}, bf16[2,4,24,1536]{3,2,1,0:T(8,128)(2,1)S(1)}, u32[]{:S(2)}, u32[]{:S(2)}) collective-permute-start(bf16[2,4,24,1536]{3,2,1,0:T(8,128)(2,1)} %get-tuple-element.455), channel_id=1, source_target_pairs={{0,4},{2,6},{4,0},{6,2},{8,12},{10,14},{12,8},{14,10},{16,20},{18,... | collective-permute-start | bytes 1769480 | tf_op jit(solution)/shard_map/ppermute | solution.py:925
  373.1 26.6 %collective-permute-start.45 = (bf16[2,4,48,1536]{3,2,1,0:T(8,128)(2,1)}, bf16[2,4,48,1536]{3,2,1,0:T(8,128)(2,1)}, u32[]{:S(2)}, u32[]{:S(2)}) collective-permute-start(bf16[2,4,48,1536]{3,2,1,0:T(8,128)(2,1)} %get-tuple-element.481), channel_id=1, source_target_pairs={{0,2},{2,0},{4,6},{6,4},{8,10},{10,8},{12,14},{14,12},{16,18},{18,... | collective-permute-start | bytes 3538952 | tf_op jit(solution)/shard_map/ppermute | solution.py:925
  373.7 26.3 %collective-permute-start.46 = (bf16[2,4,48,1536]{3,2,1,0:T(8,128)(2,1)}, bf16[2,4,48,1536]{3,2,1,0:T(8,128)(2,1)}, u32[]{:S(2)}, u32[]{:S(2)}) collective-permute-start(bf16[2,4,48,1536]{3,2,1,0:T(8,128)(2,1)} %get-tuple-element.482), channel_id=1, source_target_pairs={{0,4},{2,6},{4,0},{6,2},{8,12},{10,14},{12,8},{14,10},{16,20},{18,... | collective-permute-start | bytes 3538952 | tf_op jit(solution)/shard_map/ppermute | solution.py:925
  374.4 25.3 %collective-permute-start.42 = (bf16[24,3072]{1,0:T(8,128)(2,1)}, bf16[24,3072]{1,0:T(8,128)(2,1)}, u32[]{:S(2)}, u32[]{:S(2)}) collective-permute-start(bf16[24,3072]{1,0:T(8,128)(2,1)} %get-tuple-element.478), channel_id=1, source_target_pairs={{0,8},{2,10},{4,12},{6,14},{8,16},{10,18},{12,20},{14,22},{16,24},... | collective-permute-start | bytes 442376 | tf_op jit(solution)/shard_map/ppermute | solution.py:929
  374.7 25.1 %collective-permute-start.43 = (bf16[24,3072]{1,0:T(8,128)(2,1)}, bf16[24,3072]{1,0:T(8,128)(2,1)}, u32[]{:S(2)}, u32[]{:S(2)}) collective-permute-start(bf16[24,3072]{1,0:T(8,128)(2,1)} %get-tuple-element.479), channel_id=1, source_target_pairs={{0,16},{2,18},{4,20},{6,22},{8,24},{10,26},{12,28},{14,30},{16,0},... | collective-permute-start | bytes 442376 | tf_op jit(solution)/shard_map/ppermute | solution.py:929
  376.2 23.5 %collective-permute-start.44 = (bf16[24,3072]{1,0:T(8,128)(2,1)}, bf16[24,3072]{1,0:T(8,128)(2,1)}, u32[]{:S(2)}, u32[]{:S(2)}) collective-permute-start(bf16[24,3072]{1,0:T(8,128)(2,1)} %get-tuple-element.480), channel_id=1, source_target_pairs={{0,24},{2,26},{4,28},{6,30},{8,0},{10,2},{12,4},{14,6},{16,8},{18,... | collective-permute-start | bytes 442376 | tf_op jit(solution)/shard_map/ppermute | solution.py:929
  404.0 21.5 %collective-permute-start.47 = (bf16[4,48,1536]{2,1,0:T(8,128)(2,1)}, bf16[4,48,1536]{2,1,0:T(8,128)(2,1)S(1)}, u32[]{:S(2)}, u32[]{:S(2)}) collective-permute-start(bf16[4,48,1536]{2,1,0:T(8,128)(2,1)} %get-tuple-element.496), channel_id=1, source_target_pairs={{0,4},{2,6},{4,0},{6,2},{8,12},{10,14},{12,8},{14,10},{16,20},{18,... | collective-permute-start | bytes 1769480 | tf_op jit(solution)/shard_map/ppermute | solution.py:925
  438.7 24.9 %collective-permute-start.53 = (bf16[2,4,48,1152]{3,2,1,0:T(8,128)(2,1)}, bf16[2,4,48,1152]{3,2,1,0:T(8,128)(2,1)S(1)}, u32[]{:S(2)}, u32[]{:S(2)}) collective-permute-start(bf16[2,4,48,1152]{3,2,1,0:T(8,128)(2,1)} %get-tuple-element.513), channel_id=1, source_target_pairs={{0,2},{2,0},{4,6},{6,4},{8,10},{10,8},{12,14},{14,12},{16,18},{18,... | collective-permute-start | bytes 2654216 | tf_op jit(solution)/shard_map/ppermute | solution.py:925
  439.3 24.3 %collective-permute-start.54 = (bf16[2,4,48,896]{3,2,1,0:T(8,128)(2,1)}, bf16[2,4,48,896]{3,2,1,0:T(8,128)(2,1)S(1)}, u32[]{:S(2)}, u32[]{:S(2)}) collective-permute-start(bf16[2,4,48,896]{3,2,1,0:T(8,128)(2,1)} %get-tuple-element.514), channel_id=1, source_target_pairs={{0,4},{2,6},{4,0},{6,2},{8,12},{10,14},{12,8},{14,10},{16,20},{18,... | collective-permute-start | bytes 2064392 | tf_op jit(solution)/shard_map/ppermute | solution.py:925
  440.5 23.1 %collective-permute-start.51 = (bf16[48,3072]{1,0:T(8,128)(2,1)}, bf16[48,3072]{1,0:T(8,128)(2,1)S(1)}, u32[]{:S(2)}, u32[]{:S(2)}) collective-permute-start(bf16[48,3072]{1,0:T(8,128)(2,1)} %get-tuple-element.511), channel_id=1, source_target_pairs={{0,16},{2,18},{4,20},{6,22},{8,24},{10,26},{12,28},{14,30},{16,0},... | collective-permute-start | bytes 884744 | tf_op jit(solution)/shard_map/ppermute | solution.py:929
  442.0 21.5 %collective-permute-start.52 = (bf16[48,3072]{1,0:T(8,128)(2,1)}, bf16[48,3072]{1,0:T(8,128)(2,1)S(1)}, u32[]{:S(2)}, u32[]{:S(2)}) collective-permute-start(bf16[48,3072]{1,0:T(8,128)(2,1)} %get-tuple-element.512), channel_id=1, source_target_pairs={{0,24},{2,26},{4,28},{6,30},{8,0},{10,2},{12,4},{14,6},{16,8},{18,... | collective-permute-start | bytes 884744 | tf_op jit(solution)/shard_map/ppermute | solution.py:929
  495.3 33.8 %collective-permute-start.67 = (f32[48,384]{1,0:T(8,128)S(1)}, f32[48,384]{1,0:T(8,128)S(1)}, u32[]{:S(2)}, u32[]{:S(2)}) collective-permute-start(f32[48,384]{1,0:T(8,128)S(1)} %pad_maximum_fusion.11), channel_id=1, source_target_pairs={{0,1},{1,0},{2,3},{3,2},{4,5},{5,4},{6,7},{7,6},{8,9},{9,8},{10,11... | collective-permute-start | bytes 221192 | tf_op jit(solution)/shard_map/ppermute | solution.py:949
  (154 other events, 1332.9 us)

commit v3 on v2

--- a/solution.py
+++ b/solution.py
@@ -249,71 +249,107 @@
     sums_ref[at + 1 : at + 2, :] = shifts
 
 
-def ff_back_kernel(need, ship, *refs):
-    (d_inward, bridge_in, hidden, middle, normed, order, gains) = refs[0:7]
-    acts, slopes, ups, downs = refs[7:9], refs[9:11], refs[11:13], refs[13:15]
-    grads, branch_out, d_middle, sums = refs[15:17], refs[17], refs[18], refs[19]
-    grad, d_hidden, branch, branch_t, normed_t, d_pre = refs[20:26]
-    ff = acts[0].shape[1]
-    wide = 768
+def ff_side(branch, branch_t, normed_t, act, slope, down, d_pre, out):
+    ff = act.shape[1]
+
+    def body(span):
+        d_act = mm(branch[...], down[:, span])
+        values = (d_act * slope[:, span].astype(WIDE)).astype(LOW)
+        d_pre[:, span] = values
+        out[:, span] = mm(normed_t[...], values).astype(LOW)
+        lower = pl.ds(pl.multiple_of(span.start + ff, LANES), span.size)
+        out[:, lower] = mm(branch_t[...], act[:, span]).astype(LOW)
+
+    tiles(ff, 768, body)
+
+
+def ff_back_first_kernel(need, ship, *refs):
+    d_inward, bridge_in, hidden, normed, eye, gains, act, slope, down = refs[0:9]
+    out, d_hidden, branch, branch_t, normed_t, d_pre, sums, grad = refs[9:17]
 
     def first(span):
         grad[:, span] = mm_t(d_inward[...], bridge_in[span, :])
 
-    tiles(D, wide, first)
-
-    def write_hidden(span, values):
+    tiles(D, 256, first)
+
+    def write(span, values):
         d_hidden[span, :] = values
         branch[span, :] = values.astype(LOW)
 
-    norm_back_rows(hidden, grad, gains[4:5, :], write_hidden, sums, 0)
-    need(5, 4)
-    branch_t[...] = mm_t(order[...], branch[...]).astype(LOW)
-    normed_t[...] = mm_t(order[...], normed[...]).astype(LOW)
-    for side in (0, 1):
-        need(7 + side, 9 + side, 13 + side)
-        act, slope, down = acts[side], slopes[side], downs[side]
-        out = grads[side]
-
-        def second(span, act=act, slope=slope, down=down, out=out, side=side):
-            d_act = mm(branch[...], down[:, span])
-            values = (d_act * slope[:, span].astype(WIDE)).astype(LOW)
-            d_pre[side, :, span] = values
-            out[:, span] = mm(normed_t[...], values).astype(LOW)
-            lower = pl.ds(pl.multiple_of(span.start + ff, LANES), span.size)
-            out[:, lower] = mm(branch_t[...], act[:, span]).astype(LOW)
-
-        tiles(ff, wide, second)
-        ship(side)
-
-    need(11, 12)
+    norm_back_rows(hidden, grad, gains[4:5, :], write, sums, 0)
+    ship(1, 2)
+    need(4, 3)
+    branch_t[...] = mm_t(eye[...], branch[...]).astype(LOW)
+    normed_t[...] = mm_t(eye[...], normed[...]).astype(LOW)
+    ship(3, 4)
+    need(8, 7, 6)
+    ff_side(branch, branch_t, normed_t, act, slope, down, d_pre, out)
+
+
+def ff_back_first(d_inward, bridge_in, hidden, normed, eye, gains, act, slope, down):
+    rows, ff = act.shape
+    return on_chip(
+        ff_back_first_kernel,
+        [d_inward, bridge_in, hidden, normed, eye, gains, act, slope, down],
+        [((D, 2 * ff), LOW), ((rows, D), WIDE), ((rows, D), LOW)]
+        + [((D, rows), LOW)] * 2
+        + [((rows, ff), LOW), ((8, D), WIDE)],
+        [((rows, D), WIDE)],
+        4 * rows * D * ff,
+        late=(4, 3, 8, 7, 6),
+        early=(1, 2, 3, 4, 0, 5),
+    )
+
+
+def ff_back_second_kernel(need, ship, *refs):
+    d_hidden, branch, branch_t, normed_t, d_pre_other, middle, gains = refs[0:7]
+    act, slope, down, up_own, up_other, sums_first = refs[7:13]
+    out, branch_out, d_middle, sums, grad, d_pre = refs[13:19]
+    need(9, 8, 7)
+    ff_side(branch, branch_t, normed_t, act, slope, down, d_pre, out)
+    ship(0)
+    need(10, 4, 11)
 
     def third(span):
-        grad[:, span] = mm_t(d_pre[0], ups[0][span, :]) + mm_t(d_pre[1], ups[1][span, :])
-
-    tiles(D, wide, third)
-
-    def write_middle(span, values):
+        grad[:, span] = mm_t(d_pre[...], up_own[span, :]) + mm_t(d_pre_other[...], up_other[span, :])
+
+    tiles(D, 768, third)
+    need(5, 0)
+
+    def write(span, values):
         values = values + d_hidden[span, :]
         d_middle[span, :] = values
         branch_out[span, :] = values.astype(LOW)
 
-    need(3)
-    norm_back_rows(middle, grad, gains[2:3, :], write_middle, sums, 2)
-
-
-def ff_back(d_inward, bridge_in, hidden, middle, normed, order, gains, acts, slopes, ups, downs):
-    rows, ff = acts[0].shape
+    norm_back_rows(middle, grad, gains[2:3, :], write, sums, 2)
+    sums[0:2, :] = sums_first[0:2, :]
+
+
+def ff_back_second(
+    d_hidden,
+    branch,
+    branch_t,
+    normed_t,
+    d_pre,
+    middle,
+    gains,
+    act,
+    slope,
+    down,
+    up_own,
+    up_other,
+    sums,
+):
+    rows, ff = act.shape
     return on_chip(
-        ff_back_kernel,
-        [d_inward, bridge_in, hidden, middle, normed, order, gains]
-        + [*acts, *slopes, *ups, *downs],
-        [((D, 2 * ff), LOW)] * 2 + [((rows, D), LOW), ((rows, D), WIDE), ((8, D), WIDE)],
-        [((rows, D), WIDE)] * 2
-        + [((rows, D), LOW), ((D, rows), LOW), ((D, rows), LOW), ((2, rows, ff), LOW)],
-        8 * rows * D * ff,
-        late=(5, 4, 13, 9, 7, 14, 10, 8, 11, 12, 3),
-        early=(0, 1),
+        ff_back_second_kernel,
+        [d_hidden, branch, branch_t, normed_t, d_pre, middle, gains, act, slope, down]
+        + [up_own, up_other, sums],
+        [((D, 2 * ff), LOW), ((rows, D), LOW), ((rows, D), WIDE), ((8, D), WIDE)],
+        [((rows, D), WIDE), ((rows, ff), LOW)],
+        5 * rows * D * ff,
+        late=(9, 8, 7, 10, 4, 11, 5, 0),
+        early=(0,),
     )
 
 
@@ -718,38 +754,36 @@
     )
 
 
-def target_ff_kernel(need, ship, t_two, t_middle, gains, *refs):
-    ups, downs, (target, pre, act, total) = refs[0:2], refs[2:4], refs[4:8]
-    total[...] = t_middle[...]
-    for side in (0, 1):
-        up, down = ups[side], downs[side]
-        need(3 + side)
-
-        def first(span, up=up):
-            pre[...] = mm(t_two[...], up[:, span])
-            gelu_rows(pre, act, None, span)
-
-        tiles(act.shape[1], 512, first)
-        need(5 + side)
-        total[...] = total[...] + mm_t(act[...], down[...])
-    chosen = norm_rows(total[...], gains[4:5, :], gains[5:6, :])
-    target[...] = norm_rows(chosen, 1.0, 0.0)
-
-
-def target_ff(t_two, t_middle, gains, ups, downs):
-    rows, ff = t_two.shape[0], ups[0].shape[1]
+def target_ff_kernel(last, need, ship, t_two, start, gains, up, down, target, pre, act):
+    need(3)
+
+    def first(span):
+        pre[...] = mm(t_two[...], up[:, span])
+        gelu_rows(pre, act, None, span)
+
+    tiles(act.shape[1], 512, first)
+    need(4)
+    total = start[...] + mm_t(act[...], down[...])
+    if last:
+        total = norm_rows(total, gains[4:5, :], gains[5:6, :])
+        total = norm_rows(total, 1.0, 0.0)
+    target[...] = total
+
+
+def target_ff(last, t_two, start, gains, up, down):
+    rows, ff = t_two.shape[0], up.shape[1]
     return on_chip(
-        target_ff_kernel,
-        [t_two, t_middle, gains, *ups, *downs],
+        functools.partial(target_ff_kernel, last),
+        [t_two, start, gains, up, down],
         [((rows, D), WIDE)],
-        [((rows, 512), WIDE), ((rows, ff), LOW), ((rows, D), WIDE)],
-        rows * D * ff * 4,
-        rows * ff * 2,
-        late=(3, 5, 4, 6),
+        [((rows, 512), WIDE), ((rows, ff), LOW)],
+        rows * D * ff * 2,
+        rows * ff,
+        late=(3, 4),
     )[0]
 
 
-def pred_back_all_kernel(size, count_all, *refs):
+def pred_back_all_kernel(size, count_all, dp_count, *refs):
     (guess, target, used, context, final, bridge_in, bridge_out, gains, ids_row, ids_col) = refs[
         0:10
     ]
@@ -763,9 +797,17 @@
         refs[31:33],
     )
     logs = refs[33]
-    loss, d_inward, g_bridge_in, g_bridge_out, sums = refs[34:39]
-    g_left, g_right = refs[39:41], refs[41:43]
-    d_qk, d_v, d_normed, bias, soft, d_scores = refs[43:49]
+    p_order, side_ref, loss, d_inward, sums = refs[34:39]
+    packs = refs[39:41]
+    d_qk, d_v, d_normed, bias, soft, d_scores, g_bridge_out = refs[41:48]
+    p_rows = PW // dp_count
+    half = packs[0].shape[2] // 2
+
+    def put(side, column, values):
+        for block in range(dp_count):
+            part = values[block * p_rows : (block + 1) * p_rows]
+            packs[side][block, :, column : column + values.shape[1]] = part.astype(LOW)
+
     width = in_v[0].shape[1]
     ff = acts[0].shape[1]
     diff = guess[...] - target[...]
@@ -789,8 +831,8 @@
     total = None
     for side in (0, 1):
         d_pre = (mm(branch, downs[side][...]) * slopes[side][...].astype(WIDE)).astype(LOW)
-        g_left[side][:, 0:ff] = t_mm(branch, acts[side][...]).astype(LOW)
-        g_right[side][:, 0:ff] = t_mm(normed_two[...], d_pre).astype(LOW)
+        put(side, 0, t_mm(branch, acts[side][...]))
+        put(side, half, t_mm(normed_two[...], d_pre))
         part = mm_t(d_pre, ups[side][...])
         total = part if total is None else total + part
     d_middle = d_tail + back(middle[...], gains[2:3, :], total, 2)
@@ -801,7 +843,7 @@
     for side in (0, 1):
         qk_ref, v_ref, right = in_qk[side], in_v[side], rights[side]
         d_mixed = mm(branch, right[:, width:]).astype(LOW)
-        g_right[side][:, ff + width :] = t_mm(branch, mixeds[side][...]).astype(LOW)
+        put(side, half + ff + width, t_mm(branch, mixeds[side][...]))
         found = []
         for low in range(0, width, size):
             found.append(
@@ -824,29 +866,39 @@
         d_qk[CTX:, 0:width] = d_query
         d_qk[:, width:] = d_keys
         d_v[...] = d_values
-        g_left[side][:, ff:] = t_mm(normed[...], d_qk[...]).astype(LOW)
-        g_right[side][:, ff : ff + width] = t_mm(normed[...], d_v[...]).astype(LOW)
+        put(side, ff, t_mm(normed[...], d_qk[...]))
+        put(side, half + ff, t_mm(normed[...], d_v[...]))
         part = mm_t(d_qk[...], qks[side][...]) + mm_t(d_v[...], right[:, 0:width])
         d_normed[...] = part if side == 0 else d_normed[...] + part
     d_joined = back(joined[...], gains[0:1, :], d_normed[...], 0)
     sums[6:7, :] = jnp.sum(d_joined[CTX:] + d_middle, 0, keepdims=True)
     sums[7:8, :] = jnp.zeros((1, PW), WIDE)
     d_inward[...] = d_joined[0:CTX].astype(LOW)
-    g_bridge_in[...] = t_mm(context[...], d_inward[...]).astype(LOW)
-
-
-def pred_back_all(size, count_all, used, values, pairs, logs, idq, idk):
+    g_in = mm_t(t_mm(context[...], d_inward[...]).astype(LOW), p_order[...])
+    g_out = mm_t(g_bridge_out[...], p_order[...])
+    flip = side_ref[0] != 0
+    at = ff + 2 * width
+    for side, values in ((0, jnp.where(flip, g_out, g_in)), (1, jnp.where(flip, g_in, g_out))):
+        for block in range(dp_count):
+            for low in (0, 1):
+                start = (2 * block + low) * p_rows
+                packs[side][block, :, low * half + at : (low + 1) * half] = values[
+                    start : start + p_rows
+                ].astype(LOW)
+
+
+def pred_back_all(size, count_all, dp_count, side, order, used, values, pairs, logs, idq, idk):
     (guess, target, context, final, bridge_in, bridge_out, gains) = values[:7]
     ff, width, count = pairs[0][0].shape[1], pairs[2][0].shape[1] // 2, idk.shape[0]
     ins = [guess, target, used, context, final, bridge_in, bridge_out, gains]
     ins += [idq[None, :], idk[:, None], *values[7:]] + [part for pair in pairs for part in pair]
-    ins.append(logs)
-    outs = [((1, 1), WIDE), ((CTX, PW), LOW), ((D, PW), LOW), ((D, PW), LOW), ((8, PW), WIDE)]
-    outs += [((PW, ff + 2 * width), LOW)] * 4
+    ins += [logs, order, side]
+    outs = [((1, 1), WIDE), ((CTX, PW), LOW), ((8, PW), WIDE)]
+    outs += [((dp_count, PW // dp_count, 2 * (ff + 2 * width) + D), LOW)] * 2
     specs = [WHOLE] * len(ins)
-    specs[2] = pl.BlockSpec(memory_space=pltpu.SMEM)
+    specs[2] = specs[-1] = pl.BlockSpec(memory_space=pltpu.SMEM)
     return pl.pallas_call(
-        functools.partial(pred_back_all_kernel, size, count_all),
+        functools.partial(pred_back_all_kernel, size, count_all, dp_count),
         in_specs=specs,
         out_specs=[WHOLE] * len(outs),
         out_shape=[jax.ShapeDtypeStruct(shape, kind) for shape, kind in outs],
@@ -857,6 +909,7 @@
             pltpu.VMEM((count, idq.shape[0]), WIDE),
             pltpu.VMEM((count, idq.shape[0]), LOW),
             pltpu.VMEM((count, idq.shape[0]), LOW),
+            pltpu.VMEM((D, PW), LOW),
         ],
         cost_estimate=pl.CostEstimate(
             flops=4_000_000_000, bytes_accessed=20_000_000, transcendentals=3_000_000
@@ -1162,12 +1215,15 @@
             found += [term[0] for term in part.terms]
         return found
 
-    def swap(self):
+    def swap(self, got=None):
         if self.plain:
             return
         mine = Box(self.shaped(self.own.value))
         mine.held = True
-        got = Box(self.shaped(swap(self.other.value)))
+        if got is None:
+            got = swap(self.other.value)
+        self.other.held = True
+        got = Box(self.shaped(got))
         for part in self.parts:
             blank = (None,) * len(self.lead)
             part.terms = [(mine, blank, part.cols), (got, blank, part.cols)]
@@ -1206,7 +1262,7 @@
         return results + [jnp.pad(squares.reshape(1, 1), ((0, 0), (0, LANES - 1)))]
 
 
-def move(*steps):
+def move(*steps, hold=None):
     work = []
     for total, kind in steps:
         if total.plain:
@@ -1217,13 +1273,16 @@
             for part in total.parts:
                 work.append((part.near_send, [[part.near_job(kind)]]))
     if not work:
-        return
+        return hold
     sends = sum_parts([job for send, jobs in work for job in jobs], LOW)
+    if hold is not None:
+        sends, hold = lax.optimization_barrier((sends, hold))
     at = 0
     for send, jobs in work:
         found = sends[at : at + len(jobs)]
         at += len(jobs)
         send(found if len(jobs) > 1 else found[0])
+    return hold
 
 
 def fence_sums(sums, *values):
@@ -1251,7 +1310,8 @@
 def adam_kernel(plan, scalars, side, *refs):
     count = len(plan)
     grads = refs[3 * count : -3 * count]
-    factor = jnp.minimum(1.0, CLIP_NORM / (jnp.sqrt(scalars[0]) + 1e-06))
+    total = jnp.sum(scalars[0:1, :], 1, keepdims=True)
+    factor = jnp.minimum(1.0, CLIP_NORM / (jnp.sqrt(total) + 1e-06))
     for at, (rate, decay, pieces) in enumerate(plan):
         ins = refs[3 * at : 3 * at + 3]
         outs = refs[len(refs) - 3 * count + 3 * at :][:3]
@@ -1274,7 +1334,7 @@
     ins = [value for group in groups for value in group] + list(grads)
     found = pl.pallas_call(
         functools.partial(adam_kernel, plan),
-        in_specs=[scalar, scalar] + [WHOLE] * len(ins),
+        in_specs=[WHOLE, scalar] + [WHOLE] * len(ins),
         out_specs=[WHOLE] * len(outs),
         out_shape=outs,
         cost_estimate=pl.CostEstimate(
@@ -1531,8 +1591,6 @@
         normed_two, middle, enc_gain, enc_up, enc_down
     )
     activated, slope = pairs[:2], pairs[2:]
-    held_d, hidden, context, activated, slope = fence(held_d, hidden, context, activated, slope)
-    other_d = swap_all(held_d)
     (
         joined,
         p_normed_one,
@@ -1560,24 +1618,22 @@
         pairs[at : at + 2] for at in range(0, 10, 2)
     ]
     p_logs = pairs[10]
-    other_d, guess = fence(other_d, guess)
-    target = target_ff(
-        t_two,
-        t_middle,
-        target_gain,
-        (flat(held_d[0]), flat(other_d[0])),
-        (flat(held_d[1]), flat(other_d[1])),
-    )
+    held_d, guess, t_middle = fence(held_d, guess, t_middle)
+    other_d = swap_all(held_d)
+    target = target_ff(False, t_two, t_middle, target_gain, *[flat(part) for part in held_d])
+    target, other_d = fence(target, other_d)
+    target = target_ff(True, t_two, target, target_gain, *[flat(part) for part in other_d])
     (
         loss_local,
         d_inward,
-        grad_bridge_in,
-        grad_bridge_out,
         sums_pred,
-        *pairs,
+        *pair_p,
     ) = pred_back_all(
         p_size,
         count,
+        dp_count,
+        side[None].astype(jnp.int32),
+        p_order,
         used[None],
         [
             guess,
@@ -1608,57 +1664,43 @@
         tgt_id,
         joined_id,
     )
-    grads_left, grads_right = pairs[:2], pairs[2:]
-
-    def blocks(values):
-        return values.reshape(dp_count, p_rows, -1)
-
-    bridge_pair = [
-        mm_t(jnp.where(first, low, high), p_order).astype(LOW).reshape(dp_count, rows, -1)
-        for low, high in (
-            (grad_bridge_in, grad_bridge_out),
-            (grad_bridge_out, grad_bridge_in),
-        )
-    ]
-    pair_p = [
-        jnp.concatenate(
-            [
-                blocks(grads_left[at]),
-                bridge_pair[at][:, :p_rows],
-                blocks(grads_right[at]),
-                bridge_pair[at][:, p_rows:],
-            ],
-            2,
-        )
-        for at in (0, 1)
-    ]
     sum_p = Sums(lines, *pair_p, 4 * local, p_rows)
     (d_inward,) = fence_sums([sum_p], d_inward)
     sum_p.swap()
     (d_inward,) = fence_sums([sum_p], d_inward)
-    move((sum_p, 0))
-    grads_own, grads_other, branch, d_middle, sums_ff = ff_back(
+    d_inward = move((sum_p, 0), hold=d_inward)
+    grads_other, *parts, sums_ff = ff_back_first(
         d_inward,
         bridge_in,
         hidden,
-        middle,
         normed_two,
         eye,
         enc_gain,
-        activated,
-        slope,
-        enc_up,
-        enc_down,
+        activated[1],
+        slope[1],
+        enc_down[1],
+    )
+    grads_other, parts = fence_sums([sum_p], grads_other, parts)
+    grads_got = swap(grads_other)
+    parts = move((sum_p, 1), hold=parts)
+    grads_own, branch, d_middle, sums_ff = ff_back_second(
+        *parts,
+        middle,
+        enc_gain,
+        activated[0],
+        slope[0],
+        enc_down[0],
+        enc_up[0],
+        enc_up[1],
+        sums_ff,
     )
     sum_f = Sums(lines, grads_own, grads_other, ff, rows)
+    sum_f.swap(grads_got)
     branch, d_middle = fence_sums([sum_p, sum_f], branch, d_middle)
-    sum_f.swap()
-    move((sum_p, 1))
-    branch, d_middle = fence_sums([sum_p, sum_f], branch, d_middle)
-    move((sum_f, 0), (sum_p, 2))
+    d_middle, branch = move((sum_f, 0), (sum_p, 2), hold=(d_middle, branch))
     d_proj = attn_back(size, branch, ctx_id, enc_rest, projected, mixed, logs)
     (d_proj,) = fence_sums([sum_p, sum_f], d_proj)
-    move((sum_f, 1))
+    d_proj = move((sum_f, 1), hold=d_proj)
     grads_own, grads_other = qkv_back(
         branch,
         d_middle,
@@ -1689,8 +1731,9 @@
     bridge_other = swap(jnp.concatenate([red_left[:, low_one:], red_right[:, low_one:]], 0))
     embed_other = swap(red_rest[:, :local])
     gains_t = red_rest[:, 2 * local :].T
-    sums = jnp.concatenate([squares_p + squares_f + squares_a, loss_local], 1)
-    sums = jnp.stack([jnp.sum(sums[:, :LANES]), sums[0, LANES]])
+    sums = jnp.concatenate(
+        [squares_p + squares_f + squares_a, jnp.pad(loss_local, ((0, 0), (0, LANES - 1)))], 0
+    )
     for step in range(0, dp_count.bit_length(), 2):
         sums = lines.add_all(sums, step, min(step + 2, dp_count.bit_length()))
     groups = [
@@ -1769,7 +1812,7 @@
     results = adam_all(sums, side[None].astype(jnp.int32), groups, grads, plan)
     for at in (3, 6):
         results[at] = [value.T for value in results[at]]
-    return (*[value for result in results for value in result], sums[1], jnp.sqrt(sums[0]))
+    return (*[value for result in results for value in result], sums[1, 0], jnp.sqrt(jnp.sum(sums[0])))
 
 
 def solution(mesh):

time: 547 us -> 537 us (0.982)
  waiting for transfers between devices: 116 us -> 90.1 us
  starting transfers between devices: 80 us -> 97.3 us
  Pallas kernels: 243 us -> 256 us
  other arithmetic: 32.5 us -> 24.5 us
    ppermute x21, starting transfers between devices: 35.5 us -> 53.7 us  [shift(): return lax.ppermute(values, 'dp', pairs)]
    ppermute x28, waiting for transfers between devices: 58.9 us -> 46.5 us  [flip(): return lax.ppermute(values, 'dp', pairs)]
    pallas_call x13 -> x15, Pallas kernels: 158 us -> 170 us  [on_chip(): pl.pallas_call(kernel, in_specs=in_specs, out_specs=out_specs, out_shape=...]
    ppermute x21, waiting for transfers between devices: 41.5 us -> 31.7 us  [shift(): return lax.ppermute(values, 'dp', pairs)]
    unnamed x224 -> x190, local copies, waits for them, and re-layouts: 27.1 us -> 26.5 us
  transfers between devices with their start and end apart: 69 -> 69, of which waited for: 27 -> 22; matrix products, arithmetic and copies ran while one was open for 10% -> 8% of each run, Pallas kernels for 30% -> 33%
where the time goes in v3:
time: 537 us; the launch traced here: 528 us
  Pallas kernels  256 us (48%)
  starting transfers between devices  97.3 us (18%)
  waiting for transfers between devices  90.1 us (17%)
  local copies, waits for them, and re-layouts  44 us (8%)
  other arithmetic  24.5 us (5%)
  matrix products  10.2 us (2%)
    pallas_call x15, Pallas kernels, on_chip(): pl.pallas_call(kernel, in_specs=in_specs, out_specs=out_specs, out_shape=...  170 us
    ppermute x21, starting transfers between devices, shift(): return lax.ppermute(values, 'dp', pairs)  53.7 us
    ppermute x28, waiting for transfers between devices, flip(): return lax.ppermute(values, 'dp', pairs)  46.5 us
    pallas_call x10, Pallas kernels, sum_parts(): pl.pallas_call(functools.partial(sum_kernel, tuple(plan), squares), grid=...  34.6 us
    ppermute x21, waiting for transfers between devices, shift(): return lax.ppermute(values, 'dp', pairs)  31.7 us
    ppermute x28, starting transfers between devices, flip(): return lax.ppermute(values, 'dp', pairs)  29.3 us
    unnamed x190, local copies, waits for them, and re-layouts  26.5 us
    pallas_call x1, Pallas kernels, pred_back_all(): pl.pallas_call(functools.partial(pred_back_all_kernel, size, count_all, d...  25.2 us
  transfers between devices with their start and end apart: 69, of which 22 were waited for; matrix products, arithmetic and copies ran while one was open for 8% of the time, Pallas kernels for 33%

profile of v3, /device:TPU:0, one launch (start us, length us, event | category | flops | bytes accessed | tf_op | source)
XLA Modules:
  0.0 527.6 jit_solution(10186857185064261733)
XLA Ops:
  31.5 6.1 %collective-permute-done.4 = bf16[4,48,896]{2,1,0:T(8,128)(2,1)S(1)} collective-permute-done((bf16[4,48,896]{2,1,0:T(8,128)(2,1)}, bf16[4,48,896]{2,1,0:T(8,128)(2,1)S(1)}, u32[]{:S(2)}, u32[]{:S(2)}) %collective-permute-start.4) | collective-permute-done | bytes 344096 | tf_op jit(solution)/shard_map/ppermute | solution.py:978
  46.7 4.8 collective-permute-start.9
  81.0 14.2 %collective-permute-done.13 = bf16[4,48,1536]{2,1,0:T(8,128)(2,1)S(1)} collective-permute-done((bf16[4,48,1536]{2,1,0:T(8,128)(2,1)S(1)}, bf16[4,48,1536]{2,1,0:T(8,128)(2,1)S(1)}, u32[]{:S(2)}, u32[]{:S(2)}) %collective-permute-start.13) | collective-permute-done | bytes 589856 | tf_op jit(solution)/shard_map/ppermute | solution.py:978
  103.5 6.5 %collective-permute-start.18 = (bf16[48,3072]{1,0:T(8,128)(2,1)S(1)}, bf16[48,3072]{1,0:T(8,128)(2,1)}, u32[]{:S(2)}, u32[]{:S(2)}) collective-permute-start(bf16[48,3072]{1,0:T(8,128)(2,1)S(1)} %constant_dynamic-update-slice_fusion.2.refs_0_), channel_id=1, source_target_pairs={{0,8},{2,10},{4,12},{6,14},{8,16},{10,18},{12,20},{14,22},{16,24},... | collective-permute-start | bytes 884744 | tf_op jit(solution)/shard_map/ppermute | solution.py:982
  113.9 11.1 %shard_map.517 = (f32[512,768]{1,0:T(8,128)}, bf16[512,768]{1,0:T(8,128)(2,1)}, bf16[512,1152]{1,0:T(8,128)(2,1)}, bf16[512,1152]{1,0:T(8,128)(2,1)}, f32[8,768]...) custom-call(bf16[512,768]{1,0:T(8,128)(2,1)} %fusion.6.refs_0_.refs_4_, f32[512,768]{1,0:T(8,128)} %fusion.100.refs_1_, ...), custom_call_target="tpu_custom_call" | custom-call | flops 3321888768 | bytes 15200256 | tf_op jit(solution)/shard_map/pallas_call | solution.py:204
  125.1 6.2 %collective-permute-done.17.refs_2_ = bf16[48,3072]{1,0:T(8,128)(2,1)} collective-permute-done((bf16[48,3072]{1,0:T(8,128)(2,1)S(1)}, bf16[48,3072]{1,0:T(8,128)(2,1)}, u32[]{:S(2)}, u32[]{:S(2)}) %collective-permute-start.17) | collective-permute-done | bytes 294944 | tf_op jit(solution)/shard_map/ppermute | solution.py:982
  134.8 4.1 shard_map.515
  142.4 14.9 %shard_map.518 = (f32[512,768]{1,0:T(8,128)}, bf16[512,768]{1,0:T(8,128)(2,1)}, bf16[512,384]{1,0:T(8,128)(2,1)}, bf16[512,384]{1,0:T(8,128)(2,1)}, f32[2,8,512]{2,1,0:T(8,128)}, /*index=5*/f32[2,8,512]{2,1,0:T(8,128)}) custom-call(f32[512,768]{1,0:T(8,128)} %get-tuple-element.363.refs_0_.refs_2_, ...), custom_call_target="tpu_custom_call" | custom-call | flops 1409286144 | bytes 9924608 | tf_op jit(solution)/shard_map/pallas_call | solution.py:204
  164.1 5.6 %collective-permute-start.27 = (bf16[48,3072]{1,0:T(8,128)(2,1)S(1)}, bf16[48,3072]{1,0:T(8,128)(2,1)S(1)}, u32[]{:S(2)}, u32[]{:S(2)}) collective-permute-start(bf16[48,3072]{1,0:T(8,128)(2,1)S(1)} %constant_dynamic-update-slice_fusion.4.refs_0_), channel_id=1, source_target_pairs={{0,8},{2,10},{4,12},{6,14},{8,16},{10,18},{12,20},{14,22},{16,24},... | collective-permute-start | bytes 884744 | tf_op jit(solution)/shard_map/ppermute | solution.py:982
  173.1 19.4 %shard_map.521 = (f32[256,768]{1,0:T(8,128)S(1)}, bf16[256,768]{1,0:T(8,128)(2,1)S(1)}) custom-call(bf16[784,768]{1,0:T(8,128)(2,1)S(1)} %copy-done.23, bf16[256,768]{1,0:T(8,128)(2,1)S(1)} %copy-done.24, f32[784,768]{1,0:T(8,128)S(1)} %fusion.99.refs_2_, f32[256,768]{1,0:T(8,128)S(1)} %fusion.101.refs_3_, f32[8,768]{1,0:T(8,128)S(1)} %copy-done.12, ...), custom_call_target="tpu_custom_call" | custom-call | flops 4297064448 | bytes 13078592 | tf_op jit(solution)/shard_map/pallas_call | solution.py:204
  205.4 5.2 shard_map.522
  210.6 7.1 %collective-permute-done.30 = bf16[4,48,1536]{2,1,0:T(8,128)(2,1)S(1)} collective-permute-done((bf16[4,48,1536]{2,1,0:T(8,128)(2,1)S(1)}, bf16[4,48,1536]{2,1,0:T(8,128)(2,1)S(1)}, u32[]{:S(2)}, u32[]{:S(2)}) %collective-permute-start.30) | collective-permute-done | bytes 589856 | tf_op jit(solution)/shard_map/ppermute | solution.py:978
  222.1 17.8 %shard_map.524 = (f32[512,768]{1,0:T(8,128)}, bf16[512,768]{1,0:T(8,128)(2,1)}, bf16[512,1536]{1,0:T(8,128)(2,1)}, bf16[512,1536]{1,0:T(8,128)(2,1)}, bf16[512,1...) custom-call(bf16[512,768]{1,0:T(8,128)(2,1)} %get-tuple-element.412.refs_0_.refs_3_, ...), custom_call_target="tpu_custom_call" | custom-call | flops 5435817984 | bytes 20471808 | tf_op jit(solution)/shard_map/pallas_call | solution.py:204
  240.0 17.9 %shard_map.525 = (f32[768,384]{1,0:T(8,128)}, bf16[768,384]{1,0:T(8,128)(2,1)}, f32[256,384]{1,0:T(8,128)}, bf16[256,384]{1,0:T(8,128)(2,1)}, f32[256,384]{1,0:T...) custom-call(bf16[512,768]{1,0:T(8,128)(2,1)} %get-tuple-element.418., ...), custom_call_target="tpu_custom_call" | custom-call | flops 2000000000 | bytes 13991936 | tf_op jit(solution)/shard_map/pallas_call | solution.py:204
  264.5 7.2 %shard_map.526.refs_1_ = f32[256,768]{1,0:T(8,128)} custom-call(bf16[256,768]{1,0:T(8,128)(2,1)} %copy-done.2, f32[256,768]{1,0:T(8,128)} %copy-done.9, f32[8,768]{1,0:T(8,128)} %get-tuple-element.384.refs_4_.refs_2_, bf16[768,1536]{1,0:T(8,128)(2,1)} %bitcast.150, bf16[768,1536]{1,0:T(8,128)(2,1)} %bitcast.148), custom_call_target="tpu_custom_call" | custom-call | flops 1207959552 | bytes 6709248 | tf_op jit(solution)/shard_map/pallas_call | solution.py:204
  273.9 7.9 %shard_map.527.refs_1_ = f32[256,768]{1,0:T(8,128)} custom-call(bf16[256,768]{1,0:T(8,128)(2,1)} %copy-done.2, f32[256,768]{1,0:T(8,128)} %shard_map.526.refs_1_, f32[8,768]{1,0:T(8,128)} %get-tuple-element.384.refs_4_.refs_2_, bf16[768,1536]{1,0:T(8,128)(2,1)} %bitcast.149, bf16[768,1536]{1,0:T(8,128)(2,1)} %bitcast.151), custom_call_target="tpu_custom_call" | custom-call | flops 1207959552 | bytes 6709248 | tf_op jit(solution)/shard_map/pallas_call | solution.py:204
  281.8 25.2 %shard_map.528 = (f32[1,1]{1,0:T(1,128)}, bf16[512,384]{1,0:T(8,128)(2,1)}, f32[8,384]{1,0:T(8,128)}, bf16[16,24,3072]{2,1,0:T(8,128)(2,1)}, bf16[16,24,3072]{2,1,0:T(8,128)(2,1)}) custom-call(f32[256,768]{1,0:T(8,128)} %get-tuple-element.434.refs_0_, f32[256,768]{1,0:T(8,128)} %shard_map.527.refs_1_, s32[1]{0:T(128)} %bitcast.47.refs_2_, ...), custom_call_target="tpu_custom_call" | custom-call | flops 4000000000 | bytes 20000000 | tf_op jit(solution)/shard_map/pallas_call | solution.py:900
  307.2 4.7 collective-permute-done.36
  318.8 14.2 %shard_map.530 = (bf16[768,3072]{1,0:T(8,128)(2,1)}, f32[512,768]{1,0:T(8,128)}, bf16[512,768]{1,0:T(8,128)(2,1)}, bf16[768,512]{1,0:T(8,128)(2,1)}, bf16[768,51...) custom-call(bf16[512,384]{1,0:T(8,128)(2,1)} %get-tuple-element.472.refs_0_, ...), custom_call_target="tpu_custom_call" | custom-call | flops 4831838208 | bytes 20299776 | tf_op jit(solution)/shard_map/pallas_call | solution.py:204
  338.8 15.2 %shard_map.532 = (bf16[768,3072]{1,0:T(8,128)(2,1)}, bf16[512,768]{1,0:T(8,128)(2,1)}, f32[512,768]{1,0:T(8,128)}, f32[8,768]{1,0:T(8,128)}) custom-call(f32[512,768]{1,0:T(8,128)} %get-tuple-element.494.refs_0_, bf16[512,768]{1,0:T(8,128)(2,1)} %get-tuple-element.495.refs_1_, bf16[768,512]{1,0:T(8,128)(2,1)} %get-tuple-element.496.refs_2_, ...), custom_call_target="tpu_custom_call" | custom-call | flops 6039797760 | bytes 24453120 | tf_op jit(solution)/shard_map/pallas_call | solution.py:204
  356.4 6.1 %shard_map.533 = (bf16[2,4,48,1536]{3,2,1,0:T(8,128)(2,1)}, bf16[2,4,48,1536]{3,2,1,0:T(8,128)(2,1)}, bf16[24,3072]{1,0:T(8,128)(2,1)}, bf16[24,3072]{1,0:T(8,128)(2,1)}, bf16[24,3072]{1,0:T(8,128)(2,1)}) custom-call(bf16[2,2,4,48,3072]{4,3,2,1,0:T(8,128)(2,1)} %bitcast.108, bf16[2,2,4,48,3072]{4,3,2,1,0:T(8,128)(2,1)} %bitcast.100, ...), custom_call_target="tpu_custom_call" | custom-call | flops 11206656 | bytes 11206656 | tf_op jit(solution)/shard_map/pallas_call | solution.py:1156
  372.5 16.5 %shard_map.534 = (bf16[512,1152]{1,0:T(8,128)(2,1)S(1)}, bf16[512,1152]{1,0:T(8,128)(2,1)S(1)}) custom-call(bf16[512,768]{1,0:T(8,128)(2,1)S(1)} %copy-done.27, s32[1,512]{1,0:T(1,128)S(1)} %bitcast.95, s32[512,1]{1,0:T(8,128)S(1)} %copy-done.8, bf16[768,896]{1,0:T(8,128)(2,1)S(1)} %bitcast.89, bf16[768,896]{1,0:T(8,128)(2,1)S(1)} %bitcast.92, ...), custom_call_target="tpu_custom_call" | custom-call | flops 2617245696 | bytes 9113600 | tf_op jit(solution)/shard_map/pallas_call | solution.py:204
  396.9 18.8 %shard_map.537 = (bf16[768,2048]{1,0:T(8,128)(2,1)}, bf16[768,2048]{1,0:T(8,128)(2,1)}) custom-call(bf16[512,768]{1,0:T(8,128)(2,1)} %get-tuple-element.521.branch.refs_0_, f32[512,768]{1,0:T(8,128)} %get-tuple-element.540.refs_1_, f32[512,768]{1,0:T(8,128)} %get-tuple-element.363.refs_0_.refs_2_, bf16[512,768]{1,0:T(8,128)(2,1)} %get-tuple-element.541.refs_3_, ...), custom_call_target="tpu_custom_call" | custom-call | flops 6039797760 | bytes 21491712 | tf_op jit(solution)/shard_map/pallas_call | solution.py:204
  415.8 5.9 %collective-permute-done.49 = bf16[768,2048]{1,0:T(8,128)(2,1)S(1)} collective-permute-done((bf16[768,2048]{1,0:T(8,128)(2,1)}, bf16[768,2048]{1,0:T(8,128)(2,1)S(1)}, u32[]{:S(2)}, u32[]{:S(2)}) %collective-permute-start.49) | collective-permute-done | bytes 3145760 | tf_op jit(solution)/shard_map/ppermute | solution.py:1002
  423.3 5.6 %shard_map.538 = (bf16[48,3072]{1,0:T(8,128)(2,1)}, bf16[48,3072]{1,0:T(8,128)(2,1)}, bf16[48,3072]{1,0:T(8,128)(2,1)}, bf16[2,4,48,1152]{3,2,1,0:T(8,128)(2,1)}, bf16[2,4,48,896]{3,2,1,0:T(8,128)(2,1)}) custom-call(bf16[2,2,4,48,3072]{4,3,2,1,0:T(8,128)(2,1)} %bitcast.112, bf16[2,2,4,48,3072]{4,3,2,1,0:T(8,128)(2,1)} %bitcast.104, ...), custom_call_target="tpu_custom_call" | custom-call | flops 9830400 | bytes 9830400 | tf_op jit(solution)/shard_map/pallas_call | solution.py:1156
  436.6 6.7 %collective-permute-done.50.refs_4_ = bf16[48,3072]{1,0:T(8,128)(2,1)S(1)} collective-permute-done((bf16[48,3072]{1,0:T(8,128)(2,1)}, bf16[48,3072]{1,0:T(8,128)(2,1)S(1)}, u32[]{:S(2)}, u32[]{:S(2)}) %collective-permute-start.50) | collective-permute-done | bytes 294944 | tf_op jit(solution)/shard_map/ppermute | solution.py:982
  443.4 11.2 %collective-permute-done.51.refs_5_ = bf16[48,3072]{1,0:T(8,128)(2,1)S(1)} collective-permute-done((bf16[48,3072]{1,0:T(8,128)(2,1)}, bf16[48,3072]{1,0:T(8,128)(2,1)S(1)}, u32[]{:S(2)}, u32[]{:S(2)}) %collective-permute-start.51) | collective-permute-done | bytes 294944 | tf_op jit(solution)/shard_map/ppermute | solution.py:982
  461.3 9.3 %collective-permute-done.56.refs_5_.refs_11_.refs_17_.refs_8_ = bf16[4,48,896]{2,1,0:T(8,128)(2,1)S(1)} collective-permute-done((bf16[4,48,896]{2,1,0:T(8,128)(2,1)}, bf16[4,48,896]{2,1,0:T(8,128)(2,1)S(1)}, u32[]{:S(2)}, u32[]{:S(2)}) %collective-permute-start.56) | collective-permute-done | bytes 344096 | tf_op jit(solution)/shard_map/ppermute | solution.py:978
  475.3 6.9 %collective-permute-start.57 = (bf16[48,2048]{1,0:T(8,128)(2,1)}, bf16[48,2048]{1,0:T(8,128)(2,1)S(1)}, u32[]{:S(2)}, u32[]{:S(2)}) collective-permute-start(bf16[48,2048]{1,0:T(8,128)(2,1)} %get-tuple-element.567), channel_id=1, source_target_pairs={{0,8},{2,10},{4,12},{6,14},{8,16},{10,18},{12,20},{14,22},{16,24},... | collective-permute-start | bytes 589832 | tf_op jit(solution)/shard_map/ppermute | solution.py:982
  489.3 5.4 %collective-permute-done.58.refs_5_ = bf16[48,2048]{1,0:T(8,128)(2,1)S(1)} collective-permute-done((bf16[48,2048]{1,0:T(8,128)(2,1)}, bf16[48,2048]{1,0:T(8,128)(2,1)S(1)}, u32[]{:S(2)}, u32[]{:S(2)}) %collective-permute-start.58) | collective-permute-done | bytes 196640 | tf_op jit(solution)/shard_map/ppermute | solution.py:982
  504.1 4.8 collective-permute-start.65
  519.9 6.1 %shard_map.543 = (f32[48,768]{1,0:T(8,128)}, f32[48,768]{1,0:T(8,128)}, f32[48,768]{1,0:T(8,128)}, f32[48,768]{1,0:T(8,128)}, f32[48,768]{1,0:T(8,128)}, /*index...) custom-call(f32[2,128]{1,0:T(2,128)} %copy-done.84, ...), custom_call_target="tpu_custom_call" | custom-call | flops 20000000 | bytes 10000000 | tf_op jit(solution)/shard_map/pallas_call | solution.py:1335
  (449 shorter events, 203.5 us)
Async XLA Ops:
  46.7 25.2 %collective-permute-start.9 = (bf16[48,3456]{1,0:T(8,128)(2,1)}, bf16[48,3456]{1,0:T(8,128)(2,1)}, u32[]{:S(2)}, u32[]{:S(2)}) collective-permute-start(bf16[48,3456]{1,0:T(8,128)(2,1)} %constant_dynamic-update-slice_fusion.refs_0_), channel_id=1, source_target_pairs={{0,8},{2,10},{4,12},{6,14},{8,16},{10,18},{12,20},{14,22},{16,24},... | collective-permute-start | bytes 995336 | tf_op jit(solution)/shard_map/ppermute | solution.py:982
  51.4 20.4 %collective-permute-start.8 = (bf16[48,3456]{1,0:T(8,128)(2,1)}, bf16[48,3456]{1,0:T(8,128)(2,1)}, u32[]{:S(2)}, u32[]{:S(2)}) collective-permute-start(bf16[48,3456]{1,0:T(8,128)(2,1)} %constant_dynamic-update-slice_fusion.refs_0_), channel_id=1, source_target_pairs={{0,16},{2,18},{4,20},{6,22},{8,24},{10,26},{12,28},{14,30},{16,0},... | collective-permute-start | bytes 995336 | tf_op jit(solution)/shard_map/ppermute | solution.py:982
  52.0 20.1 %collective-permute-start.7 = (bf16[48,3456]{1,0:T(8,128)(2,1)}, bf16[48,3456]{1,0:T(8,128)(2,1)}, u32[]{:S(2)}, u32[]{:S(2)}) collective-permute-start(bf16[48,3456]{1,0:T(8,128)(2,1)} %constant_dynamic-update-slice_fusion.refs_0_), channel_id=1, source_target_pairs={{0,24},{2,26},{4,28},{6,30},{8,0},{10,2},{12,4},{14,6},{16,8},{18,... | collective-permute-start | bytes 995336 | tf_op jit(solution)/shard_map/ppermute | solution.py:982
  55.1 19.5 %collective-permute-start.6 = (bf16[2,4,48,896]{3,2,1,0:T(8,128)(2,1)}, bf16[2,4,48,896]{3,2,1,0:T(8,128)(2,1)}, u32[]{:S(2)}, u32[]{:S(2)}) collective-permute-start(bf16[2,4,48,896]{3,2,1,0:T(8,128)(2,1)} %pad_maximum_fusion.7.refs_1_), channel_id=1, source_target_pairs={{0,2},{2,0},{4,6},{6,4},{8,10},{10,8},{12,14},{14,12},{16,18},{18,... | collective-permute-start | bytes 2064392 | tf_op jit(solution)/shard_map/ppermute | solution.py:978
  56.6 19.9 %collective-permute-start.5 = (bf16[2,4,48,1152]{3,2,1,0:T(8,128)(2,1)}, bf16[2,4,48,1152]{3,2,1,0:T(8,128)(2,1)}, u32[]{:S(2)}, u32[]{:S(2)}) collective-permute-start(bf16[2,4,48,1152]{3,2,1,0:T(8,128)(2,1)} %pad_maximum_fusion.6.refs_0_), channel_id=1, source_target_pairs={{0,4},{2,6},{4,0},{6,2},{8,12},{10,14},{12,8},{14,10},{16,20},{18,... | collective-permute-start | bytes 2654216 | tf_op jit(solution)/shard_map/ppermute | solution.py:978
  79.4 21.9 %collective-permute-start.10 = (bf16[2,2,4,48,1152]{4,3,2,1,0:T(8,128)(2,1)}, bf16[2,2,4,48,1152]{4,3,2,1,0:T(8,128)(2,1)S(1)}, u32[]{:S(2)}, u32[]{:S(2)}) collective-permute-start(bf16[2,2,4,48,1152]{4,3,2,1,0:T(8,128)(2,1)} %get-tuple-element.354), channel_id=1, source_target_pairs={{0,1},{1,0},{2,3},{3,2},{4,5},{5,4},{6,7},{7,6},{8,9},{9,8},{10,11... | collective-permute-start | bytes 5308424 | tf_op jit(solution)/shard_map/ppermute | solution.py:1002
  79.5 21.9 %collective-permute-start.11 = (bf16[2,2,4,48,896]{4,3,2,1,0:T(8,128)(2,1)}, bf16[2,2,4,48,896]{4,3,2,1,0:T(8,128)(2,1)S(1)}, u32[]{:S(2)}, u32[]{:S(2)}) collective-permute-start(bf16[2,2,4,48,896]{4,3,2,1,0:T(8,128)(2,1)} %get-tuple-element.352), channel_id=1, source_target_pairs={{0,1},{1,0},{2,3},{3,2},{4,5},{5,4},{6,7},{7,6},{8,9},{9,8},{10,11... | collective-permute-start | bytes 4128776 | tf_op jit(solution)/shard_map/ppermute | solution.py:1002
  101.3 33.5 %collective-permute-start.14 = (bf16[2,4,48,1920]{3,2,1,0:T(8,128)(2,1)}, bf16[2,4,48,1920]{3,2,1,0:T(8,128)(2,1)}, u32[]{:S(2)}, u32[]{:S(2)}) collective-permute-start(bf16[2,4,48,1920]{3,2,1,0:T(8,128)(2,1)} %pad_maximum_fusion.refs_0_), channel_id=1, source_target_pairs={{0,4},{2,6},{4,0},{6,2},{8,12},{10,14},{12,8},{14,10},{16,20},{18,... | collective-permute-start | bytes 4423688 | tf_op jit(solution)/shard_map/ppermute | solution.py:978
  102.9 30.7 %collective-permute-start.15 = (bf16[2,4,48,1536]{3,2,1,0:T(8,128)(2,1)S(1)}, bf16[2,4,48,1536]{3,2,1,0:T(8,128)(2,1)}, u32[]{:S(2)}, u32[]{:S(2)}) collective-permute-start(bf16[2,4,48,1536]{3,2,1,0:T(8,128)(2,1)S(1)} %pad_maximum_fusion.1.refs_1_), channel_id=1, source_target_pairs={{0,2},{2,0},{4,6},{6,4},{8,10},{10,8},{12,14},{14,12},{16,18},{18,... | collective-permute-start | bytes 3538952 | tf_op jit(solution)/shard_map/ppermute | solution.py:978
  103.5 21.5 %collective-permute-start.18 = (bf16[48,3072]{1,0:T(8,128)(2,1)S(1)}, bf16[48,3072]{1,0:T(8,128)(2,1)}, u32[]{:S(2)}, u32[]{:S(2)}) collective-permute-start(bf16[48,3072]{1,0:T(8,128)(2,1)S(1)} %constant_dynamic-update-slice_fusion.2.refs_0_), channel_id=1, source_target_pairs={{0,8},{2,10},{4,12},{6,14},{8,16},{10,18},{12,20},{14,22},{16,24},... | collective-permute-start | bytes 884744 | tf_op jit(solution)/shard_map/ppermute | solution.py:982
  110.0 21.2 %collective-permute-start.17 = (bf16[48,3072]{1,0:T(8,128)(2,1)S(1)}, bf16[48,3072]{1,0:T(8,128)(2,1)}, u32[]{:S(2)}, u32[]{:S(2)}) collective-permute-start(bf16[48,3072]{1,0:T(8,128)(2,1)S(1)} %constant_dynamic-update-slice_fusion.2.refs_0_), channel_id=1, source_target_pairs={{0,16},{2,18},{4,20},{6,22},{8,24},{10,26},{12,28},{14,30},{16,0},... | collective-permute-start | bytes 884744 | tf_op jit(solution)/shard_map/ppermute | solution.py:982
  138.9 22.9 %collective-permute-start.19 = (bf16[2,2,4,48,1920]{4,3,2,1,0:T(8,128)(2,1)}, bf16[2,2,4,48,1920]{4,3,2,1,0:T(8,128)(2,1)}, u32[]{:S(2)}, u32[]{:S(2)}) collective-permute-start(bf16[2,2,4,48,1920]{4,3,2,1,0:T(8,128)(2,1)} %get-tuple-element.387), channel_id=1, source_target_pairs={{0,1},{1,0},{2,3},{3,2},{4,5},{5,4},{6,7},{7,6},{8,9},{9,8},{10,11... | collective-permute-start | bytes 8847368 | tf_op jit(solution)/shard_map/ppermute | solution.py:1002
  139.0 22.8 %collective-permute-start.20 = (bf16[2,2,4,48,1536]{4,3,2,1,0:T(8,128)(2,1)}, bf16[2,2,4,48,1536]{4,3,2,1,0:T(8,128)(2,1)}, u32[]{:S(2)}, u32[]{:S(2)}) collective-permute-start(bf16[2,2,4,48,1536]{4,3,2,1,0:T(8,128)(2,1)} %get-tuple-element.395), channel_id=1, source_target_pairs={{0,1},{1,0},{2,3},{3,2},{4,5},{5,4},{6,7},{7,6},{8,9},{9,8},{10,11... | collective-permute-start | bytes 7077896 | tf_op jit(solution)/shard_map/ppermute | solution.py:1002
  161.8 36.1 %collective-permute-start.23 = (bf16[2,4,48,1536]{3,2,1,0:T(8,128)(2,1)S(1)}, bf16[2,4,48,1536]{3,2,1,0:T(8,128)(2,1)}, u32[]{:S(2)}, u32[]{:S(2)}) collective-permute-start(bf16[2,4,48,1536]{3,2,1,0:T(8,128)(2,1)S(1)} %pad_maximum_fusion.2.refs_0_), channel_id=1, source_target_pairs={{0,4},{2,6},{4,0},{6,2},{8,12},{10,14},{12,8},{14,10},{16,20},{18,... | collective-permute-start | bytes 3538952 | tf_op jit(solution)/shard_map/ppermute | solution.py:978
  162.3 35.6 %collective-permute-start.24 = (bf16[2,4,48,1536]{3,2,1,0:T(8,128)(2,1)}, bf16[2,4,48,1536]{3,2,1,0:T(8,128)(2,1)}, u32[]{:S(2)}, u32[]{:S(2)}) collective-permute-start(bf16[2,4,48,1536]{3,2,1,0:T(8,128)(2,1)} %pad_maximum_fusion.3.refs_1_), channel_id=1, source_target_pairs={{0,2},{2,0},{4,6},{6,4},{8,10},{10,8},{12,14},{14,12},{16,18},{18,... | collective-permute-start | bytes 3538952 | tf_op jit(solution)/shard_map/ppermute | solution.py:978
  164.1 30.1 %collective-permute-start.27 = (bf16[48,3072]{1,0:T(8,128)(2,1)S(1)}, bf16[48,3072]{1,0:T(8,128)(2,1)S(1)}, u32[]{:S(2)}, u32[]{:S(2)}) collective-permute-start(bf16[48,3072]{1,0:T(8,128)(2,1)S(1)} %constant_dynamic-update-slice_fusion.4.refs_0_), channel_id=1, source_target_pairs={{0,8},{2,10},{4,12},{6,14},{8,16},{10,18},{12,20},{14,22},{16,24},... | collective-permute-start | bytes 884744 | tf_op jit(solution)/shard_map/ppermute | solution.py:982
  169.6 24.5 %collective-permute-start.26 = (bf16[48,3072]{1,0:T(8,128)(2,1)S(1)}, bf16[48,3072]{1,0:T(8,128)(2,1)S(1)}, u32[]{:S(2)}, u32[]{:S(2)}) collective-permute-start(bf16[48,3072]{1,0:T(8,128)(2,1)S(1)} %constant_dynamic-update-slice_fusion.4.refs_0_), channel_id=1, source_target_pairs={{0,16},{2,18},{4,20},{6,22},{8,24},{10,26},{12,28},{14,30},{16,0},... | collective-permute-start | bytes 884744 | tf_op jit(solution)/shard_map/ppermute | solution.py:982
  173.0 21.1 %collective-permute-start.25 = (bf16[48,3072]{1,0:T(8,128)(2,1)S(1)}, bf16[48,3072]{1,0:T(8,128)(2,1)S(1)}, u32[]{:S(2)}, u32[]{:S(2)}) collective-permute-start(bf16[48,3072]{1,0:T(8,128)(2,1)S(1)} %constant_dynamic-update-slice_fusion.4.refs_0_), channel_id=1, source_target_pairs={{0,24},{2,26},{4,28},{6,30},{8,0},{10,2},{12,4},{14,6},{16,8},{18,... | collective-permute-start | bytes 884744 | tf_op jit(solution)/shard_map/ppermute | solution.py:982
  219.1 38.8 %collective-permute-start.32 = (bf16[2,4,48,1536]{3,2,1,0:T(8,128)(2,1)S(1)}, bf16[2,4,48,1536]{3,2,1,0:T(8,128)(2,1)S(1)}, u32[]{:S(2)}, u32[]{:S(2)}) collective-permute-start(bf16[2,4,48,1536]{3,2,1,0:T(8,128)(2,1)S(1)} %pad_maximum_fusion.4.refs_0_), channel_id=1, source_target_pairs={{0,4},{2,6},{4,0},{6,2},{8,12},{10,14},{12,8},{14,10},{16,20},{18,... | collective-permute-start | bytes 3538952 | tf_op jit(solution)/shard_map/ppermute | solution.py:978
  220.7 37.3 %collective-permute-start.33 = (bf16[2,4,48,1536]{3,2,1,0:T(8,128)(2,1)S(1)}, bf16[2,4,48,1536]{3,2,1,0:T(8,128)(2,1)S(1)}, u32[]{:S(2)}, u32[]{:S(2)}) collective-permute-start(bf16[2,4,48,1536]{3,2,1,0:T(8,128)(2,1)S(1)} %pad_maximum_fusion.5.refs_1_), channel_id=1, source_target_pairs={{0,2},{2,0},{4,6},{6,4},{8,10},{10,8},{12,14},{14,12},{16,18},{18,... | collective-permute-start | bytes 3538952 | tf_op jit(solution)/shard_map/ppermute | solution.py:978
  333.5 20.5 %collective-permute-start.41 = (bf16[768,3072]{1,0:T(8,128)(2,1)}, bf16[768,3072]{1,0:T(8,128)(2,1)S(1)}, u32[]{:S(2)}, u32[]{:S(2)}) collective-permute-start(bf16[768,3072]{1,0:T(8,128)(2,1)} %get-tuple-element.503), channel_id=1, source_target_pairs={{0,1},{1,0},{2,3},{3,2},{4,5},{5,4},{6,7},{7,6},{8,9},{9,8},{10,11... | collective-permute-start | bytes 14155784 | tf_op jit(solution)/shard_map/ppermute | solution.py:1002
  362.5 28.7 %collective-permute-start.45 = (bf16[2,4,48,1536]{3,2,1,0:T(8,128)(2,1)}, bf16[2,4,48,1536]{3,2,1,0:T(8,128)(2,1)}, u32[]{:S(2)}, u32[]{:S(2)}) collective-permute-start(bf16[2,4,48,1536]{3,2,1,0:T(8,128)(2,1)} %get-tuple-element.519), channel_id=1, source_target_pairs={{0,2},{2,0},{4,6},{6,4},{8,10},{10,8},{12,14},{14,12},{16,18},{18,... | collective-permute-start | bytes 3538952 | tf_op jit(solution)/shard_map/ppermute | solution.py:978
  364.0 27.2 %collective-permute-start.46 = (bf16[2,4,48,1536]{3,2,1,0:T(8,128)(2,1)}, bf16[2,4,48,1536]{3,2,1,0:T(8,128)(2,1)}, u32[]{:S(2)}, u32[]{:S(2)}) collective-permute-start(bf16[2,4,48,1536]{3,2,1,0:T(8,128)(2,1)} %get-tuple-element.520), channel_id=1, source_target_pairs={{0,4},{2,6},{4,0},{6,2},{8,12},{10,14},{12,8},{14,10},{16,20},{18,... | collective-permute-start | bytes 3538952 | tf_op jit(solution)/shard_map/ppermute | solution.py:978
  364.9 26.3 %collective-permute-start.42 = (bf16[24,3072]{1,0:T(8,128)(2,1)}, bf16[24,3072]{1,0:T(8,128)(2,1)}, u32[]{:S(2)}, u32[]{:S(2)}) collective-permute-start(bf16[24,3072]{1,0:T(8,128)(2,1)} %get-tuple-element.516), channel_id=1, source_target_pairs={{0,8},{2,10},{4,12},{6,14},{8,16},{10,18},{12,20},{14,22},{16,24},... | collective-permute-start | bytes 442376 | tf_op jit(solution)/shard_map/ppermute | solution.py:982
  368.1 23.1 %collective-permute-start.43 = (bf16[24,3072]{1,0:T(8,128)(2,1)}, bf16[24,3072]{1,0:T(8,128)(2,1)}, u32[]{:S(2)}, u32[]{:S(2)}) collective-permute-start(bf16[24,3072]{1,0:T(8,128)(2,1)} %get-tuple-element.517), channel_id=1, source_target_pairs={{0,16},{2,18},{4,20},{6,22},{8,24},{10,26},{12,28},{14,30},{16,0},... | collective-permute-start | bytes 442376 | tf_op jit(solution)/shard_map/ppermute | solution.py:982
  368.3 22.9 %collective-permute-start.44 = (bf16[24,3072]{1,0:T(8,128)(2,1)}, bf16[24,3072]{1,0:T(8,128)(2,1)}, u32[]{:S(2)}, u32[]{:S(2)}) collective-permute-start(bf16[24,3072]{1,0:T(8,128)(2,1)} %get-tuple-element.518), channel_id=1, source_target_pairs={{0,24},{2,26},{4,28},{6,30},{8,0},{10,2},{12,4},{14,6},{16,8},{18,... | collective-permute-start | bytes 442376 | tf_op jit(solution)/shard_map/ppermute | solution.py:982
  395.1 20.5 %collective-permute-start.47 = (bf16[4,48,1536]{2,1,0:T(8,128)(2,1)}, bf16[4,48,1536]{2,1,0:T(8,128)(2,1)S(1)}, u32[]{:S(2)}, u32[]{:S(2)}) collective-permute-start(bf16[4,48,1536]{2,1,0:T(8,128)(2,1)} %get-tuple-element.538), channel_id=1, source_target_pairs={{0,4},{2,6},{4,0},{6,2},{8,12},{10,14},{12,8},{14,10},{16,20},{18,... | collective-permute-start | bytes 1769480 | tf_op jit(solution)/shard_map/ppermute | solution.py:978
  396.3 19.4 %collective-permute-start.48 = (bf16[4,48,1536]{2,1,0:T(8,128)(2,1)}, bf16[4,48,1536]{2,1,0:T(8,128)(2,1)S(1)}, u32[]{:S(2)}, u32[]{:S(2)}) collective-permute-start(bf16[4,48,1536]{2,1,0:T(8,128)(2,1)} %get-tuple-element.539), channel_id=1, source_target_pairs={{0,2},{2,0},{4,6},{6,4},{8,10},{10,8},{12,14},{14,12},{16,18},{18,... | collective-permute-start | bytes 1769480 | tf_op jit(solution)/shard_map/ppermute | solution.py:978
  428.9 25.6 %collective-permute-start.53 = (bf16[2,4,48,1152]{3,2,1,0:T(8,128)(2,1)}, bf16[2,4,48,1152]{3,2,1,0:T(8,128)(2,1)S(1)}, u32[]{:S(2)}, u32[]{:S(2)}) collective-permute-start(bf16[2,4,48,1152]{3,2,1,0:T(8,128)(2,1)} %get-tuple-element.555), channel_id=1, source_target_pairs={{0,2},{2,0},{4,6},{6,4},{8,10},{10,8},{12,14},{14,12},{16,18},{18,... | collective-permute-start | bytes 2654216 | tf_op jit(solution)/shard_map/ppermute | solution.py:978
  430.4 24.1 %collective-permute-start.54 = (bf16[2,4,48,896]{3,2,1,0:T(8,128)(2,1)}, bf16[2,4,48,896]{3,2,1,0:T(8,128)(2,1)S(1)}, u32[]{:S(2)}, u32[]{:S(2)}) collective-permute-start(bf16[2,4,48,896]{3,2,1,0:T(8,128)(2,1)} %get-tuple-element.556), channel_id=1, source_target_pairs={{0,4},{2,6},{4,0},{6,2},{8,12},{10,14},{12,8},{14,10},{16,20},{18,... | collective-permute-start | bytes 2064392 | tf_op jit(solution)/shard_map/ppermute | solution.py:978
  434.3 20.3 %collective-permute-start.51 = (bf16[48,3072]{1,0:T(8,128)(2,1)}, bf16[48,3072]{1,0:T(8,128)(2,1)S(1)}, u32[]{:S(2)}, u32[]{:S(2)}) collective-permute-start(bf16[48,3072]{1,0:T(8,128)(2,1)} %get-tuple-element.553), channel_id=1, source_target_pairs={{0,16},{2,18},{4,20},{6,22},{8,24},{10,26},{12,28},{14,30},{16,0},... | collective-permute-start | bytes 884744 | tf_op jit(solution)/shard_map/ppermute | solution.py:982
  434.5 20.1 %collective-permute-start.52 = (bf16[48,3072]{1,0:T(8,128)(2,1)}, bf16[48,3072]{1,0:T(8,128)(2,1)S(1)}, u32[]{:S(2)}, u32[]{:S(2)}) collective-permute-start(bf16[48,3072]{1,0:T(8,128)(2,1)} %get-tuple-element.554), channel_id=1, source_target_pairs={{0,24},{2,26},{4,28},{6,30},{8,0},{10,2},{12,4},{14,6},{16,8},{18,... | collective-permute-start | bytes 884744 | tf_op jit(solution)/shard_map/ppermute | solution.py:982
  (138 other events, 1284.6 us)

commit v4 on v3

--- a/solution.py
+++ b/solution.py
@@ -209,7 +209,9 @@
         scratch_shapes=buffers,
         cost_estimate=pl.CostEstimate(flops=2 * macs, bytes_accessed=moved, transcendentals=exps),
         compiler_params=pltpu.CompilerParams(
-            vmem_limit_bytes=room(list(ins) + outs + held) if ahead else 58 * 2**20
+            vmem_limit_bytes=room(list(ins) + outs + held, 2 * MARGIN)
+            if late or early
+            else room(list(ins) + outs + held) if ahead else 58 * 2**20
         ),
     )(*ins)
 
@@ -1027,6 +1029,7 @@
         [((4, rows, part.stop - part.start), LOW) for part in cols],
         [],
         0,
+        ahead=True,
     )
 
 
@@ -1068,7 +1071,7 @@
         cost_estimate=pl.CostEstimate(
             flops=0, bytes_accessed=8 * sum(value.size for value in ins), transcendentals=0
         ),
-        compiler_params=pltpu.CompilerParams(vmem_limit_bytes=58 * 2**20),
+        compiler_params=pltpu.CompilerParams(vmem_limit_bytes=20 * 2**20),
     )(*ins)
 
 
@@ -1163,7 +1166,7 @@
         ],
         out_shape=shapes,
         cost_estimate=pl.CostEstimate(flops=moved, bytes_accessed=moved, transcendentals=0),
-        compiler_params=pltpu.CompilerParams(vmem_limit_bytes=58 * 2**20),
+        compiler_params=pltpu.CompilerParams(vmem_limit_bytes=34 * 2**20),
     )(*operands)
 
 

time: 537 us -> 511 us (0.952)
  Pallas kernels: 256 us -> 198 us
  local copies, waits for them, and re-layouts: 44 us -> 66.2 us
  waiting for transfers between devices: 90.1 us -> 103 us
  starting transfers between devices: 97.3 us -> 89.2 us
    pallas_call x10, Pallas kernels: 34.6 us -> 7.38 us  [sum_parts(): pl.pallas_call(functools.partial(sum_kernel, tuple(plan), squares), grid=...]
    pallas_call x15, Pallas kernels: 170 us -> 144 us  [on_chip(): pl.pallas_call(kernel, in_specs=in_specs, out_specs=out_specs, out_shape=...]
    unnamed x190 -> x322, local copies, waits for them, and re-layouts: 26.5 us -> 46.9 us
    ppermute x21, starting transfers between devices: 53.7 us -> 45.3 us  [shift(): return lax.ppermute(values, 'dp', pairs)]
    another operation x8, other arithmetic: 11.1 us -> 5.32 us  [gather_near(): jnp.stack([values, other], axis)]
  transfers between devices with their start and end apart: 69 -> 69, of which waited for: 22 -> 27; matrix products, arithmetic and copies ran while one was open for 8% -> 10% of each run, Pallas kernels for 33% -> 29%
where the time goes in v4:
time: 511 us; the launch traced here: 502 us
  Pallas kernels  198 us (39%)
  waiting for transfers between devices  103 us (20%)
  starting transfers between devices  89.2 us (17%)
  local copies, waits for them, and re-layouts  66.2 us (13%)
  other arithmetic  27.6 us (5%)
  matrix products  12.3 us (2%)
  between operations  5.71 us (1%)
    pallas_call x15, Pallas kernels, on_chip(): pl.pallas_call(kernel, in_specs=in_specs, out_specs=out_specs, out_shape=...  144 us
    ppermute x28, waiting for transfers between devices, flip(): return lax.ppermute(values, 'dp', pairs)  50.2 us
    unnamed x322, local copies, waits for them, and re-layouts  46.9 us
    ppermute x21, starting transfers between devices, shift(): return lax.ppermute(values, 'dp', pairs)  45.3 us
    ppermute x21, waiting for transfers between devices, shift(): return lax.ppermute(values, 'dp', pairs)  33 us
    ppermute x28, starting transfers between devices, flip(): return lax.ppermute(values, 'dp', pairs)  28.9 us
    pallas_call x1, Pallas kernels, pred_back_all(): pl.pallas_call(functools.partial(pred_back_all_kernel, size, count_all, d...  25.3 us
    ppermute x13, waiting for transfers between devices, swap(): return lax.ppermute(values, 'mp', [(0, 1), (1, 0)])  14.3 us
  transfers between devices with their start and end apart: 69, of which 27 were waited for; matrix products, arithmetic and copies ran while one was open for 10% of the time, Pallas kernels for 29%

profile of v4, /device:TPU:0, one launch (start us, length us, event | category | flops | bytes accessed | tf_op | source)
XLA Modules:
  0.0 501.8 jit_solution(11311603284808552214)
XLA Ops:
  38.0 4.9 collective-permute-done.4
  86.1 13.7 %collective-permute-done.13 = bf16[4,48,1536]{2,1,0:T(8,128)(2,1)S(1)} collective-permute-done((bf16[4,48,1536]{2,1,0:T(8,128)(2,1)S(1)}, bf16[4,48,1536]{2,1,0:T(8,128)(2,1)S(1)}, u32[]{:S(2)}, u32[]{:S(2)}) %collective-permute-start.13) | collective-permute-done | bytes 589856 | tf_op jit(solution)/shard_map/ppermute | solution.py:980
  100.0 3.8 collective-permute-done.12
  107.8 5.2 %collective-permute-start.18 = (bf16[48,3072]{1,0:T(8,128)(2,1)S(1)}, bf16[48,3072]{1,0:T(8,128)(2,1)S(1)}, u32[]{:S(2)}, u32[]{:S(2)}) collective-permute-start(bf16[48,3072]{1,0:T(8,128)(2,1)S(1)} %constant_dynamic-update-slice_fusion.2.refs_0_), channel_id=1, source_target_pairs={{0,8},{2,10},{4,12},{6,14},{8,16},{10,18},{12,20},{14,22},{16,24},... | collective-permute-start | bytes 884744 | tf_op jit(solution)/shard_map/ppermute | solution.py:984
  115.9 8.7 %shard_map.517 = (f32[512,768]{1,0:T(8,128)S(1)}, bf16[512,768]{1,0:T(8,128)(2,1)S(1)}, bf16[512,1152]{1,0:T(8,128)(2,1)S(1)}, bf16[512,1152]{1,0:T(8,128)(2,1)S...) custom-call(bf16[512,768]{1,0:T(8,128)(2,1)S(1)} %copy-done.90, f32[512,768]{1,0:T(8,128)S(1)} %copy-done.29, ...), custom_call_target="tpu_custom_call" | custom-call | flops 3321888768 | bytes 15200256 | tf_op jit(solution)/shard_map/pallas_call | solution.py:204
  125.7 5.1 %collective-permute-done.17.refs_2_ = bf16[48,3072]{1,0:T(8,128)(2,1)S(1)} collective-permute-done((bf16[48,3072]{1,0:T(8,128)(2,1)S(1)}, bf16[48,3072]{1,0:T(8,128)(2,1)S(1)}, u32[]{:S(2)}, u32[]{:S(2)}) %collective-permute-start.17) | collective-permute-done | bytes 294944 | tf_op jit(solution)/shard_map/ppermute | solution.py:984
  131.7 5.4 %collective-permute-done.14.refs_2_ = bf16[2,4,48,1920]{3,2,1,0:T(8,128)(2,1)S(1)} collective-permute-done((bf16[2,4,48,1920]{3,2,1,0:T(8,128)(2,1)S(1)}, bf16[2,4,48,1920]{3,2,1,0:T(8,128)(2,1)S(1)}, u32[]{:S(2)}, u32[]{:S(2)}) %collective-permute-start.14) | collective-permute-done | bytes 1474592 | tf_op jit(solution)/shard_map/ppermute | solution.py:980
  137.2 3.5 shard_map.515
  149.7 12.6 %shard_map.518 = (f32[512,768]{1,0:T(8,128)S(1)}, bf16[512,768]{1,0:T(8,128)(2,1)S(1)}, bf16[512,384]{1,0:T(8,128)(2,1)S(1)}, bf16[512,384]{1,0:T(8,128)(2,1)S(1...) custom-call(f32[512,768]{1,0:T(8,128)S(1)} %copy-done.27, ...), custom_call_target="tpu_custom_call" | custom-call | flops 1409286144 | bytes 9924608 | tf_op jit(solution)/shard_map/pallas_call | solution.py:204
  170.1 4.2 collective-permute-start.27
  176.9 20.3 %shard_map.521 = (f32[256,768]{1,0:T(8,128)S(1)}, bf16[256,768]{1,0:T(8,128)(2,1)S(1)}) custom-call(bf16[784,768]{1,0:T(8,128)(2,1)S(1)} %copy-done.88, bf16[256,768]{1,0:T(8,128)(2,1)S(1)} %copy-done.89, f32[784,768]{1,0:T(8,128)S(1)} %copy-done.25, f32[256,768]{1,0:T(8,128)S(1)} %copy-done.48, f32[8,768]{1,0:T(8,128)S(1)} %get-tuple-element.384.refs_4_.refs_2_, ...), custom_call_target="tpu_custom_call" | custom-call | flops 4297064448 | bytes 13078592 | tf_op jit(solution)/shard_map/pallas_call | solution.py:204
  204.1 5.2 %shard_map.522 = (bf16[768,384]{1,0:T(8,128)(2,1)}, bf16[768,384]{1,0:T(8,128)(2,1)}, bf16[384,768]{1,0:T(8,128)(2,1)}, bf16[384,768]{1,0:T(8,128)(2,1)}, bf16[3...) custom-call(s32[1]{0:T(128)} %bitcast.36.side_ref.refs_35_.side, ...), custom_call_target="tpu_custom_call" | custom-call | flops 1000000000 | bytes 9000000 | tf_op jit(solution)/shard_map/pallas_call | solution.py:955
  209.3 7.1 %collective-permute-done.30 = bf16[4,48,1536]{2,1,0:T(8,128)(2,1)S(1)} collective-permute-done((bf16[4,48,1536]{2,1,0:T(8,128)(2,1)S(1)}, bf16[4,48,1536]{2,1,0:T(8,128)(2,1)S(1)}, u32[]{:S(2)}, u32[]{:S(2)}) %collective-permute-start.30) | collective-permute-done | bytes 589856 | tf_op jit(solution)/shard_map/ppermute | solution.py:980
  220.8 15.7 %shard_map.524 = (f32[512,768]{1,0:T(8,128)S(1)}, bf16[512,768]{1,0:T(8,128)(2,1)S(1)}, bf16[512,1536]{1,0:T(8,128)(2,1)S(1)}, bf16[512,1536]{1,0:T(8,128)(2,1)S...) custom-call(bf16[512,768]{1,0:T(8,128)(2,1)S(1)} %copy-done.73, f32[512,768]{1,0:T(8,128)S(1)} %copy-done.70, ...), custom_call_target="tpu_custom_call" | custom-call | flops 5435817984 | bytes 20471808 | tf_op jit(solution)/shard_map/pallas_call | solution.py:204
  243.2 17.9 %shard_map.525 = (f32[768,384]{1,0:T(8,128)}, bf16[768,384]{1,0:T(8,128)(2,1)}, f32[256,384]{1,0:T(8,128)}, bf16[256,384]{1,0:T(8,128)(2,1)}, f32[256,384]{1,0:T...) custom-call(bf16[512,768]{1,0:T(8,128)(2,1)} %copy-done.84, ...), custom_call_target="tpu_custom_call" | custom-call | flops 2000000000 | bytes 13991936 | tf_op jit(solution)/shard_map/pallas_call | solution.py:204
  263.6 3.6 shard_map.526.refs_1_
  271.0 4.5 shard_map.527.refs_1_
  276.3 25.3 %shard_map.528 = (f32[1,1]{1,0:T(1,128)}, bf16[512,384]{1,0:T(8,128)(2,1)}, f32[8,384]{1,0:T(8,128)}, bf16[16,24,3072]{2,1,0:T(8,128)(2,1)}, bf16[16,24,3072]{2,1,0:T(8,128)(2,1)}) custom-call(f32[256,768]{1,0:T(8,128)} %get-tuple-element.434.refs_0_, f32[256,768]{1,0:T(8,128)} %copy-done.47, s32[1]{0:T(128)} %bitcast.47.refs_2_, ...), custom_call_target="tpu_custom_call" | custom-call | flops 4000000000 | bytes 20000000 | tf_op jit(solution)/shard_map/pallas_call | solution.py:902
  301.8 4.6 collective-permute-done.36
  312.2 12.2 %shard_map.530 = (bf16[768,3072]{1,0:T(8,128)(2,1)}, f32[512,768]{1,0:T(8,128)S(1)}, bf16[512,768]{1,0:T(8,128)(2,1)S(1)}, bf16[768,512]{1,0:T(8,128)(2,1)S(1)},...) custom-call(bf16[512,384]{1,0:T(8,128)(2,1)S(1)} %copy-done.85, ...), custom_call_target="tpu_custom_call" | custom-call | flops 4831838208 | bytes 20299776 | tf_op jit(solution)/shard_map/pallas_call | solution.py:204
  330.6 11.2 %shard_map.532 = (bf16[768,3072]{1,0:T(8,128)(2,1)}, bf16[512,768]{1,0:T(8,128)(2,1)S(1)}, f32[512,768]{1,0:T(8,128)S(1)}, f32[8,768]{1,0:T(8,128)S(1)}) custom-call(f32[512,768]{1,0:T(8,128)S(1)} %copy-done.110, bf16[512,768]{1,0:T(8,128)(2,1)S(1)} %get-tuple-element.495.refs_1_, bf16[768,512]{1,0:T(8,128)(2,1)S(1)} %get-tuple-element.496.refs_2_, ...), custom_call_target="tpu_custom_call" | custom-call | flops 6039797760 | bytes 24453120 | tf_op jit(solution)/shard_map/pallas_call | solution.py:204
  341.9 4.9 copy-done.3
  356.1 16.5 %shard_map.534 = (bf16[512,1152]{1,0:T(8,128)(2,1)S(1)}, bf16[512,1152]{1,0:T(8,128)(2,1)S(1)}) custom-call(bf16[512,768]{1,0:T(8,128)(2,1)S(1)} %copy-done.101, s32[1,512]{1,0:T(1,128)S(1)} %bitcast.158, s32[512,1]{1,0:T(8,128)S(1)} %copy-done.45, bf16[768,896]{1,0:T(8,128)(2,1)S(1)} %bitcast.145, bf16[768,896]{1,0:T(8,128)(2,1)S(1)} %bitcast.148, ...), custom_call_target="tpu_custom_call" | custom-call | flops 2617245696 | bytes 9113600 | tf_op jit(solution)/shard_map/pallas_call | solution.py:204
  385.3 18.0 %shard_map.537 = (bf16[768,2048]{1,0:T(8,128)(2,1)S(1)}, bf16[768,2048]{1,0:T(8,128)(2,1)}) custom-call(bf16[512,768]{1,0:T(8,128)(2,1)S(1)} %copy-done.102, f32[512,768]{1,0:T(8,128)S(1)} %copy-done.108, f32[512,768]{1,0:T(8,128)S(1)} %copy-done.28, bf16[512,768]{1,0:T(8,128)(2,1)S(1)} %copy-done.93, bf16[512,768]{1,0:T(8,128)(2,1)S(1)} %copy-done.91, ...), custom_call_target="tpu_custom_call" | custom-call | flops 6039797760 | bytes 21491712 | tf_op jit(solution)/shard_map/pallas_call | solution.py:204
  404.2 5.9 %collective-permute-done.49 = bf16[768,2048]{1,0:T(8,128)(2,1)S(1)} collective-permute-done((bf16[768,2048]{1,0:T(8,128)(2,1)}, bf16[768,2048]{1,0:T(8,128)(2,1)S(1)}, u32[]{:S(2)}, u32[]{:S(2)}) %collective-permute-start.49) | collective-permute-done | bytes 3145760 | tf_op jit(solution)/shard_map/ppermute | solution.py:1004
  419.6 7.5 %collective-permute-done.50.refs_4_ = bf16[48,3072]{1,0:T(8,128)(2,1)S(1)} collective-permute-done((bf16[48,3072]{1,0:T(8,128)(2,1)S(1)}, bf16[48,3072]{1,0:T(8,128)(2,1)S(1)}, u32[]{:S(2)}, u32[]{:S(2)}) %collective-permute-start.50) | collective-permute-done | bytes 294944 | tf_op jit(solution)/shard_map/ppermute | solution.py:984
  427.0 11.5 %collective-permute-done.51.refs_5_ = bf16[48,3072]{1,0:T(8,128)(2,1)S(1)} collective-permute-done((bf16[48,3072]{1,0:T(8,128)(2,1)S(1)}, bf16[48,3072]{1,0:T(8,128)(2,1)S(1)}, u32[]{:S(2)}, u32[]{:S(2)}) %collective-permute-start.51) | collective-permute-done | bytes 294944 | tf_op jit(solution)/shard_map/ppermute | solution.py:984
  441.9 8.3 %collective-permute-done.56.refs_5_.refs_11_.refs_17_.refs_8_ = bf16[4,48,896]{2,1,0:T(8,128)(2,1)S(1)} collective-permute-done((bf16[4,48,896]{2,1,0:T(8,128)(2,1)S(1)}, bf16[4,48,896]{2,1,0:T(8,128)(2,1)S(1)}, u32[]{:S(2)}, u32[]{:S(2)}) %collective-permute-start.56) | collective-permute-done | bytes 344096 | tf_op jit(solution)/shard_map/ppermute | solution.py:980
  451.8 6.9 %collective-permute-start.57 = (bf16[48,2048]{1,0:T(8,128)(2,1)}, bf16[48,2048]{1,0:T(8,128)(2,1)S(1)}, u32[]{:S(2)}, u32[]{:S(2)}) collective-permute-start(bf16[48,2048]{1,0:T(8,128)(2,1)} %get-tuple-element.567), channel_id=1, source_target_pairs={{0,8},{2,10},{4,12},{6,14},{8,16},{10,18},{12,20},{14,22},{16,24},... | collective-permute-start | bytes 589832 | tf_op jit(solution)/shard_map/ppermute | solution.py:984
  464.3 5.3 %collective-permute-done.58.refs_5_ = bf16[48,2048]{1,0:T(8,128)(2,1)S(1)} collective-permute-done((bf16[48,2048]{1,0:T(8,128)(2,1)S(1)}, bf16[48,2048]{1,0:T(8,128)(2,1)S(1)}, u32[]{:S(2)}, u32[]{:S(2)}) %collective-permute-start.58) | collective-permute-done | bytes 196640 | tf_op jit(solution)/shard_map/ppermute | solution.py:984
  477.6 5.5 %collective-permute-start.65 = (f32[2,128]{1,0:T(2,128)S(1)}, f32[2,128]{1,0:T(2,128)S(1)}, u32[]{:S(2)}, u32[]{:S(2)}) collective-permute-start(f32[2,128]{1,0:T(2,128)S(1)} %add_add_fusion.1), channel_id=1, source_target_pairs={{0,12},{1,13},{2,14},{3,15},{4,8},{5,9},{6,10},{7,11},{8,4},{9,5},... | collective-permute-start | bytes 3080 | tf_op jit(solution)/shard_map/ppermute | solution.py:990
  494.2 6.1 %shard_map.543 = (f32[48,768]{1,0:T(8,128)}, f32[48,768]{1,0:T(8,128)}, f32[48,768]{1,0:T(8,128)}, f32[48,768]{1,0:T(8,128)}, f32[48,768]{1,0:T(8,128)}, /*index...) custom-call(f32[2,128]{1,0:T(2,128)} %copy-done.150, ...), custom_call_target="tpu_custom_call" | custom-call | flops 20000000 | bytes 10000000 | tf_op jit(solution)/shard_map/pallas_call | solution.py:1338
  (579 shorter events, 205.0 us)
Async XLA Ops:
  7.3 26.6 %collective-permute-start.2 = (bf16[48,2048]{1,0:T(8,128)(2,1)S(1)}, bf16[48,2048]{1,0:T(8,128)(2,1)S(1)}, u32[]{:S(2)}, u32[]{:S(2)}) collective-permute-start(bf16[48,2048]{1,0:T(8,128)(2,1)S(1)} %concatenate.136.refs_0_), channel_id=1, source_target_pairs={{0,8},{2,10},{4,12},{6,14},{8,16},{10,18},{12,20},{14,22},{16,24},... | collective-permute-start | bytes 589832 | tf_op jit(solution)/shard_map/ppermute | solution.py:984
  10.3 23.5 %collective-permute-start.1 = (bf16[48,2048]{1,0:T(8,128)(2,1)S(1)}, bf16[48,2048]{1,0:T(8,128)(2,1)S(1)}, u32[]{:S(2)}, u32[]{:S(2)}) collective-permute-start(bf16[48,2048]{1,0:T(8,128)(2,1)S(1)} %concatenate.136.refs_0_), channel_id=1, source_target_pairs={{0,16},{2,18},{4,20},{6,22},{8,24},{10,26},{12,28},{14,30},{16,0},... | collective-permute-start | bytes 589832 | tf_op jit(solution)/shard_map/ppermute | solution.py:984
  12.9 20.9 %collective-permute-start = (bf16[48,2048]{1,0:T(8,128)(2,1)S(1)}, bf16[48,2048]{1,0:T(8,128)(2,1)S(1)}, u32[]{:S(2)}, u32[]{:S(2)}) collective-permute-start(bf16[48,2048]{1,0:T(8,128)(2,1)S(1)} %concatenate.136.refs_0_), channel_id=1, source_target_pairs={{0,24},{2,26},{4,28},{6,30},{8,0},{10,2},{12,4},{14,6},{16,8},{18,... | collective-permute-start | bytes 589832 | tf_op jit(solution)/shard_map/ppermute | solution.py:984
  54.2 25.8 %collective-permute-start.9 = (bf16[48,3456]{1,0:T(8,128)(2,1)}, bf16[48,3456]{1,0:T(8,128)(2,1)}, u32[]{:S(2)}, u32[]{:S(2)}) collective-permute-start(bf16[48,3456]{1,0:T(8,128)(2,1)} %constant_dynamic-update-slice_fusion.refs_0_), channel_id=1, source_target_pairs={{0,8},{2,10},{4,12},{6,14},{8,16},{10,18},{12,20},{14,22},{16,24},... | collective-permute-start | bytes 995336 | tf_op jit(solution)/shard_map/ppermute | solution.py:984
  54.9 25.1 %collective-permute-start.8 = (bf16[48,3456]{1,0:T(8,128)(2,1)}, bf16[48,3456]{1,0:T(8,128)(2,1)}, u32[]{:S(2)}, u32[]{:S(2)}) collective-permute-start(bf16[48,3456]{1,0:T(8,128)(2,1)} %constant_dynamic-update-slice_fusion.refs_0_), channel_id=1, source_target_pairs={{0,16},{2,18},{4,20},{6,22},{8,24},{10,26},{12,28},{14,30},{16,0},... | collective-permute-start | bytes 995336 | tf_op jit(solution)/shard_map/ppermute | solution.py:984
  55.2 24.8 %collective-permute-start.7 = (bf16[48,3456]{1,0:T(8,128)(2,1)}, bf16[48,3456]{1,0:T(8,128)(2,1)}, u32[]{:S(2)}, u32[]{:S(2)}) collective-permute-start(bf16[48,3456]{1,0:T(8,128)(2,1)} %constant_dynamic-update-slice_fusion.refs_0_), channel_id=1, source_target_pairs={{0,24},{2,26},{4,28},{6,30},{8,0},{10,2},{12,4},{14,6},{16,8},{18,... | collective-permute-start | bytes 995336 | tf_op jit(solution)/shard_map/ppermute | solution.py:984
  61.8 19.6 %collective-permute-start.6 = (bf16[2,4,48,896]{3,2,1,0:T(8,128)(2,1)}, bf16[2,4,48,896]{3,2,1,0:T(8,128)(2,1)}, u32[]{:S(2)}, u32[]{:S(2)}) collective-permute-start(bf16[2,4,48,896]{3,2,1,0:T(8,128)(2,1)} %pad_maximum_fusion.7.refs_1_), channel_id=1, source_target_pairs={{0,2},{2,0},{4,6},{6,4},{8,10},{10,8},{12,14},{14,12},{16,18},{18,... | collective-permute-start | bytes 2064392 | tf_op jit(solution)/shard_map/ppermute | solution.py:980
  83.9 20.0 %collective-permute-start.10 = (bf16[2,2,4,48,1152]{4,3,2,1,0:T(8,128)(2,1)S(1)}, bf16[2,2,4,48,1152]{4,3,2,1,0:T(8,128)(2,1)S(1)}, u32[]{:S(2)}, u32[]{:S(2)}) collective-permute-start(bf16[2,2,4,48,1152]{4,3,2,1,0:T(8,128)(2,1)S(1)} %get-tuple-element.354), channel_id=1, source_target_pairs={{0,1},{1,0},{2,3},{3,2},{4,5},{5,4},{6,7},{7,6},{8,9},{9,8},{10,11... | collective-permute-start | bytes 5308424 | tf_op jit(solution)/shard_map/ppermute | solution.py:1004
  84.0 19.9 %collective-permute-start.11 = (bf16[2,2,4,48,896]{4,3,2,1,0:T(8,128)(2,1)S(1)}, bf16[2,2,4,48,896]{4,3,2,1,0:T(8,128)(2,1)S(1)}, u32[]{:S(2)}, u32[]{:S(2)}) collective-permute-start(bf16[2,2,4,48,896]{4,3,2,1,0:T(8,128)(2,1)S(1)} %get-tuple-element.352), channel_id=1, source_target_pairs={{0,1},{1,0},{2,3},{3,2},{4,5},{5,4},{6,7},{7,6},{8,9},{9,8},{10,11... | collective-permute-start | bytes 4128776 | tf_op jit(solution)/shard_map/ppermute | solution.py:1004
  104.0 33.2 %collective-permute-start.14 = (bf16[2,4,48,1920]{3,2,1,0:T(8,128)(2,1)S(1)}, bf16[2,4,48,1920]{3,2,1,0:T(8,128)(2,1)S(1)}, u32[]{:S(2)}, u32[]{:S(2)}) collective-permute-start(bf16[2,4,48,1920]{3,2,1,0:T(8,128)(2,1)S(1)} %pad_maximum_fusion.refs_0_), channel_id=1, source_target_pairs={{0,4},{2,6},{4,0},{6,2},{8,12},{10,14},{12,8},{14,10},{16,20},{18,... | collective-permute-start | bytes 4423688 | tf_op jit(solution)/shard_map/ppermute | solution.py:980
  105.0 26.7 %collective-permute-start.15 = (bf16[2,4,48,1536]{3,2,1,0:T(8,128)(2,1)S(1)}, bf16[2,4,48,1536]{3,2,1,0:T(8,128)(2,1)S(1)}, u32[]{:S(2)}, u32[]{:S(2)}) collective-permute-start(bf16[2,4,48,1536]{3,2,1,0:T(8,128)(2,1)S(1)} %pad_maximum_fusion.1.refs_1_), channel_id=1, source_target_pairs={{0,2},{2,0},{4,6},{6,4},{8,10},{10,8},{12,14},{14,12},{16,18},{18,... | collective-permute-start | bytes 3538952 | tf_op jit(solution)/shard_map/ppermute | solution.py:980
  140.7 25.7 %collective-permute-start.19 = (bf16[2,2,4,48,1920]{4,3,2,1,0:T(8,128)(2,1)}, bf16[2,2,4,48,1920]{4,3,2,1,0:T(8,128)(2,1)}, u32[]{:S(2)}, u32[]{:S(2)}) collective-permute-start(bf16[2,2,4,48,1920]{4,3,2,1,0:T(8,128)(2,1)} %get-tuple-element.387), channel_id=1, source_target_pairs={{0,1},{1,0},{2,3},{3,2},{4,5},{5,4},{6,7},{7,6},{8,9},{9,8},{10,11... | collective-permute-start | bytes 8847368 | tf_op jit(solution)/shard_map/ppermute | solution.py:1004
  140.8 25.6 %collective-permute-start.20 = (bf16[2,2,4,48,1536]{4,3,2,1,0:T(8,128)(2,1)}, bf16[2,2,4,48,1536]{4,3,2,1,0:T(8,128)(2,1)}, u32[]{:S(2)}, u32[]{:S(2)}) collective-permute-start(bf16[2,2,4,48,1536]{4,3,2,1,0:T(8,128)(2,1)} %get-tuple-element.395), channel_id=1, source_target_pairs={{0,1},{1,0},{2,3},{3,2},{4,5},{5,4},{6,7},{7,6},{8,9},{9,8},{10,11... | collective-permute-start | bytes 7077896 | tf_op jit(solution)/shard_map/ppermute | solution.py:1004
  141.3 21.1 %collective-permute-start.21 = (bf16[4,48,1536]{2,1,0:T(8,128)(2,1)}, bf16[4,48,1536]{2,1,0:T(8,128)(2,1)}, u32[]{:S(2)}, u32[]{:S(2)}) collective-permute-start(bf16[4,48,1536]{2,1,0:T(8,128)(2,1)} %get-tuple-element.361), channel_id=1, source_target_pairs={{0,2},{2,0},{4,6},{6,4},{8,10},{10,8},{12,14},{14,12},{16,18},{18,... | collective-permute-start | bytes 1769480 | tf_op jit(solution)/shard_map/ppermute | solution.py:980
  141.9 23.1 %collective-permute-start.22 = (bf16[4,48,1536]{2,1,0:T(8,128)(2,1)S(1)}, bf16[4,48,1536]{2,1,0:T(8,128)(2,1)}, u32[]{:S(2)}, u32[]{:S(2)}) collective-permute-start(bf16[4,48,1536]{2,1,0:T(8,128)(2,1)S(1)} %get-tuple-element.362), channel_id=1, source_target_pairs={{0,4},{2,6},{4,0},{6,2},{8,12},{10,14},{12,8},{14,10},{16,20},{18,... | collective-permute-start | bytes 1769480 | tf_op jit(solution)/shard_map/ppermute | solution.py:980
  166.4 30.9 %collective-permute-start.23 = (bf16[2,4,48,1536]{3,2,1,0:T(8,128)(2,1)S(1)}, bf16[2,4,48,1536]{3,2,1,0:T(8,128)(2,1)S(1)}, u32[]{:S(2)}, u32[]{:S(2)}) collective-permute-start(bf16[2,4,48,1536]{3,2,1,0:T(8,128)(2,1)S(1)} %pad_maximum_fusion.2.refs_0_), channel_id=1, source_target_pairs={{0,4},{2,6},{4,0},{6,2},{8,12},{10,14},{12,8},{14,10},{16,20},{18,... | collective-permute-start | bytes 3538952 | tf_op jit(solution)/shard_map/ppermute | solution.py:980
  167.5 29.8 %collective-permute-start.24 = (bf16[2,4,48,1536]{3,2,1,0:T(8,128)(2,1)S(1)}, bf16[2,4,48,1536]{3,2,1,0:T(8,128)(2,1)S(1)}, u32[]{:S(2)}, u32[]{:S(2)}) collective-permute-start(bf16[2,4,48,1536]{3,2,1,0:T(8,128)(2,1)S(1)} %pad_maximum_fusion.3.refs_1_), channel_id=1, source_target_pairs={{0,2},{2,0},{4,6},{6,4},{8,10},{10,8},{12,14},{14,12},{16,18},{18,... | collective-permute-start | bytes 3538952 | tf_op jit(solution)/shard_map/ppermute | solution.py:980
  170.1 27.0 %collective-permute-start.27 = (bf16[48,3072]{1,0:T(8,128)(2,1)S(1)}, bf16[48,3072]{1,0:T(8,128)(2,1)S(1)}, u32[]{:S(2)}, u32[]{:S(2)}) collective-permute-start(bf16[48,3072]{1,0:T(8,128)(2,1)S(1)} %constant_dynamic-update-slice_fusion.4.refs_0_), channel_id=1, source_target_pairs={{0,8},{2,10},{4,12},{6,14},{8,16},{10,18},{12,20},{14,22},{16,24},... | collective-permute-start | bytes 884744 | tf_op jit(solution)/shard_map/ppermute | solution.py:984
  174.4 22.8 %collective-permute-start.26 = (bf16[48,3072]{1,0:T(8,128)(2,1)S(1)}, bf16[48,3072]{1,0:T(8,128)(2,1)S(1)}, u32[]{:S(2)}, u32[]{:S(2)}) collective-permute-start(bf16[48,3072]{1,0:T(8,128)(2,1)S(1)} %constant_dynamic-update-slice_fusion.4.refs_0_), channel_id=1, source_target_pairs={{0,16},{2,18},{4,20},{6,22},{8,24},{10,26},{12,28},{14,30},{16,0},... | collective-permute-start | bytes 884744 | tf_op jit(solution)/shard_map/ppermute | solution.py:984
  174.7 22.5 %collective-permute-start.25 = (bf16[48,3072]{1,0:T(8,128)(2,1)S(1)}, bf16[48,3072]{1,0:T(8,128)(2,1)S(1)}, u32[]{:S(2)}, u32[]{:S(2)}) collective-permute-start(bf16[48,3072]{1,0:T(8,128)(2,1)S(1)} %constant_dynamic-update-slice_fusion.4.refs_0_), channel_id=1, source_target_pairs={{0,24},{2,26},{4,28},{6,30},{8,0},{10,2},{12,4},{14,6},{16,8},{18,... | collective-permute-start | bytes 884744 | tf_op jit(solution)/shard_map/ppermute | solution.py:984
  217.7 43.4 %collective-permute-start.32 = (bf16[2,4,48,1536]{3,2,1,0:T(8,128)(2,1)S(1)}, bf16[2,4,48,1536]{3,2,1,0:T(8,128)(2,1)S(1)}, u32[]{:S(2)}, u32[]{:S(2)}) collective-permute-start(bf16[2,4,48,1536]{3,2,1,0:T(8,128)(2,1)S(1)} %pad_maximum_fusion.4.refs_0_), channel_id=1, source_target_pairs={{0,4},{2,6},{4,0},{6,2},{8,12},{10,14},{12,8},{14,10},{16,20},{18,... | collective-permute-start | bytes 3538952 | tf_op jit(solution)/shard_map/ppermute | solution.py:980
  219.3 41.8 %collective-permute-start.33 = (bf16[2,4,48,1536]{3,2,1,0:T(8,128)(2,1)S(1)}, bf16[2,4,48,1536]{3,2,1,0:T(8,128)(2,1)S(1)}, u32[]{:S(2)}, u32[]{:S(2)}) collective-permute-start(bf16[2,4,48,1536]{3,2,1,0:T(8,128)(2,1)S(1)} %pad_maximum_fusion.5.refs_1_), channel_id=1, source_target_pairs={{0,2},{2,0},{4,6},{6,4},{8,10},{10,8},{12,14},{14,12},{16,18},{18,... | collective-permute-start | bytes 3538952 | tf_op jit(solution)/shard_map/ppermute | solution.py:980
  347.6 28.1 %collective-permute-start.45 = (bf16[2,4,48,1536]{3,2,1,0:T(8,128)(2,1)S(1)}, bf16[2,4,48,1536]{3,2,1,0:T(8,128)(2,1)S(1)}, u32[]{:S(2)}, u32[]{:S(2)}) collective-permute-start(bf16[2,4,48,1536]{3,2,1,0:T(8,128)(2,1)S(1)} %get-tuple-element.519), channel_id=1, source_target_pairs={{0,2},{2,0},{4,6},{6,4},{8,10},{10,8},{12,14},{14,12},{16,18},{18,... | collective-permute-start | bytes 3538952 | tf_op jit(solution)/shard_map/ppermute | solution.py:980
  349.2 27.7 %collective-permute-start.46 = (bf16[2,4,48,1536]{3,2,1,0:T(8,128)(2,1)S(1)}, bf16[2,4,48,1536]{3,2,1,0:T(8,128)(2,1)S(1)}, u32[]{:S(2)}, u32[]{:S(2)}) collective-permute-start(bf16[2,4,48,1536]{3,2,1,0:T(8,128)(2,1)S(1)} %get-tuple-element.520), channel_id=1, source_target_pairs={{0,4},{2,6},{4,0},{6,2},{8,12},{10,14},{12,8},{14,10},{16,20},{18,... | collective-permute-start | bytes 3538952 | tf_op jit(solution)/shard_map/ppermute | solution.py:980
  349.7 25.0 %collective-permute-start.42 = (bf16[24,3072]{1,0:T(8,128)(2,1)S(1)}, bf16[24,3072]{1,0:T(8,128)(2,1)S(1)}, u32[]{:S(2)}, u32[]{:S(2)}) collective-permute-start(bf16[24,3072]{1,0:T(8,128)(2,1)S(1)} %get-tuple-element.516), channel_id=1, source_target_pairs={{0,8},{2,10},{4,12},{6,14},{8,16},{10,18},{12,20},{14,22},{16,24},... | collective-permute-start | bytes 442376 | tf_op jit(solution)/shard_map/ppermute | solution.py:984
  352.2 22.5 %collective-permute-start.43 = (bf16[24,3072]{1,0:T(8,128)(2,1)S(1)}, bf16[24,3072]{1,0:T(8,128)(2,1)S(1)}, u32[]{:S(2)}, u32[]{:S(2)}) collective-permute-start(bf16[24,3072]{1,0:T(8,128)(2,1)S(1)} %get-tuple-element.517), channel_id=1, source_target_pairs={{0,16},{2,18},{4,20},{6,22},{8,24},{10,26},{12,28},{14,30},{16,0},... | collective-permute-start | bytes 442376 | tf_op jit(solution)/shard_map/ppermute | solution.py:984
  354.9 19.8 %collective-permute-start.44 = (bf16[24,3072]{1,0:T(8,128)(2,1)S(1)}, bf16[24,3072]{1,0:T(8,128)(2,1)S(1)}, u32[]{:S(2)}, u32[]{:S(2)}) collective-permute-start(bf16[24,3072]{1,0:T(8,128)(2,1)S(1)} %get-tuple-element.518), channel_id=1, source_target_pairs={{0,24},{2,26},{4,28},{6,30},{8,0},{10,2},{12,4},{14,6},{16,8},{18,... | collective-permute-start | bytes 442376 | tf_op jit(solution)/shard_map/ppermute | solution.py:984
  378.3 24.9 %collective-permute-start.47 = (bf16[4,48,1536]{2,1,0:T(8,128)(2,1)}, bf16[4,48,1536]{2,1,0:T(8,128)(2,1)S(1)}, u32[]{:S(2)}, u32[]{:S(2)}) collective-permute-start(bf16[4,48,1536]{2,1,0:T(8,128)(2,1)} %get-tuple-element.538), channel_id=1, source_target_pairs={{0,4},{2,6},{4,0},{6,2},{8,12},{10,14},{12,8},{14,10},{16,20},{18,... | collective-permute-start | bytes 1769480 | tf_op jit(solution)/shard_map/ppermute | solution.py:980
  378.8 24.5 %collective-permute-start.48 = (bf16[4,48,1536]{2,1,0:T(8,128)(2,1)}, bf16[4,48,1536]{2,1,0:T(8,128)(2,1)S(1)}, u32[]{:S(2)}, u32[]{:S(2)}) collective-permute-start(bf16[4,48,1536]{2,1,0:T(8,128)(2,1)} %get-tuple-element.539), channel_id=1, source_target_pairs={{0,2},{2,0},{4,6},{6,4},{8,10},{10,8},{12,14},{14,12},{16,18},{18,... | collective-permute-start | bytes 1769480 | tf_op jit(solution)/shard_map/ppermute | solution.py:980
  413.1 25.4 %collective-permute-start.53 = (bf16[2,4,48,1152]{3,2,1,0:T(8,128)(2,1)S(1)}, bf16[2,4,48,1152]{3,2,1,0:T(8,128)(2,1)S(1)}, u32[]{:S(2)}, u32[]{:S(2)}) collective-permute-start(bf16[2,4,48,1152]{3,2,1,0:T(8,128)(2,1)S(1)} %get-tuple-element.555), channel_id=1, source_target_pairs={{0,2},{2,0},{4,6},{6,4},{8,10},{10,8},{12,14},{14,12},{16,18},{18,... | collective-permute-start | bytes 2654216 | tf_op jit(solution)/shard_map/ppermute | solution.py:980
  413.9 24.7 %collective-permute-start.54 = (bf16[2,4,48,896]{3,2,1,0:T(8,128)(2,1)S(1)}, bf16[2,4,48,896]{3,2,1,0:T(8,128)(2,1)S(1)}, u32[]{:S(2)}, u32[]{:S(2)}) collective-permute-start(bf16[2,4,48,896]{3,2,1,0:T(8,128)(2,1)S(1)} %get-tuple-element.556), channel_id=1, source_target_pairs={{0,4},{2,6},{4,0},{6,2},{8,12},{10,14},{12,8},{14,10},{16,20},{18,... | collective-permute-start | bytes 2064392 | tf_op jit(solution)/shard_map/ppermute | solution.py:980
  416.8 21.7 %collective-permute-start.51 = (bf16[48,3072]{1,0:T(8,128)(2,1)S(1)}, bf16[48,3072]{1,0:T(8,128)(2,1)S(1)}, u32[]{:S(2)}, u32[]{:S(2)}) collective-permute-start(bf16[48,3072]{1,0:T(8,128)(2,1)S(1)} %get-tuple-element.553), channel_id=1, source_target_pairs={{0,16},{2,18},{4,20},{6,22},{8,24},{10,26},{12,28},{14,30},{16,0},... | collective-permute-start | bytes 884744 | tf_op jit(solution)/shard_map/ppermute | solution.py:984
  (200 other events, 1988.9 us)

commit v5 on v4

--- a/solution.py
+++ b/solution.py
@@ -916,7 +916,7 @@
         cost_estimate=pl.CostEstimate(
             flops=4_000_000_000, bytes_accessed=20_000_000, transcendentals=3_000_000
         ),
-        compiler_params=pltpu.CompilerParams(vmem_limit_bytes=58 * 2**20),
+        compiler_params=pltpu.CompilerParams(vmem_limit_bytes=36 * 2**20),
     )(*ins)
 
 
@@ -960,7 +960,7 @@
             cost_estimate=pl.CostEstimate(
                 flops=1_000_000_000, bytes_accessed=9_000_000, transcendentals=0
             ),
-            compiler_params=pltpu.CompilerParams(vmem_limit_bytes=58 * 2**20),
+            compiler_params=pltpu.CompilerParams(vmem_limit_bytes=36 * 2**20),
         )(*ins)
     return found[0], found[1], [found[at : at + 2] for at in range(2, 10, 2)]
 

time: 511 us -> 515 us (level)
  local copies, waits for them, and re-layouts: 66.2 us -> 77.6 us
  Pallas kernels: 198 us -> 187 us
    unnamed x322 -> x432, local copies, waits for them, and re-layouts: 46.9 us -> 58 us
    pallas_call x1, Pallas kernels: 25.3 us -> 19.3 us  [pred_back_all(): pl.pallas_call(functools.partial(pred_back_all_kernel, size, count_all, d...]
  transfers between devices with their start and end apart: 69 -> 69, of which waited for: 27 -> 27; matrix products, arithmetic and copies ran while one was open for 10% -> 10% of each run, Pallas kernels for 29% -> 28%
where the time goes in v5:
time: 515 us; the launch traced here: 505 us
  Pallas kernels  187 us (36%)
  waiting for transfers between devices  105 us (20%)
  starting transfers between devices  88.9 us (17%)
  local copies, waits for them, and re-layouts  77.6 us (15%)
  other arithmetic  27.9 us (5%)
  matrix products  12.4 us (2%)
  between operations  6.36 us (1%)
    pallas_call x15, Pallas kernels, on_chip(): pl.pallas_call(kernel, in_specs=in_specs, out_specs=out_specs, out_shape=...  142 us
    unnamed x432, local copies, waits for them, and re-layouts  58 us
    ppermute x28, waiting for transfers between devices, flip(): return lax.ppermute(values, 'dp', pairs)  53.3 us
    ppermute x21, starting transfers between devices, shift(): return lax.ppermute(values, 'dp', pairs)  45 us
    ppermute x21, waiting for transfers between devices, shift(): return lax.ppermute(values, 'dp', pairs)  32.9 us
    ppermute x28, starting transfers between devices, flip(): return lax.ppermute(values, 'dp', pairs)  28.8 us
    pallas_call x1, Pallas kernels, pred_back_all(): pl.pallas_call(functools.partial(pred_back_all_kernel, size, count_all, d...  19.3 us
    ppermute x13, waiting for transfers between devices, swap(): return lax.ppermute(values, 'mp', [(0, 1), (1, 0)])  14.1 us
  transfers between devices with their start and end apart: 69, of which 27 were waited for; matrix products, arithmetic and copies ran while one was open for 10% of the time, Pallas kernels for 28%

profile of v5, /device:TPU:0, one launch (start us, length us, event | category | flops | bytes accessed | tf_op | source)
XLA Modules:
  0.0 505.4 jit_solution(14462830438803796015)
XLA Ops:
  38.1 4.9 collective-permute-done.4
  86.4 13.5 %collective-permute-done.13 = bf16[4,48,1536]{2,1,0:T(8,128)(2,1)S(1)} collective-permute-done((bf16[4,48,1536]{2,1,0:T(8,128)(2,1)S(1)}, bf16[4,48,1536]{2,1,0:T(8,128)(2,1)S(1)}, u32[]{:S(2)}, u32[]{:S(2)}) %collective-permute-start.13) | collective-permute-done | bytes 589856 | tf_op jit(solution)/shard_map/ppermute | solution.py:980
  100.1 4.0 collective-permute-done.12
  108.0 5.0 collective-permute-start.18
  116.0 8.7 %shard_map.517 = (f32[512,768]{1,0:T(8,128)S(1)}, bf16[512,768]{1,0:T(8,128)(2,1)S(1)}, bf16[512,1152]{1,0:T(8,128)(2,1)S(1)}, bf16[512,1152]{1,0:T(8,128)(2,1)S...) custom-call(bf16[512,768]{1,0:T(8,128)(2,1)S(1)} %copy-done.140, ...), custom_call_target="tpu_custom_call" | custom-call | flops 3321888768 | bytes 15200256 | tf_op jit(solution)/shard_map/pallas_call | solution.py:204
  125.9 5.0 collective-permute-done.17.refs_2_
  132.1 5.4 %collective-permute-done.14.refs_2_ = bf16[2,4,48,1920]{3,2,1,0:T(8,128)(2,1)S(1)} collective-permute-done((bf16[2,4,48,1920]{3,2,1,0:T(8,128)(2,1)S(1)}, bf16[2,4,48,1920]{3,2,1,0:T(8,128)(2,1)S(1)}, u32[]{:S(2)}, u32[]{:S(2)}) %collective-permute-start.14) | collective-permute-done | bytes 1474592 | tf_op jit(solution)/shard_map/ppermute | solution.py:980
  137.4 3.5 shard_map.515
  149.8 12.6 %shard_map.518 = (f32[512,768]{1,0:T(8,128)S(1)}, bf16[512,768]{1,0:T(8,128)(2,1)S(1)}, bf16[512,384]{1,0:T(8,128)(2,1)S(1)}, bf16[512,384]{1,0:T(8,128)(2,1)S(1...) custom-call(f32[512,768]{1,0:T(8,128)S(1)} %copy-done.26, ...), custom_call_target="tpu_custom_call" | custom-call | flops 1409286144 | bytes 9924608 | tf_op jit(solution)/shard_map/pallas_call | solution.py:204
  172.0 4.1 collective-permute-start.27
  178.6 20.3 %shard_map.521 = (f32[256,768]{1,0:T(8,128)S(1)}, bf16[256,768]{1,0:T(8,128)(2,1)S(1)}) custom-call(bf16[784,768]{1,0:T(8,128)(2,1)S(1)} %copy-done.135, bf16[256,768]{1,0:T(8,128)(2,1)S(1)} %copy-done.138, f32[784,768]{1,0:T(8,128)S(1)} %copy-done.24, f32[256,768]{1,0:T(8,128)S(1)} %copy-done.49, f32[8,768]{1,0:T(8,128)S(1)} %get-tuple-element.384.refs_4_.refs_2_, ...), custom_call_target="tpu_custom_call" | custom-call | flops 4297064448 | bytes 13078592 | tf_op jit(solution)/shard_map/pallas_call | solution.py:204
  204.4 3.5 shard_map.522
  208.9 7.9 %collective-permute-done.30 = bf16[4,48,1536]{2,1,0:T(8,128)(2,1)S(1)} collective-permute-done((bf16[4,48,1536]{2,1,0:T(8,128)(2,1)S(1)}, bf16[4,48,1536]{2,1,0:T(8,128)(2,1)S(1)}, u32[]{:S(2)}, u32[]{:S(2)}) %collective-permute-start.30) | collective-permute-done | bytes 589856 | tf_op jit(solution)/shard_map/ppermute | solution.py:980
  227.4 14.8 %shard_map.524 = (f32[512,768]{1,0:T(8,128)S(1)}, bf16[512,768]{1,0:T(8,128)(2,1)S(1)}, bf16[512,1536]{1,0:T(8,128)(2,1)S(1)}, bf16[512,1536]{1,0:T(8,128)(2,1)S...) custom-call(bf16[512,768]{1,0:T(8,128)(2,1)S(1)} %get-tuple-element.412.refs_0_.refs_3_, ...), custom_call_target="tpu_custom_call" | custom-call | flops 5435817984 | bytes 20471808 | tf_op jit(solution)/shard_map/pallas_call | solution.py:204
  248.9 17.8 %shard_map.525 = (f32[768,384]{1,0:T(8,128)}, bf16[768,384]{1,0:T(8,128)(2,1)}, f32[256,384]{1,0:T(8,128)}, bf16[256,384]{1,0:T(8,128)(2,1)}, f32[256,384]{1,0:T...) custom-call(bf16[512,768]{1,0:T(8,128)(2,1)} %copy-done.117, ...), custom_call_target="tpu_custom_call" | custom-call | flops 2000000000 | bytes 13991936 | tf_op jit(solution)/shard_map/pallas_call | solution.py:204
  269.3 3.6 shard_map.526.refs_1_
  276.7 4.5 shard_map.527.refs_1_
  281.5 19.3 %shard_map.528 = (f32[1,1]{1,0:T(1,128)}, bf16[512,384]{1,0:T(8,128)(2,1)S(1)}, f32[8,384]{1,0:T(8,128)S(1)}, bf16[16,24,3072]{2,1,0:T(8,128)(2,1)S(1)}, bf16[16,24,3072]{2,1,0:T(8,128)(2,1)}) custom-call(f32[256,768]{1,0:T(8,128)S(1)} %copy-done.119, f32[256,768]{1,0:T(8,128)S(1)} %shard_map.527.refs_1_, s32[1]{0:T(128)} %bitcast.47.refs_2_, ...), custom_call_target="tpu_custom_call" | custom-call | flops 4000000000 | bytes 20000000 | tf_op jit(solution)/shard_map/pallas_call | solution.py:902
  300.9 4.6 collective-permute-done.36
  310.0 12.3 %shard_map.530 = (bf16[768,3072]{1,0:T(8,128)(2,1)}, f32[512,768]{1,0:T(8,128)S(1)}, bf16[512,768]{1,0:T(8,128)(2,1)S(1)}, bf16[768,512]{1,0:T(8,128)(2,1)S(1)},...) custom-call(bf16[512,384]{1,0:T(8,128)(2,1)S(1)} %get-tuple-element.472.refs_0_, ...), custom_call_target="tpu_custom_call" | custom-call | flops 4831838208 | bytes 20299776 | tf_op jit(solution)/shard_map/pallas_call | solution.py:204
  331.2 10.2 %shard_map.532 = (bf16[768,3072]{1,0:T(8,128)(2,1)}, bf16[512,768]{1,0:T(8,128)(2,1)S(1)}, f32[512,768]{1,0:T(8,128)S(1)}, f32[8,768]{1,0:T(8,128)S(1)}) custom-call(f32[512,768]{1,0:T(8,128)S(1)} %copy-done.160, bf16[512,768]{1,0:T(8,128)(2,1)S(1)} %copy-done.164, bf16[768,512]{1,0:T(8,128)(2,1)S(1)} %get-tuple-element.496.refs_2_, ...), custom_call_target="tpu_custom_call" | custom-call | flops 6039797760 | bytes 24453120 | tf_op jit(solution)/shard_map/pallas_call | solution.py:204
  341.6 4.9 copy-done.3
  355.9 16.5 %shard_map.534 = (bf16[512,1152]{1,0:T(8,128)(2,1)S(1)}, bf16[512,1152]{1,0:T(8,128)(2,1)S(1)}) custom-call(bf16[512,768]{1,0:T(8,128)(2,1)S(1)} %copy-done.151, s32[1,512]{1,0:T(1,128)S(1)} %bitcast.157, s32[512,1]{1,0:T(8,128)S(1)} %copy-done.45, bf16[768,896]{1,0:T(8,128)(2,1)S(1)} %bitcast.145, bf16[768,896]{1,0:T(8,128)(2,1)S(1)} %bitcast.148, ...), custom_call_target="tpu_custom_call" | custom-call | flops 2617245696 | bytes 9113600 | tf_op jit(solution)/shard_map/pallas_call | solution.py:204
  388.8 18.0 %shard_map.537 = (bf16[768,2048]{1,0:T(8,128)(2,1)S(1)}, bf16[768,2048]{1,0:T(8,128)(2,1)}) custom-call(bf16[512,768]{1,0:T(8,128)(2,1)S(1)} %copy-done.152, f32[512,768]{1,0:T(8,128)S(1)} %copy-done.158, f32[512,768]{1,0:T(8,128)S(1)} %copy-done.27, bf16[512,768]{1,0:T(8,128)(2,1)S(1)} %copy-done.143, bf16[512,768]{1,0:T(8,128)(2,1)S(1)} %copy-done.141, ...), custom_call_target="tpu_custom_call" | custom-call | flops 6039797760 | bytes 21491712 | tf_op jit(solution)/shard_map/pallas_call | solution.py:204
  407.7 5.9 %collective-permute-done.49 = bf16[768,2048]{1,0:T(8,128)(2,1)S(1)} collective-permute-done((bf16[768,2048]{1,0:T(8,128)(2,1)}, bf16[768,2048]{1,0:T(8,128)(2,1)S(1)}, u32[]{:S(2)}, u32[]{:S(2)}) %collective-permute-start.49) | collective-permute-done | bytes 3145760 | tf_op jit(solution)/shard_map/ppermute | solution.py:1004
  423.5 7.5 %collective-permute-done.50.refs_4_ = bf16[48,3072]{1,0:T(8,128)(2,1)S(1)} collective-permute-done((bf16[48,3072]{1,0:T(8,128)(2,1)S(1)}, bf16[48,3072]{1,0:T(8,128)(2,1)S(1)}, u32[]{:S(2)}, u32[]{:S(2)}) %collective-permute-start.50) | collective-permute-done | bytes 294944 | tf_op jit(solution)/shard_map/ppermute | solution.py:984
  431.0 11.5 %collective-permute-done.51.refs_5_ = bf16[48,3072]{1,0:T(8,128)(2,1)S(1)} collective-permute-done((bf16[48,3072]{1,0:T(8,128)(2,1)S(1)}, bf16[48,3072]{1,0:T(8,128)(2,1)S(1)}, u32[]{:S(2)}, u32[]{:S(2)}) %collective-permute-start.51) | collective-permute-done | bytes 294944 | tf_op jit(solution)/shard_map/ppermute | solution.py:984
  445.4 8.3 %collective-permute-done.56.refs_5_.refs_11_.refs_17_.refs_8_ = bf16[4,48,896]{2,1,0:T(8,128)(2,1)S(1)} collective-permute-done((bf16[4,48,896]{2,1,0:T(8,128)(2,1)S(1)}, bf16[4,48,896]{2,1,0:T(8,128)(2,1)S(1)}, u32[]{:S(2)}, u32[]{:S(2)}) %collective-permute-start.56) | collective-permute-done | bytes 344096 | tf_op jit(solution)/shard_map/ppermute | solution.py:980
  455.8 6.9 %collective-permute-start.57 = (bf16[48,2048]{1,0:T(8,128)(2,1)}, bf16[48,2048]{1,0:T(8,128)(2,1)S(1)}, u32[]{:S(2)}, u32[]{:S(2)}) collective-permute-start(bf16[48,2048]{1,0:T(8,128)(2,1)} %get-tuple-element.567), channel_id=1, source_target_pairs={{0,8},{2,10},{4,12},{6,14},{8,16},{10,18},{12,20},{14,22},{16,24},... | collective-permute-start | bytes 589832 | tf_op jit(solution)/shard_map/ppermute | solution.py:984
  468.3 5.3 %collective-permute-done.58.refs_5_ = bf16[48,2048]{1,0:T(8,128)(2,1)S(1)} collective-permute-done((bf16[48,2048]{1,0:T(8,128)(2,1)S(1)}, bf16[48,2048]{1,0:T(8,128)(2,1)S(1)}, u32[]{:S(2)}, u32[]{:S(2)}) %collective-permute-start.58) | collective-permute-done | bytes 196640 | tf_op jit(solution)/shard_map/ppermute | solution.py:984
  481.1 5.6 %collective-permute-start.65 = (f32[2,128]{1,0:T(2,128)S(1)}, f32[2,128]{1,0:T(2,128)S(1)}, u32[]{:S(2)}, u32[]{:S(2)}) collective-permute-start(f32[2,128]{1,0:T(2,128)S(1)} %add_add_fusion.1), channel_id=1, source_target_pairs={{0,12},{1,13},{2,14},{3,15},{4,8},{5,9},{6,10},{7,11},{8,4},{9,5},... | collective-permute-start | bytes 3080 | tf_op jit(solution)/shard_map/ppermute | solution.py:990
  497.7 6.1 %shard_map.543 = (f32[48,768]{1,0:T(8,128)}, f32[48,768]{1,0:T(8,128)}, f32[48,768]{1,0:T(8,128)}, f32[48,768]{1,0:T(8,128)}, f32[48,768]{1,0:T(8,128)}, /*index...) custom-call(f32[2,128]{1,0:T(2,128)} %copy-done.205, ...), custom_call_target="tpu_custom_call" | custom-call | flops 20000000 | bytes 10000000 | tf_op jit(solution)/shard_map/pallas_call | solution.py:1338
  (689 shorter events, 217.3 us)
Async XLA Ops:
  7.3 26.7 %collective-permute-start.2 = (bf16[48,2048]{1,0:T(8,128)(2,1)S(1)}, bf16[48,2048]{1,0:T(8,128)(2,1)S(1)}, u32[]{:S(2)}, u32[]{:S(2)}) collective-permute-start(bf16[48,2048]{1,0:T(8,128)(2,1)S(1)} %concatenate.136.refs_0_), channel_id=1, source_target_pairs={{0,8},{2,10},{4,12},{6,14},{8,16},{10,18},{12,20},{14,22},{16,24},... | collective-permute-start | bytes 589832 | tf_op jit(solution)/shard_map/ppermute | solution.py:984
  10.3 23.6 %collective-permute-start.1 = (bf16[48,2048]{1,0:T(8,128)(2,1)S(1)}, bf16[48,2048]{1,0:T(8,128)(2,1)S(1)}, u32[]{:S(2)}, u32[]{:S(2)}) collective-permute-start(bf16[48,2048]{1,0:T(8,128)(2,1)S(1)} %concatenate.136.refs_0_), channel_id=1, source_target_pairs={{0,16},{2,18},{4,20},{6,22},{8,24},{10,26},{12,28},{14,30},{16,0},... | collective-permute-start | bytes 589832 | tf_op jit(solution)/shard_map/ppermute | solution.py:984
  12.9 21.0 %collective-permute-start = (bf16[48,2048]{1,0:T(8,128)(2,1)S(1)}, bf16[48,2048]{1,0:T(8,128)(2,1)S(1)}, u32[]{:S(2)}, u32[]{:S(2)}) collective-permute-start(bf16[48,2048]{1,0:T(8,128)(2,1)S(1)} %concatenate.136.refs_0_), channel_id=1, source_target_pairs={{0,24},{2,26},{4,28},{6,30},{8,0},{10,2},{12,4},{14,6},{16,8},{18,... | collective-permute-start | bytes 589832 | tf_op jit(solution)/shard_map/ppermute | solution.py:984
  54.3 26.0 %collective-permute-start.9 = (bf16[48,3456]{1,0:T(8,128)(2,1)}, bf16[48,3456]{1,0:T(8,128)(2,1)}, u32[]{:S(2)}, u32[]{:S(2)}) collective-permute-start(bf16[48,3456]{1,0:T(8,128)(2,1)} %constant_dynamic-update-slice_fusion.refs_0_), channel_id=1, source_target_pairs={{0,8},{2,10},{4,12},{6,14},{8,16},{10,18},{12,20},{14,22},{16,24},... | collective-permute-start | bytes 995336 | tf_op jit(solution)/shard_map/ppermute | solution.py:984
  55.0 25.3 %collective-permute-start.8 = (bf16[48,3456]{1,0:T(8,128)(2,1)}, bf16[48,3456]{1,0:T(8,128)(2,1)}, u32[]{:S(2)}, u32[]{:S(2)}) collective-permute-start(bf16[48,3456]{1,0:T(8,128)(2,1)} %constant_dynamic-update-slice_fusion.refs_0_), channel_id=1, source_target_pairs={{0,16},{2,18},{4,20},{6,22},{8,24},{10,26},{12,28},{14,30},{16,0},... | collective-permute-start | bytes 995336 | tf_op jit(solution)/shard_map/ppermute | solution.py:984
  55.3 25.0 %collective-permute-start.7 = (bf16[48,3456]{1,0:T(8,128)(2,1)}, bf16[48,3456]{1,0:T(8,128)(2,1)}, u32[]{:S(2)}, u32[]{:S(2)}) collective-permute-start(bf16[48,3456]{1,0:T(8,128)(2,1)} %constant_dynamic-update-slice_fusion.refs_0_), channel_id=1, source_target_pairs={{0,24},{2,26},{4,28},{6,30},{8,0},{10,2},{12,4},{14,6},{16,8},{18,... | collective-permute-start | bytes 995336 | tf_op jit(solution)/shard_map/ppermute | solution.py:984
  61.9 19.8 %collective-permute-start.6 = (bf16[2,4,48,896]{3,2,1,0:T(8,128)(2,1)}, bf16[2,4,48,896]{3,2,1,0:T(8,128)(2,1)}, u32[]{:S(2)}, u32[]{:S(2)}) collective-permute-start(bf16[2,4,48,896]{3,2,1,0:T(8,128)(2,1)} %pad_maximum_fusion.7.refs_1_), channel_id=1, source_target_pairs={{0,2},{2,0},{4,6},{6,4},{8,10},{10,8},{12,14},{14,12},{16,18},{18,... | collective-permute-start | bytes 2064392 | tf_op jit(solution)/shard_map/ppermute | solution.py:980
  84.0 20.2 %collective-permute-start.10 = (bf16[2,2,4,48,1152]{4,3,2,1,0:T(8,128)(2,1)S(1)}, bf16[2,2,4,48,1152]{4,3,2,1,0:T(8,128)(2,1)S(1)}, u32[]{:S(2)}, u32[]{:S(2)}) collective-permute-start(bf16[2,2,4,48,1152]{4,3,2,1,0:T(8,128)(2,1)S(1)} %get-tuple-element.354), channel_id=1, source_target_pairs={{0,1},{1,0},{2,3},{3,2},{4,5},{5,4},{6,7},{7,6},{8,9},{9,8},{10,11... | collective-permute-start | bytes 5308424 | tf_op jit(solution)/shard_map/ppermute | solution.py:1004
  84.1 20.1 %collective-permute-start.11 = (bf16[2,2,4,48,896]{4,3,2,1,0:T(8,128)(2,1)S(1)}, bf16[2,2,4,48,896]{4,3,2,1,0:T(8,128)(2,1)S(1)}, u32[]{:S(2)}, u32[]{:S(2)}) collective-permute-start(bf16[2,2,4,48,896]{4,3,2,1,0:T(8,128)(2,1)S(1)} %get-tuple-element.352), channel_id=1, source_target_pairs={{0,1},{1,0},{2,3},{3,2},{4,5},{5,4},{6,7},{7,6},{8,9},{9,8},{10,11... | collective-permute-start | bytes 4128776 | tf_op jit(solution)/shard_map/ppermute | solution.py:1004
  104.3 33.2 %collective-permute-start.14 = (bf16[2,4,48,1920]{3,2,1,0:T(8,128)(2,1)S(1)}, bf16[2,4,48,1920]{3,2,1,0:T(8,128)(2,1)S(1)}, u32[]{:S(2)}, u32[]{:S(2)}) collective-permute-start(bf16[2,4,48,1920]{3,2,1,0:T(8,128)(2,1)S(1)} %pad_maximum_fusion.refs_0_), channel_id=1, source_target_pairs={{0,4},{2,6},{4,0},{6,2},{8,12},{10,14},{12,8},{14,10},{16,20},{18,... | collective-permute-start | bytes 4423688 | tf_op jit(solution)/shard_map/ppermute | solution.py:980
  105.1 26.9 %collective-permute-start.15 = (bf16[2,4,48,1536]{3,2,1,0:T(8,128)(2,1)S(1)}, bf16[2,4,48,1536]{3,2,1,0:T(8,128)(2,1)S(1)}, u32[]{:S(2)}, u32[]{:S(2)}) collective-permute-start(bf16[2,4,48,1536]{3,2,1,0:T(8,128)(2,1)S(1)} %pad_maximum_fusion.1.refs_1_), channel_id=1, source_target_pairs={{0,2},{2,0},{4,6},{6,4},{8,10},{10,8},{12,14},{14,12},{16,18},{18,... | collective-permute-start | bytes 3538952 | tf_op jit(solution)/shard_map/ppermute | solution.py:980
  141.0 27.1 %collective-permute-start.19 = (bf16[2,2,4,48,1920]{4,3,2,1,0:T(8,128)(2,1)}, bf16[2,2,4,48,1920]{4,3,2,1,0:T(8,128)(2,1)}, u32[]{:S(2)}, u32[]{:S(2)}) collective-permute-start(bf16[2,2,4,48,1920]{4,3,2,1,0:T(8,128)(2,1)} %get-tuple-element.387), channel_id=1, source_target_pairs={{0,1},{1,0},{2,3},{3,2},{4,5},{5,4},{6,7},{7,6},{8,9},{9,8},{10,11... | collective-permute-start | bytes 8847368 | tf_op jit(solution)/shard_map/ppermute | solution.py:1004
  141.1 27.0 %collective-permute-start.20 = (bf16[2,2,4,48,1536]{4,3,2,1,0:T(8,128)(2,1)}, bf16[2,2,4,48,1536]{4,3,2,1,0:T(8,128)(2,1)}, u32[]{:S(2)}, u32[]{:S(2)}) collective-permute-start(bf16[2,2,4,48,1536]{4,3,2,1,0:T(8,128)(2,1)} %get-tuple-element.395), channel_id=1, source_target_pairs={{0,1},{1,0},{2,3},{3,2},{4,5},{5,4},{6,7},{7,6},{8,9},{9,8},{10,11... | collective-permute-start | bytes 7077896 | tf_op jit(solution)/shard_map/ppermute | solution.py:1004
  141.6 21.5 %collective-permute-start.21 = (bf16[4,48,1536]{2,1,0:T(8,128)(2,1)}, bf16[4,48,1536]{2,1,0:T(8,128)(2,1)}, u32[]{:S(2)}, u32[]{:S(2)}) collective-permute-start(bf16[4,48,1536]{2,1,0:T(8,128)(2,1)} %get-tuple-element.361), channel_id=1, source_target_pairs={{0,2},{2,0},{4,6},{6,4},{8,10},{10,8},{12,14},{14,12},{16,18},{18,... | collective-permute-start | bytes 1769480 | tf_op jit(solution)/shard_map/ppermute | solution.py:980
  142.1 23.6 %collective-permute-start.22 = (bf16[4,48,1536]{2,1,0:T(8,128)(2,1)}, bf16[4,48,1536]{2,1,0:T(8,128)(2,1)S(1)}, u32[]{:S(2)}, u32[]{:S(2)}) collective-permute-start(bf16[4,48,1536]{2,1,0:T(8,128)(2,1)} %get-tuple-element.362), channel_id=1, source_target_pairs={{0,4},{2,6},{4,0},{6,2},{8,12},{10,14},{12,8},{14,10},{16,20},{18,... | collective-permute-start | bytes 1769480 | tf_op jit(solution)/shard_map/ppermute | solution.py:980
  168.1 30.9 %collective-permute-start.23 = (bf16[2,4,48,1536]{3,2,1,0:T(8,128)(2,1)S(1)}, bf16[2,4,48,1536]{3,2,1,0:T(8,128)(2,1)S(1)}, u32[]{:S(2)}, u32[]{:S(2)}) collective-permute-start(bf16[2,4,48,1536]{3,2,1,0:T(8,128)(2,1)S(1)} %pad_maximum_fusion.2.refs_0_), channel_id=1, source_target_pairs={{0,4},{2,6},{4,0},{6,2},{8,12},{10,14},{12,8},{14,10},{16,20},{18,... | collective-permute-start | bytes 3538952 | tf_op jit(solution)/shard_map/ppermute | solution.py:980
  169.4 29.6 %collective-permute-start.24 = (bf16[2,4,48,1536]{3,2,1,0:T(8,128)(2,1)S(1)}, bf16[2,4,48,1536]{3,2,1,0:T(8,128)(2,1)S(1)}, u32[]{:S(2)}, u32[]{:S(2)}) collective-permute-start(bf16[2,4,48,1536]{3,2,1,0:T(8,128)(2,1)S(1)} %pad_maximum_fusion.3.refs_1_), channel_id=1, source_target_pairs={{0,2},{2,0},{4,6},{6,4},{8,10},{10,8},{12,14},{14,12},{16,18},{18,... | collective-permute-start | bytes 3538952 | tf_op jit(solution)/shard_map/ppermute | solution.py:980
  172.0 26.8 %collective-permute-start.27 = (bf16[48,3072]{1,0:T(8,128)(2,1)S(1)}, bf16[48,3072]{1,0:T(8,128)(2,1)S(1)}, u32[]{:S(2)}, u32[]{:S(2)}) collective-permute-start(bf16[48,3072]{1,0:T(8,128)(2,1)S(1)} %constant_dynamic-update-slice_fusion.4.refs_0_), channel_id=1, source_target_pairs={{0,8},{2,10},{4,12},{6,14},{8,16},{10,18},{12,20},{14,22},{16,24},... | collective-permute-start | bytes 884744 | tf_op jit(solution)/shard_map/ppermute | solution.py:984
  176.1 22.8 %collective-permute-start.26 = (bf16[48,3072]{1,0:T(8,128)(2,1)S(1)}, bf16[48,3072]{1,0:T(8,128)(2,1)S(1)}, u32[]{:S(2)}, u32[]{:S(2)}) collective-permute-start(bf16[48,3072]{1,0:T(8,128)(2,1)S(1)} %constant_dynamic-update-slice_fusion.4.refs_0_), channel_id=1, source_target_pairs={{0,16},{2,18},{4,20},{6,22},{8,24},{10,26},{12,28},{14,30},{16,0},... | collective-permute-start | bytes 884744 | tf_op jit(solution)/shard_map/ppermute | solution.py:984
  176.4 22.5 %collective-permute-start.25 = (bf16[48,3072]{1,0:T(8,128)(2,1)S(1)}, bf16[48,3072]{1,0:T(8,128)(2,1)S(1)}, u32[]{:S(2)}, u32[]{:S(2)}) collective-permute-start(bf16[48,3072]{1,0:T(8,128)(2,1)S(1)} %constant_dynamic-update-slice_fusion.4.refs_0_), channel_id=1, source_target_pairs={{0,24},{2,26},{4,28},{6,30},{8,0},{10,2},{12,4},{14,6},{16,8},{18,... | collective-permute-start | bytes 884744 | tf_op jit(solution)/shard_map/ppermute | solution.py:984
  221.1 45.7 %collective-permute-start.32 = (bf16[2,4,48,1536]{3,2,1,0:T(8,128)(2,1)S(1)}, bf16[2,4,48,1536]{3,2,1,0:T(8,128)(2,1)S(1)}, u32[]{:S(2)}, u32[]{:S(2)}) collective-permute-start(bf16[2,4,48,1536]{3,2,1,0:T(8,128)(2,1)S(1)} %pad_maximum_fusion.4.refs_0_), channel_id=1, source_target_pairs={{0,4},{2,6},{4,0},{6,2},{8,12},{10,14},{12,8},{14,10},{16,20},{18,... | collective-permute-start | bytes 3538952 | tf_op jit(solution)/shard_map/ppermute | solution.py:980
  222.6 44.2 %collective-permute-start.33 = (bf16[2,4,48,1536]{3,2,1,0:T(8,128)(2,1)S(1)}, bf16[2,4,48,1536]{3,2,1,0:T(8,128)(2,1)S(1)}, u32[]{:S(2)}, u32[]{:S(2)}) collective-permute-start(bf16[2,4,48,1536]{3,2,1,0:T(8,128)(2,1)S(1)} %pad_maximum_fusion.5.refs_1_), channel_id=1, source_target_pairs={{0,2},{2,0},{4,6},{6,4},{8,10},{10,8},{12,14},{14,12},{16,18},{18,... | collective-permute-start | bytes 3538952 | tf_op jit(solution)/shard_map/ppermute | solution.py:980
  305.8 19.7 %collective-permute-start.37 = (bf16[2,4,24,1536]{3,2,1,0:T(8,128)(2,1)S(1)}, bf16[2,4,24,1536]{3,2,1,0:T(8,128)(2,1)S(1)}, u32[]{:S(2)}, u32[]{:S(2)}) collective-permute-start(bf16[2,4,24,1536]{3,2,1,0:T(8,128)(2,1)S(1)} %get-tuple-element.470), channel_id=1, source_target_pairs={{0,2},{2,0},{4,6},{6,4},{8,10},{10,8},{12,14},{14,12},{16,18},{18,... | collective-permute-start | bytes 1769480 | tf_op jit(solution)/shard_map/ppermute | solution.py:980
  347.4 28.1 %collective-permute-start.45 = (bf16[2,4,48,1536]{3,2,1,0:T(8,128)(2,1)S(1)}, bf16[2,4,48,1536]{3,2,1,0:T(8,128)(2,1)S(1)}, u32[]{:S(2)}, u32[]{:S(2)}) collective-permute-start(bf16[2,4,48,1536]{3,2,1,0:T(8,128)(2,1)S(1)} %get-tuple-element.519), channel_id=1, source_target_pairs={{0,2},{2,0},{4,6},{6,4},{8,10},{10,8},{12,14},{14,12},{16,18},{18,... | collective-permute-start | bytes 3538952 | tf_op jit(solution)/shard_map/ppermute | solution.py:980
  348.9 27.8 %collective-permute-start.46 = (bf16[2,4,48,1536]{3,2,1,0:T(8,128)(2,1)S(1)}, bf16[2,4,48,1536]{3,2,1,0:T(8,128)(2,1)S(1)}, u32[]{:S(2)}, u32[]{:S(2)}) collective-permute-start(bf16[2,4,48,1536]{3,2,1,0:T(8,128)(2,1)S(1)} %get-tuple-element.520), channel_id=1, source_target_pairs={{0,4},{2,6},{4,0},{6,2},{8,12},{10,14},{12,8},{14,10},{16,20},{18,... | collective-permute-start | bytes 3538952 | tf_op jit(solution)/shard_map/ppermute | solution.py:980
  349.4 23.0 %collective-permute-start.42 = (bf16[24,3072]{1,0:T(8,128)(2,1)S(1)}, bf16[24,3072]{1,0:T(8,128)(2,1)S(1)}, u32[]{:S(2)}, u32[]{:S(2)}) collective-permute-start(bf16[24,3072]{1,0:T(8,128)(2,1)S(1)} %get-tuple-element.516), channel_id=1, source_target_pairs={{0,8},{2,10},{4,12},{6,14},{8,16},{10,18},{12,20},{14,22},{16,24},... | collective-permute-start | bytes 442376 | tf_op jit(solution)/shard_map/ppermute | solution.py:984
  351.9 20.5 %collective-permute-start.43 = (bf16[24,3072]{1,0:T(8,128)(2,1)S(1)}, bf16[24,3072]{1,0:T(8,128)(2,1)S(1)}, u32[]{:S(2)}, u32[]{:S(2)}) collective-permute-start(bf16[24,3072]{1,0:T(8,128)(2,1)S(1)} %get-tuple-element.517), channel_id=1, source_target_pairs={{0,16},{2,18},{4,20},{6,22},{8,24},{10,26},{12,28},{14,30},{16,0},... | collective-permute-start | bytes 442376 | tf_op jit(solution)/shard_map/ppermute | solution.py:984
  378.0 28.8 %collective-permute-start.47 = (bf16[4,48,1536]{2,1,0:T(8,128)(2,1)}, bf16[4,48,1536]{2,1,0:T(8,128)(2,1)S(1)}, u32[]{:S(2)}, u32[]{:S(2)}) collective-permute-start(bf16[4,48,1536]{2,1,0:T(8,128)(2,1)} %get-tuple-element.538), channel_id=1, source_target_pairs={{0,4},{2,6},{4,0},{6,2},{8,12},{10,14},{12,8},{14,10},{16,20},{18,... | collective-permute-start | bytes 1769480 | tf_op jit(solution)/shard_map/ppermute | solution.py:980
  378.5 28.3 %collective-permute-start.48 = (bf16[4,48,1536]{2,1,0:T(8,128)(2,1)}, bf16[4,48,1536]{2,1,0:T(8,128)(2,1)S(1)}, u32[]{:S(2)}, u32[]{:S(2)}) collective-permute-start(bf16[4,48,1536]{2,1,0:T(8,128)(2,1)} %get-tuple-element.539), channel_id=1, source_target_pairs={{0,2},{2,0},{4,6},{6,4},{8,10},{10,8},{12,14},{14,12},{16,18},{18,... | collective-permute-start | bytes 1769480 | tf_op jit(solution)/shard_map/ppermute | solution.py:980
  416.6 25.9 %collective-permute-start.53 = (bf16[2,4,48,1152]{3,2,1,0:T(8,128)(2,1)S(1)}, bf16[2,4,48,1152]{3,2,1,0:T(8,128)(2,1)S(1)}, u32[]{:S(2)}, u32[]{:S(2)}) collective-permute-start(bf16[2,4,48,1152]{3,2,1,0:T(8,128)(2,1)S(1)} %get-tuple-element.555), channel_id=1, source_target_pairs={{0,2},{2,0},{4,6},{6,4},{8,10},{10,8},{12,14},{14,12},{16,18},{18,... | collective-permute-start | bytes 2654216 | tf_op jit(solution)/shard_map/ppermute | solution.py:980
  417.3 25.2 %collective-permute-start.54 = (bf16[2,4,48,896]{3,2,1,0:T(8,128)(2,1)S(1)}, bf16[2,4,48,896]{3,2,1,0:T(8,128)(2,1)S(1)}, u32[]{:S(2)}, u32[]{:S(2)}) collective-permute-start(bf16[2,4,48,896]{3,2,1,0:T(8,128)(2,1)S(1)} %get-tuple-element.556), channel_id=1, source_target_pairs={{0,4},{2,6},{4,0},{6,2},{8,12},{10,14},{12,8},{14,10},{16,20},{18,... | collective-permute-start | bytes 2064392 | tf_op jit(solution)/shard_map/ppermute | solution.py:980
  420.8 21.7 %collective-permute-start.51 = (bf16[48,3072]{1,0:T(8,128)(2,1)S(1)}, bf16[48,3072]{1,0:T(8,128)(2,1)S(1)}, u32[]{:S(2)}, u32[]{:S(2)}) collective-permute-start(bf16[48,3072]{1,0:T(8,128)(2,1)S(1)} %get-tuple-element.553), channel_id=1, source_target_pairs={{0,16},{2,18},{4,20},{6,22},{8,24},{10,26},{12,28},{14,30},{16,0},... | collective-permute-start | bytes 884744 | tf_op jit(solution)/shard_map/ppermute | solution.py:984
  (255 other events, 2620.7 us)
